TPU v7x, 32 devices: a whole 2x2x4 slice. The times are simulated.
32 devices in a mesh: cols: 1, trc: 16 (over z, x, core), lev: 2 (over y).
Axes of the slice: x: 2, y: 2, z: 4, core: 2. Of those that a mesh axis runs over, the one named last changes fastest.
Arguments:
- potential_warmth: float32 [128, 8, 128], P('lev', 'cols', 'trc'), may hold values from -6 to 6
- saltiness_anomaly: float32 [128, 8, 128], P('lev', 'cols', 'trc'), may hold values from -6 to 6
- zonal_speed: float32 [128, 8, 128], P('lev', 'cols', 'trc'), may hold values from -3 to 3
- meridional_speed: float32 [128, 8, 128], P('lev', 'cols', 'trc'), may hold values from -3 to 3
- marine_indicator: int32 [128, 8, 128], P('lev', 'cols', 'trc'), may hold values from 0 to 1, as said below
- species_concentrations: float32 [64, 128, 8, 128], P('trc', 'lev', 'cols'), may hold values from 0.1 to 2
- coupling_matrix: bfloat16 [64, 64], replicated, may hold values from -0.75 to 0.75
- species_guild_number: int32 [64], replicated, may hold values from 0 to 7
- guild_extinction_coefficient: float32 [8], replicated, may hold values from 0.0001 to 0.0012
Outputs:
- warmth_final: float32 [128, 8, 128], P('lev', 'cols', 'trc')
- saltiness_final: float32 [128, 8, 128], P('lev', 'cols', 'trc')
- zonal_speed_final: float32 [128, 8, 128], P('lev', 'cols', 'trc')
- meridional_speed_final: float32 [128, 8, 128], P('lev', 'cols', 'trc')
- species_final: float32 [64, 128, 8, 128], P('trc', 'lev', 'cols')
Inputs may be any that keep to these rules, and one draw needn't show every extreme that they name: `marine_indicator`: each column is sea from level 0 down to a depth drawn per column and land below it; the columns at the first index and at the last two indices of the second horizontal dimension are sea at every level.
All inputs are finite; a program needn't handle non-finite values.
Results may differ from a plain program's by a relative error of at most 0.00066.
Values may be sent and summed in bfloat16 or wider, within the bound.
No kernel may reach another device: no remote copies, remote signals or barrier semaphores. Data moves between devices by JAX's collectives and lax.ppermute only.
A program may use at most 64 MiB of HBM per device.

v0:
```python
import jax
import jax.numpy as jnp
from jax import lax
from jax.sharding import PartitionSpec as P

viscosity = 0.2
buoyancy = 0.25
marine_advance = 0.05
tracer_step = 0.2
level_step = 0.04
react_step = 0.25
warming_amount = 60.0


def entering(part, axis, combine, identity, reverse):
    count = lax.axis_size(axis)
    place = lax.axis_index(axis)
    ahead = count - 1 - place if reverse else place
    gathered = lax.all_gather(part, axis)
    state = jnp.zeros_like(part) + jnp.asarray(identity, part.dtype)

    def one(turn, state):
        source = count - 1 - turn if reverse else turn
        return combine(state, lax.dynamic_index_in_dim(gathered, source, 0, False))

    return lax.fori_loop(0, ahead, one, state)


def extended(block, sides, width, periodic):
    for axis, dim in sides:
        count = lax.axis_size(axis)
        forward = [(i, i + 1) for i in range(count - 1)]
        if periodic:
            forward.append((count - 1, 0))
        backward = [(target, source) for source, target in forward]
        low = lax.ppermute(
            lax.slice_in_dim(block, block.shape[dim] - width, None, axis=dim), axis, forward
        )
        high = lax.ppermute(lax.slice_in_dim(block, 0, width, axis=dim), axis, backward)
        block = jnp.concatenate([low, block, high], axis=dim)
    return block


def from_behind(value, axis, steps):
    count = lax.axis_size(axis)
    pairs = [(source, (source + steps) % count) for source in range(count)]
    return lax.ppermute(value, axis, pairs)


def minmod(slope_left, slope_right):
    return (
        0.5
        * (jnp.sign(slope_left) + jnp.sign(slope_right))
        * jnp.minimum(jnp.abs(slope_left), jnp.abs(slope_right))
    )


def limited_div(padded, face_speed, dimension):
    length = padded.shape[dimension] - 4
    far_left = lax.slice_in_dim(padded, 0, length + 1, axis=dimension)
    left_cell = lax.slice_in_dim(padded, 1, length + 2, axis=dimension)
    right_cell = lax.slice_in_dim(padded, 2, length + 3, axis=dimension)
    far_right = lax.slice_in_dim(padded, 3, length + 4, axis=dimension)
    plus_side = left_cell + 0.5 * minmod(left_cell - far_left, right_cell - left_cell)
    minus_side = right_cell - 0.5 * minmod(right_cell - left_cell, far_right - right_cell)
    face_flux = jnp.maximum(face_speed, 0.0) * plus_side + jnp.minimum(face_speed, 0.0) * minus_side
    return lax.slice_in_dim(face_flux, 1, length + 1, axis=dimension) - lax.slice_in_dim(
        face_flux, 0, length, axis=dimension
    )


def add_up(earlier, latter):
    return earlier + latter


def shards(
    potential_warmth,
    saltiness_anomaly,
    zonal_speed,
    meridional_speed,
    marine_indicator,
    species_concentrations,
    coupling_matrix,
    species_guild_number,
    guild_extinction_coefficient,
):
    layer_sum = potential_warmth.shape[0]
    marine_indicator_real = marine_indicator.astype(jnp.float32)
    fluid_mass_per_volume = 0.8 * saltiness_anomaly - 0.2 * potential_warmth
    profile_beginning = jnp.zeros(potential_warmth.shape[1:], jnp.float32)
    above_density = entering(
        jnp.sum(fluid_mass_per_volume, axis=0), "lev", add_up, profile_beginning, False
    )
    hydrostatic_pressure = buoyancy * (
        above_density[None]
        + jnp.cumsum(fluid_mass_per_volume, axis=0)
        - 0.5 * fluid_mass_per_volume
    )
    stacked_fields = jnp.stack(
        [
            hydrostatic_pressure,
            zonal_speed,
            meridional_speed,
            marine_indicator_real,
            potential_warmth,
            saltiness_anomaly,
        ]
    )
    padded_block = extended(stacked_fields, (("cols", 2), ("trc", 3), ("lev", 1)), 1, True)
    east_side = padded_block[:, 1:-1, 2:, 1:-1]
    west_side = padded_block[:, 1:-1, :-2, 1:-1]
    north_side = padded_block[:, 1:-1, 1:-1, 2:]
    south_side = padded_block[:, 1:-1, 1:-1, :-2]
    mask_east = marine_indicator_real * east_side[3]
    mask_north = marine_indicator_real * north_side[3]
    east_laplace = east_side[1] + west_side[1] + north_side[1] + south_side[1] - 4.0 * zonal_speed
    north_laplace = (
        east_side[2] + west_side[2] + north_side[2] + south_side[2] - 4.0 * meridional_speed
    )
    zonal_speed_final = mask_east * (
        zonal_speed
        + marine_advance * (-(east_side[0] - hydrostatic_pressure) + viscosity * east_laplace)
    )
    meridional_speed_final = mask_north * (
        meridional_speed
        + marine_advance * (-(north_side[0] - hydrostatic_pressure) + viscosity * north_laplace)
    )
    east_west = from_behind(zonal_speed_final[:, -1:, :], "cols", 1)
    north_south = from_behind(meridional_speed_final[:, :, -1:], "trc", 1)
    faces_east = jnp.concatenate([east_west, zonal_speed_final], axis=1)
    faces_north = jnp.concatenate([north_south, meridional_speed_final], axis=2)
    divergence = (
        zonal_speed_final - faces_east[:, :-1] + meridional_speed_final - faces_north[:, :, :-1]
    )
    flow_next = entering(jnp.sum(divergence, axis=0), "lev", add_up, profile_beginning, True)
    deeper_sum = jnp.cumsum(divergence[::-1], axis=0)[::-1] + flow_next[None]
    level_index = lax.axis_index("lev") * layer_sum + lax.broadcasted_iota(
        jnp.int32, deeper_sum.shape, 0
    )
    faces_vertical = jnp.concatenate(
        [jnp.where(level_index == 0, 0.0, deeper_sum), flow_next[None]], axis=0
    )

    def donor_quantity(member):
        values = padded_block[member]
        cells_east = values[1:-1, :, 1:-1]
        flux_east = (
            jnp.maximum(faces_east, 0.0) * cells_east[:, :-1]
            + jnp.minimum(faces_east, 0.0) * cells_east[:, 1:]
        )
        cells_north = values[1:-1, 1:-1, :]
        flux_north = (
            jnp.maximum(faces_north, 0.0) * cells_north[:, :, :-1]
            + jnp.minimum(faces_north, 0.0) * cells_north[:, :, 1:]
        )
        cells_down = values[:, 1:-1, 1:-1]
        flux_down = (
            jnp.maximum(faces_vertical, 0.0) * cells_down[:-1]
            + jnp.minimum(faces_vertical, 0.0) * cells_down[1:]
        )
        return (
            flux_east[:, 1:]
            - flux_east[:, :-1]
            + (flux_north[:, :, 1:] - flux_north[:, :, :-1])
            + (flux_down[1:] - flux_down[:-1])
        )

    tracer_east, tracer_north, tracer_down = (
        lax.all_gather(faces_east, "trc", axis=2, tiled=True),
        lax.all_gather(meridional_speed_final, "trc", axis=2, tiled=True),
        lax.all_gather(faces_vertical, "trc", axis=2, tiled=True),
    )
    tracer_faces_north = jnp.concatenate([tracer_north[:, :, -1:], tracer_north], axis=2)
    advected = species_concentrations
    for repeat in range(2):
        beside = extended(advected, (("cols", 2),), 2, True)
        stacks = extended(advected, (("lev", 1),), 2, False)
        beside_all = jnp.concatenate([advected[..., -2:], advected, advected[..., :2]], axis=3)
        sideways = limited_div(beside, tracer_east[None], 2) + limited_div(
            beside_all, tracer_faces_north[None], 3
        )
        upright = limited_div(stacks, tracer_down[None], 1)
        advected = advected - (tracer_step * sideways + level_step * upright)
    rounded = lax.optimization_barrier(advected.astype(jnp.bfloat16))
    onehot = (
        species_guild_number[:, None]
        == lax.broadcasted_iota(
            jnp.int32, (species_guild_number.shape[0], guild_extinction_coefficient.shape[0]), 1
        )
    ).astype(jnp.float32)
    absorb = jnp.sum(onehot * guild_extinction_coefficient[None, :], axis=1)
    level_block = lax.all_to_all(rounded, "trc", split_axis=3, concat_axis=0, tiled=True)
    products = jnp.einsum(
        "st,tzxy->szxy", coupling_matrix, level_block, preferred_element_type=jnp.float32
    )
    summed = jnp.sum(absorb[:, None, None, None] * level_block.astype(jnp.float32), axis=0)
    products, stacked_light = (products, summed[None])
    reaction = lax.all_to_all(products, "trc", split_axis=0, concat_axis=3, tiled=True)
    attenuation = stacked_light[0]
    species_final = advected + react_step * reaction
    light_top = entering(jnp.sum(attenuation, axis=0), "lev", add_up, profile_beginning, False)
    light_path = light_top[None] + jnp.cumsum(attenuation, axis=0) - attenuation
    radiation_captured = jnp.exp(-light_path) * (1.0 - jnp.exp(-attenuation))
    warmth_final = (
        potential_warmth
        - marine_advance * donor_quantity(4)
        + warming_amount * marine_indicator_real * radiation_captured
    )
    saltiness_final = saltiness_anomaly - marine_advance * donor_quantity(5)
    return (warmth_final, saltiness_final, zonal_speed_final, meridional_speed_final, species_final)


def solution(mesh):
    in_specs = (
        P("lev", "cols", "trc"),
        P("lev", "cols", "trc"),
        P("lev", "cols", "trc"),
        P("lev", "cols", "trc"),
        P("lev", "cols", "trc"),
        P("trc", "lev", "cols", None),
        P(),
        P(),
        P(),
    )
    out_specs = (
        P("lev", "cols", "trc"),
        P("lev", "cols", "trc"),
        P("lev", "cols", "trc"),
        P("lev", "cols", "trc"),
        P("trc", "lev", "cols", None),
    )
    return jax.shard_map(shards, mesh=mesh, in_specs=in_specs, out_specs=out_specs, check_vma=False)
```

profile of v0, /device:TPU:0, one launch (start us, length us, event | category | flops | bytes accessed | tf_op | source)
XLA Modules:
  0.0 297.2 jit_solution(950084461760988787)
XLA Ops:
  1.8 6.3 %fusion.91 = f32[64,8,8]{2,1,0:T(8,128)S(1)} fusion(f32[64,8,8]{2,1,0:T(8,128)S(1)} %copy.260), kind=kOutput, calls=%fused_computation.203 | output fusion | flops 258048 | bytes 32768 | tf_op jit(solution)/shard_map/jit(cumsum)/reduce_window_sum | solution.py:96
  8.2 5.3 %all-gather = f32[16,8]{1,0:T(8,128)S(1)} all-gather(f32[8,8]{1,0:T(8,128)S(1)} %get-tuple-element.229), channel_id=2, replica_groups=mesh['cols'=1,'trc'=16,'lev'=2] {'lev'}, dimensions={0}, use_global_device_ids=true | all-gather | bytes 768 | tf_op jit(solution)/shard_map/all_gather | solution.py:19
  20.2 5.9 %collective-permute-start.10 = (f32[4,2,8,128]{3,2,1,0:T(8,128)}, f32[4,2,8,128]{3,2,1,0:T(8,128)}, u32[]{:S(2)}, u32[]{:S(2)}) collective-permute-start(f32[4,2,8,128]{3,2,1,0:T(8,128)} %get-tuple-element.243), channel_id=1, source_target_pairs={{0,1},{2,3},{4,5},{6,7},{8,9},{10,11},{12,13},{14,15},{16,17},{18,... | collective-permute-start | bytes 98312 | tf_op jit(solution)/shard_map/ppermute | solution.py:36
  27.8 4.7 %collective-permute-start.9 = (f32[4,64,2,128]{1,3,2,0:T(8,128)}, f32[4,64,2,128]{1,3,2,0:T(8,128)}, u32[]{:S(2)}, u32[]{:S(2)}) collective-permute-start(f32[4,64,2,128]{1,3,2,0:T(8,128)} %get-tuple-element.238), channel_id=1, source_target_pairs={{0,0},{1,1},{2,2},{3,3},{4,4},{5,5},{6,6},{7,7},{8,8},{9,9},{10,10... | collective-permute-start | bytes 786440 | tf_op jit(solution)/shard_map/ppermute | solution.py:39
  33.3 4.4 %collective-permute-start.2 = (f32[6,64,10,1]{1,3,2,0:T(1,128)S(1)}, f32[6,64,10,1]{1,3,2,0:T(1,128)S(1)}, u32[]{:S(2)}, u32[]{:S(2)}) collective-permute-start(f32[6,64,10,1]{1,3,2,0:T(1,128)S(1)} %get-tuple-element.253), channel_id=1, source_target_pairs={{2,0},{4,2},{6,4},{8,6},{10,8},{12,10},{14,12},{16,14},{18,16},{20... | collective-permute-start | bytes 46088 | tf_op jit(solution)/shard_map/ppermute | solution.py:39
  40.1 21.0 %all_gather.32 = f32[64,8,128]{0,1,2:T(8,128)S(1)} all-gather(f32[64,8,8]{0,1,2:T(8,128)S(1)} %copy.280), channel_id=1, replica_groups=mesh['cols'=1,'trc'=16,'lev'=2] {'trc'}, dimensions={2}, use_global_device_ids=true | all-gather | bytes 278528 | tf_op jit(solution)/shard_map/all_gather | solution.py:170
  68.9 5.9 %multiply_add_fusion.3 = f32[4,64,8,129]{1,3,2,0:T(8,128)} fusion(f32[4,64,8,2]{1,3,2,0:T(2,128)} %get-tuple-element.240, f32[4,64,8,128]{1,3,2,0:T(8,128)S(1)} %copy.298, f32[4,64,8,2]{1,3,2,0:T(2,128)} %get-tuple-element.239, f32[64,8,129]{0,2,1:T(8,128)S(1)} %copy.288, f32[64,8,129]{0,2,1:T(8,128)S(1)} %copy.283), kind=kLoop, calls=%fused_computation.38 | loop fusion | flops 7397376 | bytes 2666496 | tf_op jit(solution)/shard_map/add | solution.py:66
  79.6 17.5 %all-gather.1 = f32[16,8]{1,0:T(8,128)S(1)} all-gather(f32[8,8]{1,0:T(8,128)S(1)} %get-tuple-element.225), channel_id=3, replica_groups=mesh['cols'=1,'trc'=16,'lev'=2] {'lev'}, dimensions={0}, use_global_device_ids=true | all-gather | bytes 768 | tf_op jit(solution)/shard_map/all_gather | solution.py:19
  98.0 6.3 %fusion.92 = f32[64,8,8]{2,1,0:T(8,128)S(1)} fusion(f32[64,8,8]{2,1,0:T(8,128)S(1)} %copy.269), kind=kOutput, calls=%fused_computation.204 | output fusion | flops 258048 | bytes 32768 | tf_op jit(solution)/shard_map/jit(cumsum)/reduce_window_sum | solution.py:136
  106.1 4.7 %collective-permute-start.8 = (f32[4,64,2,128]{1,3,2,0:T(8,128)}, f32[4,64,2,128]{1,3,2,0:T(8,128)}, u32[]{:S(2)}, u32[]{:S(2)}) collective-permute-start(f32[4,64,2,128]{1,3,2,0:T(8,128)} %get-tuple-element.237), channel_id=1, source_target_pairs={{0,0},{1,1},{2,2},{3,3},{4,4},{5,5},{6,6},{7,7},{8,8},{9,9},{10,10... | collective-permute-start | bytes 786440 | tf_op jit(solution)/shard_map/ppermute | solution.py:36
  114.5 18.7 %all_gather.33 = f32[65,8,128]{0,1,2:T(8,128)S(1)} all-gather(f32[65,8,8]{0,1,2:T(8,128)S(1)} %copy.289), channel_id=1, replica_groups=mesh['cols'=1,'trc'=16,'lev'=2] {'trc'}, dimensions={2}, use_global_device_ids=true | all-gather | bytes 282880 | tf_op jit(solution)/shard_map/all_gather | solution.py:171
  135.6 21.1 %all_gather.31 = f32[64,9,128]{0,2,1:T(8,128)S(1)} all-gather(f32[64,9,8]{0,2,1:T(8,128)S(1)} %get-tuple-element.259), channel_id=1, replica_groups=mesh['cols'=1,'trc'=16,'lev'=2] {'trc'}, dimensions={2}, use_global_device_ids=true | all-gather | bytes 313344 | tf_op jit(solution)/shard_map/all_gather | solution.py:169
  167.2 6.7 %multiply_add_fusion.5 = f32[4,65,8,128]{1,3,2,0:T(8,128)S(1)} fusion(f32[4,2,8,128]{1,3,2,0:T(8,128)} %copy.295, f32[4,64,8,128]{1,3,2,0:T(8,128)S(1)} %copy.298, f32[4,2,8,128]{1,3,2,0:T(8,128)} %copy.292, f32[65,8,128]{0,2,1:T(8,128)} %copy.297, f32[65,8,128]{0,2,1:T(8,128)} %copy.291), kind=kLoop, calls=%fused_computation.72 | loop fusion | flops 7454720 | bytes 2711552 | tf_op jit(solution)/shard_map/add | solution.py:66
  174.0 4.9 %multiply_add_fusion.1 = f32[4,64,9,128]{1,3,2,0:T(8,128)S(1)} fusion(f32[4,64,2,128]{1,3,2,0:T(8,128)} %collective-permute-done.9, f32[4,64,8,128]{1,3,2,0:T(8,128)S(1)} %copy.298, f32[4,64,2,128]{1,3,2,0:T(8,128)} %collective-permute-done.8, f32[64,9,128]{0,2,1:T(8,128)S(1)} %get-tuple-element.246, f32[64,9,128]{0,2,1:T(8,128)S(1)} %get-tuple-element.245), kind=kLoop, calls=%fused_computation.24 | loop fusion | flops 8257536 | bytes 3342336 | tf_op jit(solution)/shard_map/add | solution.py:66
  192.8 5.8 %collective-permute-start.14 = (f32[4,2,8,128]{3,2,1,0:T(8,128)}, f32[4,2,8,128]{3,2,1,0:T(8,128)}, u32[]{:S(2)}, u32[]{:S(2)}) collective-permute-start(f32[4,2,8,128]{3,2,1,0:T(8,128)} %copy.299), channel_id=1, source_target_pairs={{0,1},{2,3},{4,5},{6,7},{8,9},{10,11},{12,13},{14,15},{16,17},{18,... | collective-permute-start | bytes 98312 | tf_op jit(solution)/shard_map/ppermute | solution.py:36
  198.6 4.7 %collective-permute-start.13 = (f32[4,64,2,128]{1,3,2,0:T(8,128)}, f32[4,64,2,128]{1,3,2,0:T(8,128)}, u32[]{:S(2)}, u32[]{:S(2)}) collective-permute-start(f32[4,64,2,128]{1,3,2,0:T(8,128)} %get-tuple-element.232), channel_id=1, source_target_pairs={{0,0},{1,1},{2,2},{3,3},{4,4},{5,5},{6,6},{7,7},{8,8},{9,9},{10,10... | collective-permute-start | bytes 786440 | tf_op jit(solution)/shard_map/ppermute | solution.py:39
  203.3 4.7 %collective-permute-start.12 = (f32[4,64,2,128]{1,3,2,0:T(8,128)}, f32[4,64,2,128]{1,3,2,0:T(8,128)}, u32[]{:S(2)}, u32[]{:S(2)}) collective-permute-start(f32[4,64,2,128]{1,3,2,0:T(8,128)} %get-tuple-element.231), channel_id=1, source_target_pairs={{0,0},{1,1},{2,2},{3,3},{4,4},{5,5},{6,6},{7,7},{8,8},{9,9},{10,10... | collective-permute-start | bytes 786440 | tf_op jit(solution)/shard_map/ppermute | solution.py:36
  208.1 5.9 %multiply_add_fusion.2 = f32[4,64,8,129]{1,3,2,0:T(8,128)} fusion(f32[4,64,8,2]{1,3,2,0:T(2,128)} %get-tuple-element.234, f32[4,64,8,128]{1,3,2,0:T(8,128)S(1)} %fusion.21, f32[4,64,8,2]{1,3,2,0:T(2,128)S(1)} %get-tuple-element.233, f32[64,8,129]{0,2,1:T(8,128)} %copy-done.5, f32[64,8,129]{0,2,1:T(8,128)} %copy-done.6), kind=kLoop, calls=%fused_computation.37 | loop fusion | flops 7397376 | bytes 2666496 | tf_op jit(solution)/shard_map/add | solution.py:66
  219.5 6.5 %multiply_add_fusion.4 = f32[4,65,8,128]{1,3,2,0:T(8,128)S(1)} fusion(f32[4,2,8,128]{1,3,2,0:T(8,128)} %copy.302, f32[4,64,8,128]{1,3,2,0:T(8,128)S(1)} %fusion.21, f32[4,2,8,128]{1,3,2,0:T(8,128)} %copy.300, f32[65,8,128]{0,2,1:T(8,128)} %copy.297, f32[65,8,128]{0,2,1:T(8,128)} %copy.291), kind=kLoop, calls=%fused_computation.71 | loop fusion | flops 7454720 | bytes 2711552 | tf_op jit(solution)/shard_map/add | solution.py:66
  226.0 4.9 %multiply_add_fusion = f32[4,64,9,128]{1,3,2,0:T(8,128)S(1)} fusion(f32[4,64,2,128]{1,3,2,0:T(8,128)} %collective-permute-done.13, f32[4,64,8,128]{1,3,2,0:T(8,128)S(1)} %fusion.21, f32[4,64,2,128]{1,3,2,0:T(8,128)} %collective-permute-done.12, f32[64,9,128]{0,2,1:T(8,128)S(1)} %get-tuple-element.246, f32[64,9,128]{0,2,1:T(8,128)S(1)} %get-tuple-element.245), kind=kLoop, calls=%fused_computation.23 | loop fusion | flops 8257536 | bytes 3342336 | tf_op jit(solution)/shard_map/add | solution.py:66
  240.5 13.1 %all-to-all-done = bf16[16,2,8192]{2,1,0:T(2,128)(2,1)S(1)} async-done(((bf16[16,2,8192]{2,1,0:T(2,128)(2,1)}), bf16[16,2,8192]{2,1,0:T(2,128)(2,1)S(1)}, u32[]{:S(2)}, u32[]{:S(2)}) %all-to-all-start) | async-done | bytes 524320 | tf_op jit(solution)/shard_map/all_to_all | solution.py:192
  267.8 6.3 %fusion.93 = f32[64,8,8]{2,1,0:T(8,128)S(1)} fusion(f32[64,8,8]{2,1,0:T(8,128)S(1)} %copy.307), kind=kOutput, calls=%fused_computation.205 | output fusion | flops 258048 | bytes 32768 | tf_op jit(solution)/shard_map/jit(cumsum)/reduce_window_sum | solution.py:202
  274.3 4.3 %all-gather.2 = f32[16,8]{1,0:T(8,128)S(1)} all-gather(f32[8,8]{1,0:T(8,128)S(1)} %get-tuple-element.195), channel_id=4, replica_groups=mesh['cols'=1,'trc'=16,'lev'=2] {'lev'}, dimensions={0}, use_global_device_ids=true | all-gather | bytes 768 | tf_op jit(solution)/shard_map/all_gather | solution.py:19
  279.3 9.9 %all-to-all-done.1 = f32[16,1,16384]{2,1,0:T(1,128)S(1)} async-done(((f32[16,1,16384]{2,1,0:T(1,128)}), f32[16,1,16384]{2,1,0:T(1,128)S(1)}, u32[]{:S(2)}, u32[]{:S(2)}) %all-to-all-start.1) | async-done | bytes 1048608 | tf_op jit(solution)/shard_map/all_to_all | solution.py:198
  (173 shorter events, 96.3 us)
Async XLA Ops:
  0.6 254.4 %copy-start = (bf16[64,64]{1,0:T(8,128)(2,1)S(1)}, bf16[64,64]{1,0:T(8,128)(2,1)}, u32[]{:S(2)}) copy-start(bf16[64,64]{1,0:T(8,128)(2,1)} %param.21) | copy-start | bytes 24580
  13.6 25.8 %copy-start.17 = (f32[64,8,8]{0,2,1:T(8,128)}, f32[64,8,8]{0,2,1:T(8,128)S(1)}, u32[]{:S(2)}) copy-start(f32[64,8,8]{0,2,1:T(8,128)S(1)} %get-tuple-element.228) | copy-start | bytes 49156
  17.4 15.8 %collective-permute-start = (f32[6,64,1,8]{1,3,2,0:T(8,128)S(1)}, f32[6,64,1,8]{1,3,2,0:T(8,128)S(1)}, u32[]{:S(2)}, u32[]{:S(2)}) collective-permute-start(f32[6,64,1,8]{1,3,2,0:T(8,128)S(1)} %get-tuple-element.256), channel_id=1, source_target_pairs={{0,0},{1,1},{2,2},{3,3},{4,4},{5,5},{6,6},{7,7},{8,8},{9,9},{10,10... | collective-permute-start | bytes 36872 | tf_op jit(solution)/shard_map/ppermute | solution.py:39
  17.4 15.8 %collective-permute-start.1 = (f32[6,64,1,8]{1,3,2,0:T(8,128)S(1)}, f32[6,64,1,8]{1,3,2,0:T(8,128)S(1)}, u32[]{:S(2)}, u32[]{:S(2)}) collective-permute-start(f32[6,64,1,8]{1,3,2,0:T(8,128)S(1)} %get-tuple-element.255), channel_id=1, source_target_pairs={{0,0},{1,1},{2,2},{3,3},{4,4},{5,5},{6,6},{7,7},{8,8},{9,9},{10,10... | collective-permute-start | bytes 36872 | tf_op jit(solution)/shard_map/ppermute | solution.py:36
  18.8 142.8 %collective-permute-start.11 = (f32[4,2,8,128]{3,2,1,0:T(8,128)}, f32[4,2,8,128]{3,2,1,0:T(8,128)}, u32[]{:S(2)}, u32[]{:S(2)}) collective-permute-start(f32[4,2,8,128]{3,2,1,0:T(8,128)} %get-tuple-element.244), channel_id=1, source_target_pairs={{1,0},{3,2},{5,4},{7,6},{9,8},{11,10},{13,12},{15,14},{17,16},{19,... | collective-permute-start | bytes 98312 | tf_op jit(solution)/shard_map/ppermute | solution.py:39
  20.2 144.3 %collective-permute-start.10 = (f32[4,2,8,128]{3,2,1,0:T(8,128)}, f32[4,2,8,128]{3,2,1,0:T(8,128)}, u32[]{:S(2)}, u32[]{:S(2)}) collective-permute-start(f32[4,2,8,128]{3,2,1,0:T(8,128)} %get-tuple-element.243), channel_id=1, source_target_pairs={{0,1},{2,3},{4,5},{6,7},{8,9},{10,11},{12,13},{14,15},{16,17},{18,... | collective-permute-start | bytes 98312 | tf_op jit(solution)/shard_map/ppermute | solution.py:36
  26.6 147.3 %copy-start.1 = (f32[4,64,8,128]{1,3,2,0:T(8,128)}, f32[4,64,8,128]{1,3,2,0:T(8,128)S(1)}, u32[]{:S(2)}) copy-start(f32[4,64,8,128]{1,3,2,0:T(8,128)S(1)} %copy.298) | copy-start | bytes 3145732
  27.8 146.1 %collective-permute-start.9 = (f32[4,64,2,128]{1,3,2,0:T(8,128)}, f32[4,64,2,128]{1,3,2,0:T(8,128)}, u32[]{:S(2)}, u32[]{:S(2)}) collective-permute-start(f32[4,64,2,128]{1,3,2,0:T(8,128)} %get-tuple-element.238), channel_id=1, source_target_pairs={{0,0},{1,1},{2,2},{3,3},{4,4},{5,5},{6,6},{7,7},{8,8},{9,9},{10,10... | collective-permute-start | bytes 786440 | tf_op jit(solution)/shard_map/ppermute | solution.py:39
  33.3 6.1 %collective-permute-start.3 = (f32[6,64,10,1]{1,3,2,0:T(1,128)S(1)}, f32[6,64,10,1]{1,3,2,0:T(1,128)S(1)}, u32[]{:S(2)}, u32[]{:S(2)}) collective-permute-start(f32[6,64,10,1]{1,3,2,0:T(1,128)S(1)} %get-tuple-element.254), channel_id=1, source_target_pairs={{0,2},{2,4},{4,6},{6,8},{8,10},{10,12},{12,14},{14,16},{16,18},{18... | collective-permute-start | bytes 46088 | tf_op jit(solution)/shard_map/ppermute | solution.py:36
  33.3 6.0 %collective-permute-start.2 = (f32[6,64,10,1]{1,3,2,0:T(1,128)S(1)}, f32[6,64,10,1]{1,3,2,0:T(1,128)S(1)}, u32[]{:S(2)}, u32[]{:S(2)}) collective-permute-start(f32[6,64,10,1]{1,3,2,0:T(1,128)S(1)} %get-tuple-element.253), channel_id=1, source_target_pairs={{2,0},{4,2},{6,4},{8,6},{10,8},{12,10},{14,12},{16,14},{18,16},{20... | collective-permute-start | bytes 46088 | tf_op jit(solution)/shard_map/ppermute | solution.py:39
  39.3 26.5 %copy-start.20 = (f32[6,64,10,1]{1,3,2,0:T(1,128)}, f32[6,64,10,1]{1,3,2,0:T(1,128)S(1)}, u32[]{:S(2)}) copy-start(f32[6,64,10,1]{1,3,2,0:T(1,128)S(1)} %collective-permute-done.2) | copy-start | bytes 46084
  39.4 200.3 %copy-start.9 = (f32[64,8,8]{0,2,1:T(8,128)}, f32[64,8,8]{0,2,1:T(8,128)S(1)}, u32[]{:S(2)}) copy-start(f32[64,8,8]{0,2,1:T(8,128)S(1)} %fusion.60) | copy-start | bytes 49156
  62.8 13.9 %collective-permute-start.7 = (f32[64,8,1]{0,2,1:T(1,128)}, f32[64,8,1]{0,2,1:T(1,128)}, u32[]{:S(2)}, u32[]{:S(2)}) collective-permute-start(f32[64,8,1]{0,2,1:T(1,128)} %slice.461), channel_id=1, source_target_pairs={{0,2},{2,4},{4,6},{6,8},{8,10},{10,12},{12,14},{14,16},{16,18},{18... | collective-permute-start | bytes 6152 | tf_op jit(solution)/shard_map/ppermute | solution.py:47
  64.0 70.2 %copy-start.11 = (f32[64,8,8]{0,2,1:T(8,128)}, f32[64,8,8]{0,2,1:T(8,128)S(1)}, u32[]{:S(2)}) copy-start(f32[64,8,8]{0,2,1:T(8,128)S(1)} %fusion.72) | copy-start | bytes 49156
  64.6 12.2 %collective-permute-start.4 = (f32[64,1,8]{0,2,1:T(8,128)}, f32[64,1,8]{0,2,1:T(8,128)}, u32[]{:S(2)}, u32[]{:S(2)}) collective-permute-start(f32[64,1,8]{0,2,1:T(8,128)} %slice.454), channel_id=1, source_target_pairs={{0,0},{1,1},{2,2},{3,3},{4,4},{5,5},{6,6},{7,7},{8,8},{9,9},{10,10... | collective-permute-start | bytes 6152 | tf_op jit(solution)/shard_map/ppermute | solution.py:47
  76.7 29.4 %collective-permute-start.6 = (f32[6,1,10,10]{1,0,3,2:T(8,128)S(1)}, f32[6,1,10,10]{1,0,3,2:T(8,128)}, u32[]{:S(2)}, u32[]{:S(2)}) collective-permute-start(f32[6,1,10,10]{1,0,3,2:T(8,128)S(1)} %get-tuple-element.250), channel_id=1, source_target_pairs={{1,0},{0,1},{3,2},{2,3},{5,4},{4,5},{7,6},{6,7},{9,8},{8,9},{11,10... | collective-permute-start | bytes 7208 | tf_op jit(solution)/shard_map/ppermute | solution.py:39
  76.8 34.0 %collective-permute-start.5 = (f32[6,1,10,10]{1,0,3,2:T(8,128)S(1)}, f32[6,1,10,10]{1,0,3,2:T(8,128)}, u32[]{:S(2)}, u32[]{:S(2)}) collective-permute-start(f32[6,1,10,10]{1,0,3,2:T(8,128)S(1)} %get-tuple-element.249), channel_id=1, source_target_pairs={{0,1},{1,0},{2,3},{3,2},{4,5},{5,4},{6,7},{7,6},{8,9},{9,8},{10,11... | collective-permute-start | bytes 7208 | tf_op jit(solution)/shard_map/ppermute | solution.py:36
  106.1 67.8 %collective-permute-start.8 = (f32[4,64,2,128]{1,3,2,0:T(8,128)}, f32[4,64,2,128]{1,3,2,0:T(8,128)}, u32[]{:S(2)}, u32[]{:S(2)}) collective-permute-start(f32[4,64,2,128]{1,3,2,0:T(8,128)} %get-tuple-element.237), channel_id=1, source_target_pairs={{0,0},{1,1},{2,2},{3,3},{4,4},{5,5},{6,6},{7,7},{8,8},{9,9},{10,10... | collective-permute-start | bytes 786440 | tf_op jit(solution)/shard_map/ppermute | solution.py:36
  188.7 25.2 %collective-permute-start.15 = (f32[4,2,8,128]{3,2,1,0:T(8,128)}, f32[4,2,8,128]{3,2,1,0:T(8,128)}, u32[]{:S(2)}, u32[]{:S(2)}) collective-permute-start(f32[4,2,8,128]{3,2,1,0:T(8,128)} %copy.301), channel_id=1, source_target_pairs={{1,0},{3,2},{5,4},{7,6},{9,8},{11,10},{13,12},{15,14},{17,16},{19,... | collective-permute-start | bytes 98312 | tf_op jit(solution)/shard_map/ppermute | solution.py:39
  192.8 23.9 %collective-permute-start.14 = (f32[4,2,8,128]{3,2,1,0:T(8,128)}, f32[4,2,8,128]{3,2,1,0:T(8,128)}, u32[]{:S(2)}, u32[]{:S(2)}) collective-permute-start(f32[4,2,8,128]{3,2,1,0:T(8,128)} %copy.299), channel_id=1, source_target_pairs={{0,1},{2,3},{4,5},{6,7},{8,9},{10,11},{12,13},{14,15},{16,17},{18,... | collective-permute-start | bytes 98312 | tf_op jit(solution)/shard_map/ppermute | solution.py:36
  198.6 27.4 %collective-permute-start.13 = (f32[4,64,2,128]{1,3,2,0:T(8,128)}, f32[4,64,2,128]{1,3,2,0:T(8,128)}, u32[]{:S(2)}, u32[]{:S(2)}) collective-permute-start(f32[4,64,2,128]{1,3,2,0:T(8,128)} %get-tuple-element.232), channel_id=1, source_target_pairs={{0,0},{1,1},{2,2},{3,3},{4,4},{5,5},{6,6},{7,7},{8,8},{9,9},{10,10... | collective-permute-start | bytes 786440 | tf_op jit(solution)/shard_map/ppermute | solution.py:39
  203.3 22.7 %collective-permute-start.12 = (f32[4,64,2,128]{1,3,2,0:T(8,128)}, f32[4,64,2,128]{1,3,2,0:T(8,128)}, u32[]{:S(2)}, u32[]{:S(2)}) collective-permute-start(f32[4,64,2,128]{1,3,2,0:T(8,128)} %get-tuple-element.231), channel_id=1, source_target_pairs={{0,0},{1,1},{2,2},{3,3},{4,4},{5,5},{6,6},{7,7},{8,8},{9,9},{10,10... | collective-permute-start | bytes 786440 | tf_op jit(solution)/shard_map/ppermute | solution.py:36
  235.6 18.0 %all-to-all-start = ((bf16[16,2,8192]{2,1,0:T(2,128)(2,1)}), bf16[16,2,8192]{2,1,0:T(2,128)(2,1)S(1)}, u32[]{:S(2)}, u32[]{:S(2)}) async-start(bf16[16,2,8192]{2,1,0:T(2,128)(2,1)} %reshape.73), calls=%async_computation | async-start | bytes 1048576 | tf_op jit(solution)/shard_map/all_to_all | solution.py:192
  262.2 27.1 %all-to-all-start.1 = ((f32[16,1,16384]{2,1,0:T(1,128)}), f32[16,1,16384]{2,1,0:T(1,128)S(1)}, u32[]{:S(2)}, u32[]{:S(2)}) async-start(f32[16,1,16384]{2,1,0:T(1,128)} %reshape.75), calls=%async_computation.1 | async-start | bytes 2097152 | tf_op jit(solution)/shard_map/all_to_all | solution.py:198
  (22 other events, 207.8 us)
where the time goes:
time: 301 us; the launch traced here: 297 us
  blocking collectives  87.9 us (29%)
  other arithmetic  76.6 us (25%)
  local copies, waits for them, and re-layouts  57 us (19%)
  starting transfers between devices  49.3 us (16%)
  waiting for transfers between devices  24 us (8%)
    add x6, other arithmetic, limited_div(): jnp.maximum(face_speed, 0.0) * plus_side  34.7 us
    all_gather x3, blocking collectives, entering(): gathered = lax.all_gather(part, axis)  27.1 us
    ppermute x7, starting transfers between devices, extended(): lax.ppermute(lax.slice_in_dim(block, block.shape[dim] - width, None, axis...  23.2 us
    all_gather x1, blocking collectives, shards(): lax.all_gather(faces_east, 'trc', axis=2, tiled=True)  21.1 us
    all_gather x1, blocking collectives, shards(): lax.all_gather(meridional_speed_final, 'trc', axis=2, tiled=True)  21 us
    all_gather x1, blocking collectives, shards(): lax.all_gather(faces_vertical, 'trc', axis=2, tiled=True)  18.7 us
    ppermute x7, starting transfers between devices, extended(): lax.ppermute(lax.slice_in_dim(block, 0, width, axis=dim), axis, backward)  16.5 us
    unnamed x67, local copies, waits for them, and re-layouts  15.1 us
  transfers between devices with their start and end apart: 18, of which 3 were waited for; matrix products, arithmetic and copies ran while one was open for 27% of the time, Pallas kernels for 0%

commit v1 on v0

v1 whole, which is shorter than its diff:
```python
import math

import jax
import jax.numpy as jnp
from jax import lax
from jax.experimental import pallas as pl
from jax.experimental.pallas import tpu as pltpu
from jax.sharding import PartitionSpec as P

viscosity = 0.2
buoyancy = 0.25
marine_advance = 0.05
tracer_step = 0.2
level_step = 0.04
react_step = 0.25
warming_amount = 60.0

speed_bound = 3.0
hydro_bound = 6.0
species_bound = 2.0
coupling_bound = 0.75

LANES = 128
DRY = 1e30
F32 = jnp.float32


def call(kernel, out_shape, args, specs=None, scratch=(), name=None):
    vmem = pl.BlockSpec(memory_space=pltpu.VMEM)
    outs = jax.tree.map(lambda _: vmem, out_shape)
    return pl.pallas_call(
        kernel,
        out_shape=out_shape,
        in_specs=[vmem] * len(args) if specs is None else specs,
        out_specs=outs,
        scratch_shapes=list(scratch),
        compiler_params=pltpu.CompilerParams(vmem_limit_bytes=40 * 1024 * 1024),
        name=name,
    )(*args)


def f32(*shape):
    return jax.ShapeDtypeStruct(shape, F32)


def shift(a, steps, axis):
    return pltpu.roll(a, (-steps) % a.shape[axis], axis)


def minmod(p, r):
    return jnp.maximum(jnp.minimum(p, r), 0.0) + jnp.minimum(jnp.maximum(p, r), 0.0)


def sideways(c, speed, axis):
    d = shift(c, 1, axis) - c
    half = 0.5 * minmod(shift(d, -1, axis), d)
    flux = speed * jnp.where(speed > 0.0, c + half, shift(c - half, 1, axis))
    return flux - shift(flux, -1, axis)


def exchange_levels(part):
    return lax.ppermute(part, "lev", [(0, 1), (1, 0)])


def shards(
    potential_warmth,
    saltiness_anomaly,
    zonal_speed,
    meridional_speed,
    marine_indicator,
    species_concentrations,
    coupling_matrix,
    species_guild_number,
    guild_extinction_coefficient,
):
    cols, ntrc, nlev = lax.axis_size("cols"), lax.axis_size("trc"), lax.axis_size("lev")
    D, X, Y = potential_warmth.shape
    T = species_concentrations.shape[0]
    NT = coupling_matrix.shape[0]
    YG = species_concentrations.shape[3]
    assert nlev == 2 and YG == LANES and X % 8 == 0 and Y % 8 == 0 and ntrc % 2 == 0
    assert LANES % D == 0 and D % 8 == 0 and X % (LANES // D) == 0
    H = X if cols > 1 else 0
    XE = X + 2 * H
    W, DX = D * XE, D * X
    G = LANES // D
    XL = XE // G

    def widen(block, dim):
        if H == 0:
            return block
        ahead = [(i, (i + 1) % cols) for i in range(cols)]
        back = [(i, (i - 1) % cols) for i in range(cols)]
        low = lax.ppermute(block, "cols", ahead)
        high = lax.ppermute(block, "cols", back)
        return jnp.concatenate([low, block, high], axis=dim)

    warmth, salt, zonal, merid, marine = (
        widen(jnp.transpose(a, (1, 2, 0)), 0)
        for a in (potential_warmth, saltiness_anomaly, zonal_speed, meridional_speed, marine_indicator)
    )
    species = widen(species_concentrations, 2)
    NP = ntrc // 2
    pairs_apart = [[2 * g + c for g in range(NP)] for c in range(2)]

    def pack(t_ref, s_ref, u_ref, v_ref, m_ref, pay_ref, lo_ref, hi_ref, lt_ref):
        t, s = t_ref[...], s_ref[...]
        density = jnp.where(m_ref[...] > 0, 0.8 * s - 0.2 * t, DRY)
        for f, a in enumerate((density, u_ref[...], v_ref[...])):
            rows = jnp.concatenate([a[g * XL : (g + 1) * XL] for g in range(G)], axis=2)
            rows = rows.reshape(XL * Y, LANES)
            for g in range(NP):
                pay_ref[g, f * XL * Y : (f + 1) * XL * Y] = rows
        lane = lax.broadcasted_iota(jnp.int32, (Y, LANES), 1)
        upper = lax.axis_index("lev") == 0
        for i, a in enumerate((t, s)):
            edge = jnp.zeros((Y, LANES), F32)
            for x in range(XE):
                lo_ref[i * XE + x : i * XE + x + 1] = a[x, 0:1]
                hi_ref[i * XE + x : i * XE + x + 1] = a[x, Y - 1 : Y]
                column = jnp.where(upper, a[x, :, D - 1 : D], a[x, :, 0:1])
                edge = jnp.where(lane == x, column, edge)
            lt_ref[i * Y : (i + 1) * Y] = edge

    payload, lo, hi, edges = call(
        pack,
        (f32(NP, 3 * XL * Y, LANES), f32(2 * XE, D), f32(2 * XE, D), f32(2 * Y, LANES)),
        (warmth, salt, zonal, merid, marine),
        name="pack_ocean",
    )
    mine = lax.all_to_all(
        payload, "trc", split_axis=0, concat_axis=0, tiled=True, axis_index_groups=pairs_apart
    )

    start = jnp.where(lax.axis_index("lev") == 0, D - 4, 0)
    outer_levels = exchange_levels(lax.dynamic_slice_in_dim(species, start, 4, 1))
    mine, outer_levels = lax.optimization_barrier((mine, outer_levels))
    other = lax.ppermute(mine, "trc", [(i, i ^ 1) for i in range(ntrc)])

    def unpack(a_ref, b_ref, e_ref, f_ref, l_ref):
        core = lax.axis_index("trc") % 2
        for f in range(3):
            for x in range(XL):
                at = slice((f * XL + x) * Y, (f * XL + x + 1) * Y)
                rows = []
                for g in range(NP):
                    a, b = a_ref[g, at], b_ref[g, at]
                    rows += [jnp.where(core == 0, a, b), jnp.where(core == 0, b, a)]
                turned = jnp.concatenate(rows, axis=0).T
                for g in range(G):
                    f_ref[f, pl.ds(x + g * XL, D, stride=XE), :] = turned[g * D : (g + 1) * D]
        density = f_ref[0].reshape(D, XE, YG)
        l_ref[0:XE] = jnp.sum(jnp.where(density < 0.5 * DRY, density, 0.0), axis=0)
        first = jnp.where(lax.axis_index("lev") == 0, D - 2, 0)
        for f in range(3):
            for k in range(2):
                at = (1 + 2 * f + k) * XE
                l_ref[at : at + XE] = f_ref[f, pl.ds(pl.multiple_of((first + k) * XE, 8), XE)]
        l_ref[7 * XE :] = e_ref[...]

    fields, own_levels = call(
        unpack, (f32(3, W, YG), f32(7 * XE + 2 * Y, YG)), (mine, other, edges), name="unpack_ocean"
    )
    fields = fields.reshape(3, D, XE, YG)
    far_levels = exchange_levels(own_levels)

    def speeds(f_ref, r_ref, uv_ref, fv_ref, sum_ref):
        lev = lax.axis_index("lev")
        above = jnp.where(lev > 0, r_ref[0:XE], 0.0)

        def far(f, k):
            at = (1 + 2 * f + k) * XE
            return r_ref[at : at + XE]

        def dense(raw):
            return jnp.where(raw < 0.5 * DRY, raw, 0.0)

        def level(e, raw, u, v, before):
            wet = jnp.where(raw < 0.5 * DRY, 1.0, 0.0)
            d = dense(raw)
            total = before + d
            p = buoyancy * (total - 0.5 * d)

            def moved(a, axis):
                mask = wet * shift(wet, 1, axis)
                lap = shift(a, 1, 0) + shift(a, -1, 0) + shift(a, 1, 1) + shift(a, -1, 1) - 4.0 * a
                return mask * (a + marine_advance * (-(shift(p, 1, axis) - p) + viscosity * lap))

            uv_ref[0, e] = moved(u, 0)
            uv_ref[1, e] = moved(v, 1)
            return total

        total = above - dense(far(0, 0)) - dense(far(0, 1))
        for k in range(2):
            total = level(k, far(0, k), far(1, k), far(2, k), total)
        total = lax.fori_loop(
            0,
            D,
            lambda k, t: level(k + 2, f_ref[0, k], f_ref[1, k], f_ref[2, k], t),
            above,
            unroll=4,
        )
        for k in range(2):
            total = level(D + 2 + k, far(0, k), far(1, k), far(2, k), total)

        def divergence(e):
            u, v = uv_ref[0, e], uv_ref[1, e]
            return u - shift(u, -1, 0) + v - shift(v, -1, 1)

        fv_ref[D + 2] = jnp.zeros((XE, YG), F32)
        below = -divergence(D + 2)
        fv_ref[D + 3] = below
        fv_ref[D + 4] = below - divergence(D + 3)

        def climb(i, total):
            e = D + 1 - i
            total = total + divergence(e)
            fv_ref[e] = total
            return total

        total = lax.fori_loop(0, D, climb, jnp.zeros((XE, YG), F32), unroll=4)
        sum_ref[...] = total
        for e in (1, 0):
            total = total + divergence(e)
            fv_ref[e] = total

    uv, fv, own_sum = call(
        speeds,
        (f32(2, D + 4, XE, YG), f32(D + 5, XE, YG), f32(XE, YG)),
        (fields, far_levels),
        name="face_speeds",
    )
    far_sum = exchange_levels(own_sum)

    def deeper(r_ref):
        return jnp.where(lax.axis_index("lev") == nlev - 1, 0.0, r_ref[...])

    def advect(c_ref, h_ref, uv_ref, fv_ref, r_ref, adv_ref, msg_ref, c_pad, a_pad, sem):
        lev = lax.axis_index("lev")
        copy = pltpu.make_async_copy(c_ref, c_pad.at[:, pl.ds(4, D)], sem)
        copy.start()
        below = deeper(r_ref)
        has_above, has_below = lev > 0, lev < nlev - 1
        for k in range(4):
            c_pad[:, k] = jnp.where(has_above, h_ref[:, k], 0.0)
            c_pad[:, D + 4 + k] = jnp.where(has_below, h_ref[:, k], 0.0)
        copy.wait()

        def step(src, off, e0, count, put):
            def face(e):
                w = fv_ref[e] + below
                return jnp.where((lev == 0) & (e == 2), 0.0, w)

            def slope(lo, mid, hi):
                return 0.5 * minmod(mid - lo, hi - mid)

            def down(e, up_cell, lo, mid, hi):
                half = slope(lo, mid, hi)
                w = face(e)
                return w * jnp.where(w > 0.0, up_cell, mid - half), mid + half

            c0 = src[:, e0 - 2 + off]
            c1 = src[:, e0 - 1 + off]
            c2 = src[:, e0 + off]
            c3 = src[:, e0 + 1 + off]
            up_cell = c1 + slope(c0, c1, c2)
            flux, up_cell = down(e0, up_cell, c1, c2, c3)

            def one(i, carry):
                mid, hi, flux, up_cell = carry
                e = e0 + i
                nxt = src[:, e + 2 + off]
                flux_next, up_next = down(e + 1, up_cell, mid, hi, nxt)
                u, v = uv_ref[0, e], uv_ref[1, e]
                flat = sideways(mid, u[None], 1) + sideways(mid, v[None], 2)
                put(i, mid - (tracer_step * flat + level_step * (flux_next - flux)))
                return hi, nxt, flux_next, up_next

            lax.fori_loop(0, count, one, (c2, c3, flux, up_cell), unroll=16)

        def keep(i, a):
            a_pad[:, i] = a

        step(c_pad, 2, 0, D + 4, keep)
        for k in range(2):
            a_pad[:, k] = jnp.where(has_above, a_pad[:, k], 0.0)
            a_pad[:, D + 2 + k] = jnp.where(has_below, a_pad[:, D + 2 + k], 0.0)

        def give(i, a):
            adv_ref[:, pl.ds(pl.multiple_of(i * X, 8), X)] = a[:, H : H + X]

        step(a_pad, 0, 2, D, give)
        for w in range(DX // LANES):
            turned = []
            for t in range(T):
                rows = [adv_ref[t, pl.ds(w * G + g, D, stride=X), :] for g in range(G)]
                turned.append(jnp.concatenate(rows, axis=0).T)
            for d in range(ntrc):
                rows = [turned[t][d * Y : (d + 1) * Y] for t in range(T)]
                msg_ref[d, :, w * LANES : (w + 1) * LANES] = jnp.concatenate(rows, axis=0).astype(
                    jnp.bfloat16
                )

    vmem = pl.BlockSpec(memory_space=pltpu.VMEM)
    advected, message = call(
        advect,
        (f32(T, DX, YG), jax.ShapeDtypeStruct((ntrc, T * Y, DX), jnp.bfloat16)),
        (species, outer_levels, uv, fv, far_sum),
        specs=[pl.BlockSpec(memory_space=pl.ANY)] + [vmem] * 4,
        scratch=(
            pltpu.VMEM((T, D + 8, XE, YG), F32),
            pltpu.VMEM((T, D + 4, XE, YG), F32),
            pltpu.SemaphoreType.DMA(()),
        ),
        name="advect_tracers",
    )
    gathered = lax.all_to_all(message, "trc", split_axis=0, concat_axis=0, tiled=True)

    ring = [(i, (i + 1) % ntrc) for i in range(ntrc)]
    south = lax.ppermute(hi, "trc", ring)
    north = lax.ppermute(lo, "trc", [(b, a) for a, b in ring])

    def ocean(
        t_ref, s_ref, uv_ref, fv_ref, r_ref, l_ref, so_ref, no_ref, sa_ref, wa_ref, ua_ref, va_ref, turn
    ):
        me, lev = lax.axis_index("trc"), lax.axis_index("lev")
        below = deeper(r_ref)
        for x in range(XE):
            def level_rows(ref, first):
                return ref[pl.ds(first * XE + x, D, stride=XE), :]

            under = below[x : x + 1]
            turn[0, x] = level_rows(uv_ref.at[0], 2).T
            turn[1, x] = level_rows(uv_ref.at[1], 2).T
            turn[2, x] = (level_rows(fv_ref, 2) + under).T
            turn[3, x] = (level_rows(fv_ref, 3) + under).T
        here = pl.ds(pl.multiple_of(me * Y, 8), Y)
        past = pl.ds(pl.multiple_of(lax.rem(me + ntrc - 1, ntrc) * Y, 8), Y)
        u, v, w, w_next = (turn[i, :, here] for i in range(4))
        v_south = turn[1, :, past][:, Y - 1 : Y]
        level = lax.broadcasted_iota(jnp.int32, (XE, Y, D), 2)
        row = lax.broadcasted_iota(jnp.int32, (XE, Y, D), 1)
        w = jnp.where((lev == 0) & (level == 0), 0.0, w)

        def east(a):
            return jnp.concatenate([a[1:], a[:1]], axis=0)

        def west(a):
            return jnp.concatenate([a[-1:], a[:-1]], axis=0)

        def donor(speed, near, far):
            return jnp.maximum(speed, 0.0) * near + jnp.minimum(speed, 0.0) * far

        def advance(c, i):
            so = jnp.stack([so_ref[i * XE + x : i * XE + x + 1] for x in range(XE)])
            no = jnp.stack([no_ref[i * XE + x : i * XE + x + 1] for x in range(XE)])
            tile = l_ref[7 * XE + i * Y : 7 * XE + (i + 1) * Y]
            edge = jnp.stack([tile[:, x : x + 1] for x in range(XE)])
            wide = jnp.concatenate([c, jnp.zeros((XE, Y, LANES - D), F32)], axis=2) if D < LANES else c
            upper = shift(wide, -1, 2)[:, :, :D]
            upper = jnp.where(level == 0, jnp.where(lev > 0, edge, 0.0), upper)
            lower = shift(wide, 1, 2)[:, :, :D]
            lower = jnp.where(level == D - 1, jnp.where(lev < nlev - 1, edge, 0.0), lower)
            fe = donor(u, c, east(c))
            fn = donor(v, c, jnp.where(row == Y - 1, no, shift(c, 1, 1)))
            fn_south = jnp.where(row == 0, donor(v_south, so, c[:, 0:1]), shift(fn, -1, 1))
            fall = donor(w_next, c, lower) - donor(w, upper, c)
            return c - marine_advance * ((fe - west(fe)) + (fn - fn_south) + fall)

        sa_ref[...] = advance(s_ref[...], 1)[H : H + X]
        wa_ref[...] = advance(t_ref[...], 0)[H : H + X]
        ua_ref[...] = u[H : H + X]
        va_ref[...] = v[H : H + X]

    saltiness_final, warmth_moved, zonal_speed_final, meridional_speed_final = call(
        ocean,
        (f32(X, Y, D),) * 4,
        (
            warmth,
            salt,
            uv.reshape(2, (D + 4) * XE, YG),
            fv.reshape((D + 5) * XE, YG),
            far_sum,
            far_levels,
            south,
            north,
        ),
        scratch=(pltpu.VMEM((4, XE, YG, D), F32),),
        name="own_ocean",
    )

    speed_most = speed_bound + marine_advance * (
        2 * buoyancy * hydro_bound * D * nlev + viscosity * 8 * speed_bound
    )
    growth = 1 + 4 * tracer_step * speed_most + 2 * level_step * (4 * speed_most * D * nlev)
    react_most = NT * coupling_bound * species_bound * growth**2
    unit = 2.0 ** max(0, math.ceil(math.log2(react_most / 65504.0)))

    def spread_columns(c_ref, o_ref):
        n = NT * Y

        def pick(shape, along):
            wide, narrow = (lax.broadcasted_iota(jnp.int32, shape, d) for d in (along, 1 - along))
            return jnp.where(wide // Y == narrow, 1.0, 0.0).astype(jnp.bfloat16)

        tall = jnp.dot(pick((n, NT), 0), c_ref[...], preferred_element_type=F32)
        full = jnp.dot(
            tall.astype(jnp.bfloat16), pick((NT, n), 1), preferred_element_type=F32
        )
        row, lane = (lax.broadcasted_iota(jnp.int32, (n, n), d) for d in (0, 1))
        o_ref[...] = jnp.where(row % Y == lane % Y, full, 0.0).astype(jnp.bfloat16)

    spread = call(
        spread_columns,
        jax.ShapeDtypeStruct((NT * Y, NT * Y), jnp.bfloat16),
        (coupling_matrix,),
        name="spread_coupling",
    )
    flat_tracers = gathered.reshape(NT * Y, DX)
    reaction = jnp.dot(spread, flat_tracers, preferred_element_type=F32)
    reaction = (reaction * (1.0 / unit)).astype(jnp.float16).reshape(ntrc, T * Y, DX)
    returned = lax.all_to_all(reaction, "trc", split_axis=0, concat_axis=0, tiled=True)

    def shade(x_ref, g_ref, k_ref, att_ref, cum_ref):
        att = jnp.zeros((Y, DX), F32)
        for d in range(ntrc):
            rows = x_ref[d].astype(F32)
            for t in range(T):
                att = att + k_ref[g_ref[d * T + t]] * rows[t * Y : (t + 1) * Y]
        att_ref[...] = att
        lane = lax.broadcasted_iota(jnp.int32, (Y, DX), 1)
        total = att
        width = 1
        while width < D:
            total = total + jnp.where(lane % D < width, 0.0, shift(total, -width, 1))
            width *= 2
        cum_ref[...] = total

    smem = pl.BlockSpec(memory_space=pltpu.SMEM)
    attenuation, shaded = call(
        shade,
        (f32(Y, DX), f32(Y, DX)),
        (gathered, species_guild_number, guild_extinction_coefficient),
        specs=[vmem, smem, smem],
        name="shade",
    )
    far_shade = exchange_levels(shaded)

    def heat(att_ref, cum_ref, r_ref, w_ref, m_ref, o_ref):
        att = att_ref[...]
        path = cum_ref[...] - att
        caught = 1.0 - jnp.exp(-att)
        lev = lax.axis_index("lev")
        for x in range(X):
            at = slice(x * D, (x + 1) * D)
            above = jnp.where(lev > 0, r_ref[:, (x + 1) * D - 1 : (x + 1) * D], 0.0)
            absorbed = jnp.exp(-(above + path[:, at])) * caught[:, at]
            o_ref[x] = w_ref[x] + warming_amount * (m_ref[x].astype(F32) * absorbed)

    warmth_final = call(
        heat,
        f32(X, Y, D),
        (attenuation, shaded, far_shade, warmth_moved, jnp.transpose(marine_indicator, (1, 2, 0))),
        name="heat",
    )

    def finish(r_ref, a_ref, o_ref):
        for t in range(T):
            for w in range(DX // LANES):
                rows = [
                    r_ref[d, t * Y : (t + 1) * Y, w * LANES : (w + 1) * LANES] for d in range(ntrc)
                ]
                turned = (react_step * unit) * jnp.concatenate(rows, axis=0).T
                for g in range(G):
                    at = pl.ds(w * G + g, D, stride=X)
                    o_ref[t, at, :] = a_ref[t, at, :] + turned[g * D : (g + 1) * D]

    species_final = call(
        finish, f32(T, DX, YG), (returned.astype(F32), advected), name="finish_tracers"
    )
    ocean_outputs = (warmth_final, saltiness_final, zonal_speed_final, meridional_speed_final)
    ocean_outputs = tuple(jnp.transpose(a, (2, 0, 1)) for a in ocean_outputs)
    return ocean_outputs + (species_final.reshape(T, D, X, YG),)


def solution(mesh):
    ocean = P("lev", "cols", "trc")
    in_specs = (ocean,) * 5 + (P("trc", "lev", "cols", None), P(), P(), P())
    out_specs = (ocean,) * 4 + (P("trc", "lev", "cols", None),)
    return jax.shard_map(shards, mesh=mesh, in_specs=in_specs, out_specs=out_specs, check_vma=False)
```

time: 301 us -> 86.5 us (0.29); the launches traced: 297 us -> 85.7 us
  blocking collectives: 87.9 us -> 0 us
  other arithmetic: 76.6 us -> 0.12 us
  local copies, waits for them, and re-layouts: 57 us -> 4.76 us
  starting transfers between devices: 49.3 us -> 25.9 us
  Pallas kernels: 0 us -> 16.5 us
  waiting for transfers between devices: 24 us -> 36.5 us
    all_gather x6 -> x0, blocking collectives: 87.9 us -> none  [the longest x3 27.1 us: entering(): gathered = lax.all_gather(part, axis)]
    add x13 -> x0, other arithmetic: 38.7 us -> none  [the longest x6 34.7 us: limited_div(): jnp.maximum(face_speed, 0.0) * plus_side]
    ppermute x16 -> x7, starting transfers between devices: 41.3 us -> 10.7 us  [the longest x4 6.21 us: exchange_levels(): return lax.ppermute(part, 'lev', [(0, 1), (1, 0)])]
    another operation x3 -> x0, other arithmetic: 19 us -> none  [the longest x1 6.33 us: shards(): deeper_sum = jnp.cumsum(divergence[::-1], axis=0)[::-1] + flow_next[None]]
    pallas_call x0 -> x9, Pallas kernels: none -> 16.5 us  [call(): pl.pallas_call(kernel, out_shape=out_shape, in_specs=[vmem] * len(args) i...]
    slice x15 -> x0, local copies, waits for them, and re-layouts: 15.9 us -> none  [the longest x7 10.4 us: extended(): lax.slice_in_dim(block, block.shape[dim] - width, None, axis=dim)]
    ppermute x16 -> x7, waiting for transfers between devices: 1.03 us -> 15.9 us  [the longest x4 7.28 us: exchange_levels(): return lax.ppermute(part, 'lev', [(0, 1), (1, 0)])]
    unnamed x67 -> x24, local copies, waits for them, and re-layouts: 15.1 us -> 3.82 us
  transfers between devices with their start and end apart: 18 -> 10, of which waited for: 3 -> 7; matrix products, arithmetic and copies ran while one was open for 27% -> 1% of each run, Pallas kernels for 0% -> 4%
where the time goes in v1:
time: 86.5 us; the launch traced here: 85.7 us
  waiting for transfers between devices  36.5 us (42%)
  starting transfers between devices  25.9 us (30%)
  Pallas kernels  16.5 us (19%)
  local copies, waits for them, and re-layouts  4.76 us (6%)
  matrix products  1.23 us (1%)
    pallas_call x9, Pallas kernels, call(): pl.pallas_call(kernel, out_shape=out_shape, in_specs=[vmem] * len(args) i...  16.5 us
    all_to_all x1, waiting for transfers between devices, shards(): lax.all_to_all(message, 'trc', split_axis=0, concat_axis=0, tiled=True)  14.1 us
    ppermute x4, waiting for transfers between devices, exchange_levels(): return lax.ppermute(part, 'lev', [(0, 1), (1, 0)])  7.28 us
    all_to_all x1, starting transfers between devices, shards(): lax.all_to_all(payload, 'trc', split_axis=0, concat_axis=0, tiled=True, a...  7.25 us
    ppermute x1, waiting for transfers between devices, shards(): south = lax.ppermute(hi, 'trc', ring)  6.94 us
    all_to_all x1, waiting for transfers between devices, shards(): lax.all_to_all(payload, 'trc', split_axis=0, concat_axis=0, tiled=True, a...  6.48 us
    ppermute x4, starting transfers between devices, exchange_levels(): return lax.ppermute(part, 'lev', [(0, 1), (1, 0)])  6.21 us
    ppermute x1, starting transfers between devices, shards(): north = lax.ppermute(lo, 'trc', [(b, a) for a, b in ring])  4.29 us
  transfers between devices with their start and end apart: 10, of which 7 were waited for; matrix products, arithmetic and copies ran while one was open for 1% of the time, Pallas kernels for 4%

profile of v1, /device:TPU:0, one launch (start us, length us, event | category | flops | bytes accessed | tf_op | source)
XLA Modules:
  0.0 85.7 jit_solution(14887530130246108806)
XLA Ops:
  4.4 0.9 %pack_ocean.1 = (f32[8,96,128]{2,1,0:T(8,128)}, f32[16,64]{1,0:T(8,128)S(1)}, f32[16,64]{1,0:T(8,128)S(1)}, f32[16,128]{1,0:T(8,128)S(1)}) custom-call(f32[8,8,64]{2,1,0:T(8,128)S(1)} %bitcast.25, f32[8,8,64]{2,1,0:T(8,128)S(1)} %bitcast.27, f32[8,8,64]{2,1,0:T(8,128)S(1)} %bitcast.29, f32[8,8,64]{2,1,0:T(8,128)S(1)} %bitcast.30, s32[8,8,64]{2,1,0:T(8,128)S(1)} %bitcast.23), custom_call_target="tpu_custom_call" | custom-call | tf_op jit(solution)/shard_map/pack_ocean/pallas_call | solution.py:31
  5.3 7.3 %all-to-all-start = ((f32[8,96,128]{2,1,0:T(8,128)}), f32[8,96,128]{2,1,0:T(8,128)S(1)}, u32[]{:S(2)}, u32[]{:S(2)}) async-start(f32[8,96,128]{2,1,0:T(8,128)} %get-tuple-element.24), calls=%async_computation | async-start | bytes 786432 | tf_op jit(solution)/shard_map/all_to_all | solution.py:131
  12.6 0.9 %constant_dynamic-slice_fusion = f32[4,4,8,128]{3,2,1,0:T(8,128)S(1)} fusion(f32[4,64,8,128]{3,2,1,0:T(8,128)} %c_ref.2, s32[]{:T(128)S(6)} %select_n.5), kind=kLoop, calls=%fused_computation.2 | loop fusion | bytes 131076 | tf_op jit(solution)/shard_map/dynamic_slice | solution.py:136
  13.5 1.5 %collective-permute-start = (f32[4,4,8,128]{3,2,1,0:T(8,128)S(1)}, f32[4,4,8,128]{3,2,1,0:T(8,128)S(1)}, u32[]{:S(2)}, u32[]{:S(2)}) collective-permute-start(f32[4,4,8,128]{3,2,1,0:T(8,128)S(1)} %constant_dynamic-slice_fusion), channel_id=1, source_target_pairs={{0,1},{1,0},{2,3},{3,2},{4,5},{5,4},{6,7},{7,6},{8,9},{9,8},{10,11... | collective-permute-start | bytes 196616 | tf_op jit(solution)/shard_map/ppermute | solution.py:62
  15.0 2.7 %collective-permute-done.h_ref = f32[4,4,8,128]{3,2,1,0:T(8,128)S(1)} collective-permute-done((f32[4,4,8,128]{3,2,1,0:T(8,128)S(1)}, f32[4,4,8,128]{3,2,1,0:T(8,128)S(1)}, u32[]{:S(2)}, u32[]{:S(2)}) %collective-permute-start) | collective-permute-done | bytes 65568 | tf_op jit(solution)/shard_map/ppermute | solution.py:62
  17.8 6.5 %all-to-all-done.a_ref = f32[8,96,128]{2,1,0:T(8,128)S(1)} async-done(((f32[8,96,128]{2,1,0:T(8,128)}), f32[8,96,128]{2,1,0:T(8,128)S(1)}, u32[]{:S(2)}, u32[]{:S(2)}) %all-to-all-start) | async-done | bytes 393248 | tf_op jit(solution)/shard_map/all_to_all | solution.py:131
  24.2 1.7 %collective-permute-done.1.b_ref = f32[8,96,128]{2,1,0:T(8,128)S(1)} collective-permute-done((f32[8,96,128]{2,1,0:T(8,128)S(1)}, f32[8,96,128]{2,1,0:T(8,128)S(1)}, u32[]{:S(2)}, u32[]{:S(2)}) %collective-permute-start.1) | collective-permute-done | bytes 393248 | tf_op jit(solution)/shard_map/ppermute | solution.py:138
  26.2 1.6 %collective-permute-start.2 = (f32[72,128]{1,0:T(8,128)S(1)}, f32[72,128]{1,0:T(8,128)S(1)}, u32[]{:S(2)}, u32[]{:S(2)}) collective-permute-start(f32[72,128]{1,0:T(8,128)S(1)} %get-tuple-element.29), channel_id=1, source_target_pairs={{0,1},{1,0},{2,3},{3,2},{4,5},{5,4},{6,7},{7,6},{8,9},{9,8},{10,11... | collective-permute-start | bytes 110600 | tf_op jit(solution)/shard_map/ppermute | solution.py:62
  27.8 2.4 %collective-permute-done.2.r_ref.l_ref = f32[72,128]{1,0:T(8,128)S(1)} collective-permute-done((f32[72,128]{1,0:T(8,128)S(1)}, f32[72,128]{1,0:T(8,128)S(1)}, u32[]{:S(2)}, u32[]{:S(2)}) %collective-permute-start.2) | collective-permute-done | bytes 36896 | tf_op jit(solution)/shard_map/ppermute | solution.py:62
  30.3 2.9 %face_speeds.1 = (f32[2,68,8,128]{3,2,1,0:T(8,128)S(1)}, f32[69,8,128]{2,1,0:T(8,128)S(1)}, f32[8,128]{1,0:T(8,128)S(1)}) custom-call(f32[3,64,8,128]{3,2,1,0:T(8,128)S(1)} %bitcast.22, f32[72,128]{1,0:T(8,128)S(1)} %collective-permute-done.2.r_ref.l_ref), custom_call_target="tpu_custom_call" | custom-call | tf_op jit(solution)/shard_map/face_speeds/pallas_call | solution.py:31
  33.2 1.5 %collective-permute-start.3 = (f32[8,128]{1,0:T(8,128)S(1)}, f32[8,128]{1,0:T(8,128)S(1)}, u32[]{:S(2)}, u32[]{:S(2)}) collective-permute-start(f32[8,128]{1,0:T(8,128)S(1)} %get-tuple-element.32), channel_id=1, source_target_pairs={{0,1},{1,0},{2,3},{3,2},{4,5},{5,4},{6,7},{7,6},{8,9},{9,8},{10,11... | collective-permute-start | bytes 12296 | tf_op jit(solution)/shard_map/ppermute | solution.py:62
  34.8 2.1 %collective-permute-done.3.r_ref = f32[8,128]{1,0:T(8,128)S(1)} collective-permute-done((f32[8,128]{1,0:T(8,128)S(1)}, f32[8,128]{1,0:T(8,128)S(1)}, u32[]{:S(2)}, u32[]{:S(2)}) %collective-permute-start.3) | collective-permute-done | bytes 4128 | tf_op jit(solution)/shard_map/ppermute | solution.py:62
  36.9 7.4 %advect_tracers.1 = (f32[4,512,128]{2,1,0:T(8,128)S(1)}, bf16[16,32,512]{2,1,0:T(8,128)(2,1)}) custom-call(f32[4,64,8,128]{3,2,1,0:T(8,128)S(1)} %copy-done, f32[4,4,8,128]{3,2,1,0:T(8,128)S(1)} %collective-permute-done.h_ref, f32[2,68,8,128]{3,2,1,0:T(8,128)S(1)} %get-tuple-element.30.uv_ref, f32[69,8,128]{2,1,0:T(8,128)S(1)} %get-tuple-element.31.fv_ref, ...), custom_call_target="tpu_custom_call" | custom-call | tf_op jit(solution)/shard_map/advect_tracers/pallas_call | solution.py:31
  44.3 3.7 %all-to-all-start.1 = ((bf16[16,32,512]{2,1,0:T(8,128)(2,1)}), bf16[16,32,512]{2,1,0:T(8,128)(2,1)S(1)}, u32[]{:S(2)}, u32[]{:S(2)}) async-start(bf16[16,32,512]{2,1,0:T(8,128)(2,1)} %get-tuple-element.33), calls=%async_computation.1 | async-start | bytes 1048576 | tf_op jit(solution)/shard_map/all_to_all | solution.py:317
  48.4 14.1 %all-to-all-done.1.x_ref = bf16[16,32,512]{2,1,0:T(8,128)(2,1)S(1)} async-done(((bf16[16,32,512]{2,1,0:T(8,128)(2,1)}), bf16[16,32,512]{2,1,0:T(8,128)(2,1)S(1)}, u32[]{:S(2)}, u32[]{:S(2)}) %all-to-all-start.1) | async-done | bytes 524320 | tf_op jit(solution)/shard_map/all_to_all | solution.py:317
  62.5 1.2 %fusion = f16[512,512]{0,1:T(8,128)(2,1)} fusion(bf16[512,512]{1,0:T(8,128)(2,1)S(1)} %spread_coupling.1, bf16[512,512]{1,0:T(8,128)(2,1)S(1)} %bitcast.20), kind=kOutput, calls=%fused_computation.1 | convolution fusion | flops 268959744 | bytes 1572864 | tf_op jit(solution)/shard_map/dot_general | solution.py:420
  63.7 4.2 %all-to-all-start.2 = ((f16[16,32,512]{2,1,0:T(8,128)(2,1)}), f16[16,32,512]{2,1,0:T(8,128)(2,1)S(1)}, u32[]{:S(2)}, u32[]{:S(2)}) async-start(f16[16,32,512]{2,1,0:T(8,128)(2,1)} %bitcast.32), calls=%async_computation.2 | async-start | bytes 1048576 | tf_op jit(solution)/shard_map/all_to_all | solution.py:422
  68.0 1.1 %shade.1 = (f32[8,512]{1,0:T(8,128)S(1)}, f32[8,512]{1,0:T(8,128)S(1)}) custom-call(bf16[16,32,512]{2,1,0:T(8,128)(2,1)S(1)} %all-to-all-done.1.x_ref, s32[64]{0:T(128)S(1)} %copy-done.10, f32[8]{0:T(128)S(1)} %copy-done.11), custom_call_target="tpu_custom_call" | custom-call | tf_op jit(solution)/shard_map/shade/pallas_call | solution.py:31
  69.1 1.6 %collective-permute-start.4 = (f32[8,512]{1,0:T(8,128)S(1)}, f32[8,512]{1,0:T(8,128)S(1)}, u32[]{:S(2)}, u32[]{:S(2)}) collective-permute-start(f32[8,512]{1,0:T(8,128)S(1)} %get-tuple-element.35.cum_ref), channel_id=1, source_target_pairs={{0,1},{1,0},{2,3},{3,2},{4,5},{5,4},{6,7},{7,6},{8,9},{9,8},{10,11... | collective-permute-start | bytes 49160 | tf_op jit(solution)/shard_map/ppermute | solution.py:62
  70.8 4.3 %collective-permute-start.6 = (f32[16,64]{1,0:T(8,128)S(1)}, f32[16,64]{1,0:T(8,128)S(1)}, u32[]{:S(2)}, u32[]{:S(2)}) collective-permute-start(f32[16,64]{1,0:T(8,128)S(1)} %get-tuple-element.37), channel_id=1, source_target_pairs={{2,0},{4,2},{6,4},{8,6},{10,8},{12,10},{14,12},{16,14},{18,16},{20... | collective-permute-start | bytes 12296 | tf_op jit(solution)/shard_map/ppermute | solution.py:321
  75.1 6.9 %collective-permute-done.5.so_ref = f32[16,64]{1,0:T(8,128)S(1)} collective-permute-done((f32[16,64]{1,0:T(8,128)S(1)}, f32[16,64]{1,0:T(8,128)S(1)}, u32[]{:S(2)}, u32[]{:S(2)}) %collective-permute-start.5) | collective-permute-done | bytes 4128 | tf_op jit(solution)/shard_map/ppermute | solution.py:320
  82.0 1.4 %own_ocean.1 = (f32[8,8,64]{2,1,0:T(8,128)}, f32[8,8,64]{2,1,0:T(8,128)S(1)}, f32[8,8,64]{2,1,0:T(8,128)}, f32[8,8,64]{2,1,0:T(8,128)}) custom-call(f32[8,8,64]{2,1,0:T(8,128)S(1)} %bitcast.26, f32[8,8,64]{2,1,0:T(8,128)S(1)} %bitcast.28, f32[2,544,128]{2,1,0:T(8,128)S(1)} %bitcast.19, f32[552,128]{1,0:T(8,128)S(1)} %bitcast.21, ...), custom_call_target="tpu_custom_call" | custom-call | tf_op jit(solution)/shard_map/own_ocean/pallas_call | solution.py:31
  83.4 0.8 heat.1
  84.3 1.4 %finish_tracers.1 = f32[4,512,128]{2,1,0:T(8,128)} custom-call(f32[16,32,512]{2,1,0:T(8,128)S(1)} %convert_element_type.11.r_ref, f32[4,512,128]{2,1,0:T(8,128)S(1)} %get-tuple-element.42.a_ref), custom_call_target="tpu_custom_call" | custom-call | tf_op jit(solution)/shard_map/finish_tracers/pallas_call | solution.py:31
  (32 shorter events, 4.8 us)
Async XLA Ops:
  0.6 0.8 copy-start.1
  1.4 0.8 copy-start.3
  2.2 0.8 copy-start.5
  2.9 0.8 copy-start.7
  3.7 0.8 copy-start.8
  5.3 18.9 %all-to-all-start = ((f32[8,96,128]{2,1,0:T(8,128)}), f32[8,96,128]{2,1,0:T(8,128)S(1)}, u32[]{:S(2)}, u32[]{:S(2)}) async-start(f32[8,96,128]{2,1,0:T(8,128)} %get-tuple-element.24), calls=%async_computation | async-start | bytes 786432 | tf_op jit(solution)/shard_map/all_to_all | solution.py:131
  12.5 24.3 %copy-start = (f32[4,64,8,128]{3,2,1,0:T(8,128)S(1)}, f32[4,64,8,128]{3,2,1,0:T(8,128)}, u32[]{:S(2)}) copy-start(f32[4,64,8,128]{3,2,1,0:T(8,128)} %c_ref.2) | copy-start | bytes 3145732
  13.5 4.3 %collective-permute-start = (f32[4,4,8,128]{3,2,1,0:T(8,128)S(1)}, f32[4,4,8,128]{3,2,1,0:T(8,128)S(1)}, u32[]{:S(2)}, u32[]{:S(2)}) collective-permute-start(f32[4,4,8,128]{3,2,1,0:T(8,128)S(1)} %constant_dynamic-slice_fusion), channel_id=1, source_target_pairs={{0,1},{1,0},{2,3},{3,2},{4,5},{5,4},{6,7},{7,6},{8,9},{9,8},{10,11... | collective-permute-start | bytes 196616 | tf_op jit(solution)/shard_map/ppermute | solution.py:62
  24.2 1.7 %collective-permute-start.1 = (f32[8,96,128]{2,1,0:T(8,128)S(1)}, f32[8,96,128]{2,1,0:T(8,128)S(1)}, u32[]{:S(2)}, u32[]{:S(2)}) collective-permute-start(f32[8,96,128]{2,1,0:T(8,128)S(1)} %all-to-all-done.a_ref), channel_id=1, source_target_pairs={{0,2},{2,0},{4,6},{6,4},{8,10},{10,8},{12,14},{14,12},{16,18},{18,... | collective-permute-start | bytes 1179656 | tf_op jit(solution)/shard_map/ppermute | solution.py:138
  26.2 4.0 %collective-permute-start.2 = (f32[72,128]{1,0:T(8,128)S(1)}, f32[72,128]{1,0:T(8,128)S(1)}, u32[]{:S(2)}, u32[]{:S(2)}) collective-permute-start(f32[72,128]{1,0:T(8,128)S(1)} %get-tuple-element.29), channel_id=1, source_target_pairs={{0,1},{1,0},{2,3},{3,2},{4,5},{5,4},{6,7},{7,6},{8,9},{9,8},{10,11... | collective-permute-start | bytes 110600 | tf_op jit(solution)/shard_map/ppermute | solution.py:62
  33.2 3.6 %collective-permute-start.3 = (f32[8,128]{1,0:T(8,128)S(1)}, f32[8,128]{1,0:T(8,128)S(1)}, u32[]{:S(2)}, u32[]{:S(2)}) collective-permute-start(f32[8,128]{1,0:T(8,128)S(1)} %get-tuple-element.32), channel_id=1, source_target_pairs={{0,1},{1,0},{2,3},{3,2},{4,5},{5,4},{6,7},{7,6},{8,9},{9,8},{10,11... | collective-permute-start | bytes 12296 | tf_op jit(solution)/shard_map/ppermute | solution.py:62
  44.2 3.8 %copy-start.9 = (bf16[64,64]{1,0:T(8,128)(2,1)S(1)}, bf16[64,64]{1,0:T(8,128)(2,1)}, u32[]{:S(2)}) copy-start(bf16[64,64]{1,0:T(8,128)(2,1)} %c_ref.3) | copy-start | bytes 24580
  44.3 18.2 %all-to-all-start.1 = ((bf16[16,32,512]{2,1,0:T(8,128)(2,1)}), bf16[16,32,512]{2,1,0:T(8,128)(2,1)S(1)}, u32[]{:S(2)}, u32[]{:S(2)}) async-start(bf16[16,32,512]{2,1,0:T(8,128)(2,1)} %get-tuple-element.33), calls=%async_computation.1 | async-start | bytes 1048576 | tf_op jit(solution)/shard_map/all_to_all | solution.py:317
  63.7 4.2 %copy-start.10 = (s32[64]{0:T(128)S(1)}, s32[64]{0:T(128)}, u32[]{:S(2)}) copy-start(s32[64]{0:T(128)} %g_ref.1) | copy-start | bytes 772
  63.7 4.3 %copy-start.11 = (f32[8]{0:T(128)S(1)}, f32[8]{0:T(128)}, u32[]{:S(2)}) copy-start(f32[8]{0:T(128)} %k_ref.1) | copy-start | bytes 100
  63.7 20.5 %all-to-all-start.2 = ((f16[16,32,512]{2,1,0:T(8,128)(2,1)}), f16[16,32,512]{2,1,0:T(8,128)(2,1)S(1)}, u32[]{:S(2)}, u32[]{:S(2)}) async-start(f16[16,32,512]{2,1,0:T(8,128)(2,1)} %bitcast.32), calls=%async_computation.2 | async-start | bytes 1048576 | tf_op jit(solution)/shard_map/all_to_all | solution.py:422
  68.0 14.1 %copy-start.4 = (f32[64,8,8]{0,2,1:T(8,128)S(1)}, f32[64,8,8]{0,2,1:T(8,128)}, u32[]{:S(2)}) copy-start(f32[64,8,8]{0,2,1:T(8,128)} %param.9) | copy-start | bytes 49156
  68.0 14.0 %copy-start.6 = (f32[64,8,8]{0,2,1:T(8,128)S(1)}, f32[64,8,8]{0,2,1:T(8,128)}, u32[]{:S(2)}) copy-start(f32[64,8,8]{0,2,1:T(8,128)} %param.10) | copy-start | bytes 49156
  69.1 14.4 %collective-permute-start.4 = (f32[8,512]{1,0:T(8,128)S(1)}, f32[8,512]{1,0:T(8,128)S(1)}, u32[]{:S(2)}, u32[]{:S(2)}) collective-permute-start(f32[8,512]{1,0:T(8,128)S(1)} %get-tuple-element.35.cum_ref), channel_id=1, source_target_pairs={{0,1},{1,0},{2,3},{3,2},{4,5},{5,4},{6,7},{7,6},{8,9},{9,8},{10,11... | collective-permute-start | bytes 49160 | tf_op jit(solution)/shard_map/ppermute | solution.py:62
  70.6 11.4 %collective-permute-start.5 = (f32[16,64]{1,0:T(8,128)S(1)}, f32[16,64]{1,0:T(8,128)S(1)}, u32[]{:S(2)}, u32[]{:S(2)}) collective-permute-start(f32[16,64]{1,0:T(8,128)S(1)} %get-tuple-element.36), channel_id=1, source_target_pairs={{0,2},{2,4},{4,6},{6,8},{8,10},{10,12},{12,14},{14,16},{16,18},{18... | collective-permute-start | bytes 12296 | tf_op jit(solution)/shard_map/ppermute | solution.py:320
  70.8 11.2 %collective-permute-start.6 = (f32[16,64]{1,0:T(8,128)S(1)}, f32[16,64]{1,0:T(8,128)S(1)}, u32[]{:S(2)}, u32[]{:S(2)}) collective-permute-start(f32[16,64]{1,0:T(8,128)S(1)} %get-tuple-element.37), channel_id=1, source_target_pairs={{2,0},{4,2},{6,4},{8,6},{10,8},{12,10},{14,12},{16,14},{18,16},{20... | collective-permute-start | bytes 12296 | tf_op jit(solution)/shard_map/ppermute | solution.py:321
  82.0 1.4 %copy-start.2 = (s32[64,8,8]{0,2,1:T(8,128)S(1)}, s32[64,8,8]{0,2,1:T(8,128)}, u32[]{:S(2)}) copy-start(s32[64,8,8]{0,2,1:T(8,128)} %param.13) | copy-start | bytes 49156

commit v2 on v1

v2 whole, which is shorter than its diff:
```python
import math

import jax
import jax.numpy as jnp
from jax import lax
from jax.experimental import pallas as pl
from jax.experimental.pallas import tpu as pltpu
from jax.sharding import PartitionSpec as P

viscosity = 0.2
buoyancy = 0.25
marine_advance = 0.05
tracer_step = 0.2
level_step = 0.04
react_step = 0.25
warming_amount = 60.0

speed_bound = 3.0
hydro_bound = 6.0
species_bound = 2.0
coupling_bound = 0.75

LANES = 128
DRY = 1e30
F32 = jnp.float32


def call(kernel, out_shape, args, specs=None, scratch=(), name=None, mib=40):
    vmem = pl.BlockSpec(memory_space=pltpu.VMEM)
    outs = jax.tree.map(lambda _: vmem, out_shape)
    return pl.pallas_call(
        kernel,
        out_shape=out_shape,
        in_specs=[vmem] * len(args) if specs is None else specs,
        out_specs=outs,
        scratch_shapes=list(scratch),
        compiler_params=pltpu.CompilerParams(vmem_limit_bytes=mib * 1024 * 1024),
        name=name,
    )(*args)


def f32(*shape):
    return jax.ShapeDtypeStruct(shape, F32)


def shift(a, steps, axis):
    return pltpu.roll(a, (-steps) % a.shape[axis], axis)


def minmod(p, r):
    return jnp.maximum(jnp.minimum(p, r), jnp.minimum(jnp.maximum(p, r), 0.0))


def sideways(c, speed, axis):
    d = 0.5 * (shift(c, 1, axis) - c)
    half = minmod(shift(d, -1, axis), d)
    flux = speed * jnp.where(speed > 0.0, c + half, shift(c - half, 1, axis))
    return flux - shift(flux, -1, axis)


def exchange_levels(part):
    return lax.ppermute(part, "lev", [(0, 1), (1, 0)])


def shards(
    potential_warmth,
    saltiness_anomaly,
    zonal_speed,
    meridional_speed,
    marine_indicator,
    species_concentrations,
    coupling_matrix,
    species_guild_number,
    guild_extinction_coefficient,
):
    cols, ntrc, nlev = lax.axis_size("cols"), lax.axis_size("trc"), lax.axis_size("lev")
    D, X, Y = potential_warmth.shape
    T = species_concentrations.shape[0]
    NT = coupling_matrix.shape[0]
    YG = species_concentrations.shape[3]
    assert nlev == 2 and YG == LANES and X % 8 == 0 and Y % 8 == 0 and ntrc % 2 == 0
    assert LANES % D == 0 and D % 8 == 0 and X % (2 * LANES // D) == 0
    H = X if cols > 1 else 0
    XE = X + 2 * H
    W, DX = D * XE, D * X
    G = LANES // D
    XL = XE // G

    def widen(block, dim):
        if H == 0:
            return block
        ahead = [(i, (i + 1) % cols) for i in range(cols)]
        back = [(i, (i - 1) % cols) for i in range(cols)]
        low = lax.ppermute(block, "cols", ahead)
        high = lax.ppermute(block, "cols", back)
        return jnp.concatenate([low, block, high], axis=dim)

    warmth, salt, zonal, merid, marine = (
        widen(jnp.transpose(a, (1, 2, 0)), 0)
        for a in (potential_warmth, saltiness_anomaly, zonal_speed, meridional_speed, marine_indicator)
    )
    species = widen(species_concentrations, 2)
    NP = ntrc // 2
    pairs_apart = [[2 * g + c for g in range(NP)] for c in range(2)]

    UV_ROWS, DENSE_ROWS = XL * Y, XL * Y // 2
    DRY_CODE = -(2**14)
    SCALES = 31

    def top(bound):
        return 2.0 ** math.ceil(math.log2(bound))

    tops = (top(hydro_bound * 1.001), top(speed_bound), top(speed_bound))
    codes = (2**14 - 1, 2**15 - 1, 2**15 - 1)

    def pack(t_any, s_any, u_any, v_any, m_any, c_any, pay_ref, lo_ref, hi_ref, out_ref, held, wet, sems):
        upper = lax.axis_index("lev") == 0
        first = pl.multiple_of(jnp.where(upper, D - 4, 0) * XE, 8)
        copies = [
            pltpu.make_async_copy(a, held.at[i], sems.at[i])
            for i, a in enumerate((t_any, s_any, u_any, v_any))
        ]
        copies.append(pltpu.make_async_copy(m_any, wet, sems.at[4]))
        for t in range(T):
            copies.append(
                pltpu.make_async_copy(
                    c_any.at[t, pl.ds(first, 4 * XE)],
                    out_ref.at[pl.ds(t * 4 * XE, 4 * XE)],
                    sems.at[5 + t],
                )
            )
        for copy in copies:
            copy.start()
        for copy in copies:
            copy.wait()
        t, s = held[0], held[1]
        sea = wet[...] > 0
        density = jnp.where(sea, 0.8 * s - 0.2 * t, 0.0)
        numbers, halves = 0, []
        for i, a in enumerate((density, held[2], held[3])):
            most = jnp.max(jnp.abs(a))
            unit, number = tops[i], 0
            for k in range(1, SCALES + 1):
                fits = most <= tops[i] * 2.0**-k
                unit = jnp.where(fits, tops[i] * 2.0**-k, unit)
                number = jnp.where(fits, k, number)
            code = jnp.floor(jnp.clip(a * (1.0 / unit), -1.0, 1.0) * codes[i] + 0.5).astype(jnp.int32)
            if i == 0:
                code = jnp.where(sea, code, DRY_CODE)
            numbers = numbers + number * 32**i
            code = jnp.concatenate([code[g * XL : (g + 1) * XL] for g in range(G)], axis=2)
            halves.append(code.reshape(XL * Y, LANES))
        density, u, v = halves
        lane = lax.broadcasted_iota(jnp.int32, (XL * Y, LANES), 1)
        density = density * 2 + (lax.shift_right_logical(numbers, lane % 16) & 1)
        rows = jnp.concatenate(
            [u * 65536 + (v & 65535), density[:DENSE_ROWS] * 65536 + (density[DENSE_ROWS:] & 65535)],
            axis=0,
        )
        for g in range(NP):
            pay_ref[g] = rows
        lane = lax.broadcasted_iota(jnp.int32, (Y, LANES), 1)
        for i, a in enumerate((t, s)):
            edge = jnp.zeros((Y, LANES), F32)
            for x in range(XE):
                lo_ref[i * XE + x : i * XE + x + 1] = a[x, 0:1]
                hi_ref[i * XE + x : i * XE + x + 1] = a[x, Y - 1 : Y]
                column = jnp.where(upper, a[x, :, D - 1 : D], a[x, :, 0:1])
                edge = jnp.where(lane == x, column, edge)
            out_ref[4 * T * XE + i * Y : 4 * T * XE + (i + 1) * Y] = edge

    species = species.reshape(T, W, YG)
    payload, lo, hi, outer = call(
        pack,
        (
            jax.ShapeDtypeStruct((NP, UV_ROWS + DENSE_ROWS, LANES), jnp.int32),
            f32(2 * XE, D),
            f32(2 * XE, D),
            f32(4 * T * XE + 2 * Y, LANES),
        ),
        (warmth, salt, zonal, merid, marine, species),
        specs=[pl.BlockSpec(memory_space=pl.ANY)] * 6,
        scratch=(
            pltpu.VMEM((4, XE, Y, D), F32),
            pltpu.VMEM((XE, Y, D), jnp.int32),
            pltpu.SemaphoreType.DMA((5 + T,)),
        ),
        name="pack_ocean",
        mib=60,
    )
    mine = lax.all_to_all(
        payload, "trc", split_axis=0, concat_axis=0, tiled=True, axis_index_groups=pairs_apart
    )
    far_outer = exchange_levels(outer)
    mine, far_outer = lax.optimization_barrier((mine, far_outer))
    other = lax.ppermute(mine, "trc", [(i, i ^ 1) for i in range(ntrc)])

    def plane(ref, i):
        return ref[i * XE : (i + 1) * XE]

    def dense(raw):
        return jnp.where(raw < 0.5 * DRY, raw, 0.0)

    def faces(raw, u, v, before):
        wet = jnp.where(raw < 0.5 * DRY, 1.0, 0.0)
        d = dense(raw)
        total = before + d
        p = buoyancy * (total - 0.5 * d)
        result = []
        for axis, a in enumerate((u, v)):
            mask = wet * shift(wet, 1, axis)
            lap = shift(a, 1, 0) + shift(a, -1, 0) + shift(a, 1, 1) + shift(a, -1, 1) - 4.0 * a
            push = viscosity * lap - (shift(p, 1, axis) - p)
            result.append((mask * (a + marine_advance * push), mask))
        return total, result

    def unpack(a_ref, b_ref, uv_ref, mask_ref, l_ref, f_ref):
        core = lax.axis_index("trc") % 2
        lane = lax.broadcasted_iota(jnp.int32, (YG, LANES), 1)

        def words(at):
            rows = []
            for g in range(NP):
                a, b = a_ref[g, at : at + Y], b_ref[g, at : at + Y]
                rows += [jnp.where(core == 0, a, b), jnp.where(core == 0, b, a)]
            return jnp.concatenate(rows, axis=0)

        def high(w):
            return lax.shift_right_arithmetic(w, 16)

        def low(w):
            return lax.shift_right_arithmetic(lax.shift_left(w, 16), 16)

        bits = high(words(UV_ROWS)) & 1
        numbers = jnp.sum(jnp.where(lane < 16, lax.shift_left(bits, lane % 16), 0), axis=1, keepdims=True)
        units = []
        for i in range(3):
            number = lax.shift_right_logical(numbers, 5 * i) & 31
            unit = jnp.full((YG, 1), tops[i] / codes[i], F32)
            for b in range(5):
                unit = jnp.where(lax.shift_right_logical(number, b) & 1 > 0, unit * 2.0 ** -(2**b), unit)
            units.append(unit)

        def put(f, x, a):
            turned = a.T
            for g in range(G):
                f_ref[f, pl.ds(x + g * XL, D, stride=XE), :] = turned[g * D : (g + 1) * D]

        for x in range(XL):
            w = words(x * Y)
            put(1, x, high(w).astype(F32) * units[1])
            put(2, x, low(w).astype(F32) * units[2])
            if x < XL // 2:
                w = words(UV_ROWS + x * Y)
                for xx, code in ((x, high(w)), (x + XL // 2, low(w))):
                    code = lax.shift_right_arithmetic(code, 1)
                    put(0, xx, jnp.where(code == DRY_CODE, DRY, code.astype(F32) * units[0]))

        def field(f, k):
            return f_ref[f, pl.ds(pl.multiple_of(k * XE, 8), XE)]

        def one(k, carry):
            total, sums = carry
            total, new = faces(field(0, k), field(1, k), field(2, k), total)
            for i, (speed, mask) in enumerate(new):
                uv_ref[i, k] = speed
                mask_ref[i, k] = mask
            parts = (new[0][0], new[1][0], new[0][1], new[1][1])
            return total, tuple(a + b for a, b in zip(sums, parts))

        zero = jnp.zeros((XE, YG), F32)
        total, sums = lax.fori_loop(0, D, one, (zero, (zero,) * 4), unroll=16)
        for i, a in enumerate((total,) + sums):
            l_ref[i * XE : (i + 1) * XE] = a
        first = jnp.where(lax.axis_index("lev") == 0, D - 2, 0)
        for f in range(3):
            for k in range(2):
                at = (5 + 2 * f + k) * XE
                l_ref[at : at + XE] = field(f, first + k)

    near_uv, masks, own_levels = call(
        unpack,
        (f32(2, D, XE, YG), f32(2, D, XE, YG), f32(11 * XE, YG)),
        (mine, other),
        scratch=(pltpu.VMEM((3, W, YG), F32),),
        name="unpack_ocean",
    )
    far_levels = exchange_levels(own_levels)

    def speeds(n_ref, m_ref, o_ref, r_ref, uv_ref, fv_ref):
        lev = lax.axis_index("lev")
        above = jnp.where(lev > 0, plane(r_ref, 0), 0.0)
        sum_here = plane(o_ref, 0)

        def pushes(a):
            return [-marine_advance * buoyancy * (shift(a, 1, i) - a) for i in range(2)]

        def spread_out(u, v):
            return u - shift(u, -1, 0) + v - shift(v, -1, 1)

        def far(e, total):
            k = e % 2 if e < 2 else e - D - 2
            total, new = faces(plane(r_ref, 5 + k), plane(r_ref, 7 + k), plane(r_ref, 9 + k), total)
            for i in range(2):
                uv_ref[i, e] = new[i][0]
            return total

        total = above - dense(plane(r_ref, 5)) - dense(plane(r_ref, 6))
        for e in (0, 1):
            total = far(e, total)
        total = above + sum_here
        for e in (D + 2, D + 3):
            total = far(e, total)

        push = pushes(sum_here)
        lower = [plane(r_ref, 1 + i) + plane(r_ref, 3 + i) * push[i] for i in range(2)]
        below = jnp.where(lev < nlev - 1, spread_out(*lower), 0.0)

        def divergence(e):
            return spread_out(uv_ref[0, e], uv_ref[1, e])

        fv_ref[D + 2] = below
        fv_ref[D + 3] = below - divergence(D + 2)
        fv_ref[D + 4] = below - divergence(D + 2) - divergence(D + 3)
        push = pushes(above)

        def climb(j, total):
            k = D - 1 - j
            new = [n_ref[i, k] + m_ref[i, k] * push[i] for i in range(2)]
            for i in range(2):
                uv_ref[i, k + 2] = new[i]
            total = total + spread_out(*new)
            fv_ref[k + 2] = total
            return total

        total = lax.fori_loop(0, D, climb, below, unroll=16)
        fv_ref[2] = jnp.where(lev == 0, 0.0, total)
        for e in (1, 0):
            total = total + divergence(e)
            fv_ref[e] = total

    uv, fv = call(
        speeds,
        (f32(2, D + 4, XE, YG), f32(D + 5, XE, YG)),
        (near_uv, masks, own_levels, far_levels),
        name="face_speeds",
    )

    def advect(c_ref, h_ref, uv_ref, fv_ref, adv_ref, msg_ref, pad, mid_pad, sem):
        lev = lax.axis_index("lev")
        copy = pltpu.make_async_copy(c_ref, pad.at[:, pl.ds(4 * XE, W)], sem)
        copy.start()
        for t in range(T):
            outer = h_ref[t * 4 * XE : (t + 1) * 4 * XE]
            pad[t, 0 : 4 * XE] = jnp.where(lev > 0, outer, 0.0)
            pad[t, (D + 4) * XE :] = jnp.where(lev < nlev - 1, outer, 0.0)
        copy.wait()

        def step(src, dst, first, count):
            def cells(e):
                return src[:, pl.ds(pl.multiple_of((e + 2) * XE, 8), XE)]

            def half_slope(lo, mid, hi):
                return minmod(0.5 * (mid - lo), 0.5 * (hi - mid))

            def down(e, up_cell, lo, mid, hi):
                half = half_slope(lo, mid, hi)
                w = level_step * fv_ref[e]
                return w * jnp.where(w > 0.0, up_cell, mid - half), mid + half

            c0, c1, c2, c3 = (cells(first + k) for k in range(-2, 2))
            up_cell = c1 + half_slope(c0, c1, c2)
            flux, up_cell = down(first, up_cell, c1, c2, c3)

            def one(i, carry):
                e = first + i
                mid, hi, flux, up_cell = carry
                nxt = cells(e + 2)
                flux_next, up_next = down(e + 1, up_cell, mid, hi, nxt)
                u, v = tracer_step * uv_ref[0, e], tracer_step * uv_ref[1, e]
                new = mid - (sideways(mid, u[None], 1) + sideways(mid, v[None], 2) + (flux_next - flux))
                dst[:, pl.ds(pl.multiple_of((e + 2) * XE, 8), XE)] = new
                return hi, nxt, flux_next, up_next

            lax.fori_loop(0, count, one, (c2, c3, flux, up_cell), unroll=count // 4)

        step(pad, mid_pad, 0, D + 4)
        step(mid_pad, pad, 2, D)
        for w in range(DX // LANES):
            turned = []
            for t in range(T):
                rows = []
                for x in range(w * G, (w + 1) * G):
                    rows.append(pad[t, pl.ds(4 * XE + H + x, D, stride=XE), :])
                rows = jnp.concatenate(rows, axis=0)
                adv_ref[t, w * LANES : (w + 1) * LANES] = rows
                turned.append(rows.T)
            for d in range(ntrc):
                rows = [turned[t][d * Y : (d + 1) * Y] for t in range(T)]
                msg_ref[d, :, w * LANES : (w + 1) * LANES] = jnp.concatenate(rows, axis=0).astype(
                    jnp.bfloat16
                )

    vmem = pl.BlockSpec(memory_space=pltpu.VMEM)
    advected, message = call(
        advect,
        (f32(T, DX, YG), jax.ShapeDtypeStruct((ntrc, T * Y, DX), jnp.bfloat16)),
        (species, far_outer, uv, fv),
        specs=[pl.BlockSpec(memory_space=pl.ANY)] + [vmem] * 3,
        scratch=(pltpu.VMEM((T, (D + 8) * XE, YG), F32),) * 2 + (pltpu.SemaphoreType.DMA(()),),
        name="advect_tracers",
    )
    message, lo, hi = lax.optimization_barrier((message, lo, hi))
    gathered = lax.all_to_all(message, "trc", split_axis=0, concat_axis=0, tiled=True)
    ring = [(i, (i + 1) % ntrc) for i in range(ntrc)]
    south = lax.ppermute(hi, "trc", ring)
    north = lax.ppermute(lo, "trc", [(b, a) for a, b in ring])
    gathered, south, north = lax.optimization_barrier((gathered, south, north))

    def ocean(
        t_ref, s_ref, uv_ref, fv_ref, l_ref, so_ref, no_ref, sa_ref, wa_ref, ua_ref, va_ref, turn
    ):
        me, lev = lax.axis_index("trc"), lax.axis_index("lev")
        for x in range(XE):
            def level_rows(ref, first):
                return ref[pl.ds(first * XE + x, D, stride=XE), :]

            turn[0, x] = level_rows(uv_ref.at[0], 2).T
            turn[1, x] = level_rows(uv_ref.at[1], 2).T
            turn[2, x] = level_rows(fv_ref, 2).T
            turn[3, x] = level_rows(fv_ref, 3).T
        here = pl.ds(pl.multiple_of(me * Y, 8), Y)
        past = pl.ds(pl.multiple_of(lax.rem(me + ntrc - 1, ntrc) * Y, 8), Y)
        u, v, w, w_next = (turn[i, :, here] for i in range(4))
        v_south = turn[1, :, past][:, Y - 1 : Y]
        level = lax.broadcasted_iota(jnp.int32, (XE, Y, D), 2)
        row = lax.broadcasted_iota(jnp.int32, (XE, Y, D), 1)

        def east(a):
            return jnp.concatenate([a[1:], a[:1]], axis=0)

        def west(a):
            return jnp.concatenate([a[-1:], a[:-1]], axis=0)

        def donor(speed, near, far):
            return jnp.maximum(speed, 0.0) * near + jnp.minimum(speed, 0.0) * far

        def advance(c, i):
            so = jnp.stack([so_ref[i * XE + x : i * XE + x + 1] for x in range(XE)])
            no = jnp.stack([no_ref[i * XE + x : i * XE + x + 1] for x in range(XE)])
            tile = l_ref[4 * T * XE + i * Y : 4 * T * XE + (i + 1) * Y]
            edge = jnp.stack([tile[:, x : x + 1] for x in range(XE)])
            wide = jnp.concatenate([c, jnp.zeros((XE, Y, LANES - D), F32)], axis=2) if D < LANES else c
            upper = shift(wide, -1, 2)[:, :, :D]
            upper = jnp.where(level == 0, jnp.where(lev > 0, edge, 0.0), upper)
            lower = shift(wide, 1, 2)[:, :, :D]
            lower = jnp.where(level == D - 1, jnp.where(lev < nlev - 1, edge, 0.0), lower)
            fe = donor(u, c, east(c))
            fn = donor(v, c, jnp.where(row == Y - 1, no, shift(c, 1, 1)))
            fn_south = jnp.where(row == 0, donor(v_south, so, c[:, 0:1]), shift(fn, -1, 1))
            fall = donor(w_next, c, lower) - donor(w, upper, c)
            return c - marine_advance * ((fe - west(fe)) + (fn - fn_south) + fall)

        sa_ref[...] = advance(s_ref[...], 1)[H : H + X]
        wa_ref[...] = advance(t_ref[...], 0)[H : H + X]
        ua_ref[...] = u[H : H + X]
        va_ref[...] = v[H : H + X]

    saltiness_final, warmth_moved, zonal_speed_final, meridional_speed_final = call(
        ocean,
        (f32(X, Y, D),) * 4,
        (
            warmth,
            salt,
            uv.reshape(2, (D + 4) * XE, YG),
            fv.reshape((D + 5) * XE, YG),
            far_outer,
            south,
            north,
        ),
        scratch=(pltpu.VMEM((4, XE, YG, D), F32),),
        name="own_ocean",
    )

    speed_most = speed_bound + marine_advance * (
        2 * buoyancy * hydro_bound * D * nlev + viscosity * 8 * speed_bound
    )
    growth = 1 + 4 * tracer_step * speed_most + 2 * level_step * (4 * speed_most * D * nlev)
    react_most = NT * coupling_bound * species_bound * growth**2
    unit = 2.0 ** max(0, math.ceil(math.log2(react_most / 65504.0)))

    def spread_columns(c_ref, o_ref):
        n = NT * Y

        def pick(shape, along):
            wide, narrow = (lax.broadcasted_iota(jnp.int32, shape, d) for d in (along, 1 - along))
            return jnp.where(wide // Y == narrow, 1.0, 0.0).astype(jnp.bfloat16)

        tall = jnp.dot(pick((n, NT), 0), c_ref[...], preferred_element_type=F32)
        full = jnp.dot(
            tall.astype(jnp.bfloat16), pick((NT, n), 1), preferred_element_type=F32
        )
        row, lane = (lax.broadcasted_iota(jnp.int32, (n, n), d) for d in (0, 1))
        o_ref[...] = jnp.where(row % Y == lane % Y, full, 0.0).astype(jnp.bfloat16)

    spread = call(
        spread_columns,
        jax.ShapeDtypeStruct((NT * Y, NT * Y), jnp.bfloat16),
        (coupling_matrix,),
        name="spread_coupling",
    )
    flat_tracers = gathered.reshape(NT * Y, DX)
    reaction = jnp.dot(spread, flat_tracers, preferred_element_type=F32)
    reaction = (reaction * (1.0 / unit)).astype(jnp.float16).reshape(ntrc, T * Y, DX)
    returned = lax.all_to_all(reaction, "trc", split_axis=0, concat_axis=0, tiled=True)

    def shade(x_ref, g_ref, k_ref, att_ref, cum_ref):
        att = jnp.zeros((Y, DX), F32)
        for d in range(ntrc):
            rows = x_ref[d].astype(F32)
            for t in range(T):
                att = att + k_ref[g_ref[d * T + t]] * rows[t * Y : (t + 1) * Y]
        att_ref[...] = att
        lane = lax.broadcasted_iota(jnp.int32, (Y, DX), 1)
        total = att
        width = 1
        while width < D:
            total = total + jnp.where(lane % D < width, 0.0, shift(total, -width, 1))
            width *= 2
        cum_ref[...] = total

    smem = pl.BlockSpec(memory_space=pltpu.SMEM)
    attenuation, shaded = call(
        shade,
        (f32(Y, DX), f32(Y, DX)),
        (gathered, species_guild_number, guild_extinction_coefficient),
        specs=[vmem, smem, smem],
        name="shade",
    )
    far_shade = exchange_levels(shaded)

    def heat(att_ref, cum_ref, r_ref, w_ref, m_ref, o_ref):
        att = att_ref[...]
        path = cum_ref[...] - att
        caught = 1.0 - jnp.exp(-att)
        lev = lax.axis_index("lev")
        for x in range(X):
            at = slice(x * D, (x + 1) * D)
            above = jnp.where(lev > 0, r_ref[:, (x + 1) * D - 1 : (x + 1) * D], 0.0)
            absorbed = jnp.exp(-(above + path[:, at])) * caught[:, at]
            o_ref[x] = w_ref[x] + warming_amount * (m_ref[x].astype(F32) * absorbed)

    warmth_final = call(
        heat,
        f32(X, Y, D),
        (attenuation, shaded, far_shade, warmth_moved, jnp.transpose(marine_indicator, (1, 2, 0))),
        name="heat",
    )

    def finish(r_ref, a_ref, o_ref):
        for t in range(T):
            for w in range(DX // LANES):
                rows = [
                    r_ref[d, t * Y : (t + 1) * Y, w * LANES : (w + 1) * LANES] for d in range(ntrc)
                ]
                turned = (react_step * unit) * jnp.concatenate(rows, axis=0).T
                for g in range(G):
                    at = pl.ds(w * G + g, D, stride=X)
                    rows = slice(g * D, (g + 1) * D)
                    o_ref[t, at, :] = a_ref[t, w * LANES + g * D : w * LANES + (g + 1) * D] + turned[rows]

    species_final = call(
        finish, f32(T, DX, YG), (returned.astype(F32), advected), name="finish_tracers"
    )
    ocean_outputs = (warmth_final, saltiness_final, zonal_speed_final, meridional_speed_final)
    ocean_outputs = tuple(jnp.transpose(a, (2, 0, 1)) for a in ocean_outputs)
    return ocean_outputs + (species_final.reshape(T, D, X, YG),)


def solution(mesh):
    ocean = P("lev", "cols", "trc")
    in_specs = (ocean,) * 5 + (P("trc", "lev", "cols", None), P(), P(), P())
    out_specs = (ocean,) * 4 + (P("trc", "lev", "cols", None),)
    return jax.shard_map(shards, mesh=mesh, in_specs=in_specs, out_specs=out_specs, check_vma=False)
```

time: 86.5 us -> 71.5 us (0.83)
  waiting for transfers between devices: 36.5 us -> 29.6 us
  local copies, waits for them, and re-layouts: 4.76 us -> 0.05 us
  Pallas kernels: 16.5 us -> 14.8 us
  starting transfers between devices: 25.9 us -> 24.4 us
    all_to_all x1, waiting for transfers between devices: 14.1 us -> 0.48 us  [shards(): lax.all_to_all(message, 'trc', split_axis=0, concat_axis=0, tiled=True)]
    all_to_all x1, waiting for transfers between devices: 0.01 us -> 8.77 us  [shards(): lax.all_to_all(reaction, 'trc', split_axis=0, concat_axis=0, tiled=True)]
    unnamed x24 -> x18, local copies, waits for them, and re-layouts: 3.82 us -> 0.05 us
    all_to_all x1, waiting for transfers between devices: 6.48 us -> 3.39 us  [shards(): lax.all_to_all(payload, 'trc', split_axis=0, concat_axis=0, tiled=True, a...]
    ppermute x1, waiting for transfers between devices: 6.94 us -> 9.11 us  [shards(): south = lax.ppermute(hi, 'trc', ring)]
    pallas_call x9, Pallas kernels: 16.5 us -> 14.8 us  [call(): pl.pallas_call(kernel, out_shape=out_shape, in_specs=[vmem] * len(args) i...]
    ppermute x4 -> x3, starting transfers between devices: 6.21 us -> 4.67 us  [exchange_levels(): return lax.ppermute(part, 'lev', [(0, 1), (1, 0)])]
    dynamic_slice x1 -> x0, local copies, waits for them, and re-layouts: 0.94 us -> none  [shards(): lax.dynamic_slice_in_dim(species, start, 4, 1)]
  transfers between devices with their start and end apart: 10 -> 9, of which waited for: 7 -> 8; matrix products, arithmetic and copies ran while one was open for 1% -> 0% of each run, Pallas kernels for 4% -> 5%
where the time goes in v2:
time: 71.5 us; the launch traced here: 71 us
  waiting for transfers between devices  29.6 us (41%)
  starting transfers between devices  24.4 us (34%)
  Pallas kernels  14.8 us (21%)
  matrix products  1.23 us (2%)
  between operations  0.77 us (1%)
    pallas_call x9, Pallas kernels, call(): pl.pallas_call(kernel, out_shape=out_shape, in_specs=[vmem] * len(args) i...  14.8 us
    ppermute x1, waiting for transfers between devices, shards(): south = lax.ppermute(hi, 'trc', ring)  9.11 us
    all_to_all x1, waiting for transfers between devices, shards(): lax.all_to_all(reaction, 'trc', split_axis=0, concat_axis=0, tiled=True)  8.77 us
    all_to_all x1, starting transfers between devices, shards(): lax.all_to_all(payload, 'trc', split_axis=0, concat_axis=0, tiled=True, a...  7.4 us
    ppermute x3, waiting for transfers between devices, exchange_levels(): return lax.ppermute(part, 'lev', [(0, 1), (1, 0)])  6.4 us
    ppermute x3, starting transfers between devices, exchange_levels(): return lax.ppermute(part, 'lev', [(0, 1), (1, 0)])  4.67 us
    ppermute x1, starting transfers between devices, shards(): north = lax.ppermute(lo, 'trc', [(b, a) for a, b in ring])  4.16 us
    all_to_all x1, starting transfers between devices, shards(): lax.all_to_all(reaction, 'trc', split_axis=0, concat_axis=0, tiled=True)  4.15 us
  transfers between devices with their start and end apart: 9, of which 8 were waited for; matrix products, arithmetic and copies ran while one was open for 0% of the time, Pallas kernels for 5%

profile of v2, /device:TPU:0, one launch (start us, length us, event | category | flops | bytes accessed | tf_op | source)
XLA Modules:
  0.0 71.0 jit_solution(4090217430045824318)
XLA Ops:
  0.6 2.1 %pack_ocean.1 = (s32[8,48,128]{2,1,0:T(8,128)}, f32[16,64]{1,0:T(8,128)}, f32[16,64]{1,0:T(8,128)}, f32[144,128]{1,0:T(8,128)}) custom-call(f32[8,8,64]{2,1,0:T(8,128)} %bitcast.24, f32[8,8,64]{2,1,0:T(8,128)} %bitcast.26, f32[8,8,64]{2,1,0:T(8,128)} %bitcast.32, f32[8,8,64]{2,1,0:T(8,128)} %bitcast.33, s32[8,8,64]{2,1,0:T(8,128)} %bitcast.28, ...), custom_call_target="tpu_custom_call" | custom-call | tf_op jit(solution)/shard_map/pack_ocean/pallas_call | solution.py:31
  2.7 7.4 %all-to-all-start = ((s32[8,48,128]{2,1,0:T(8,128)}), s32[8,48,128]{2,1,0:T(8,128)S(1)}, u32[]{:S(2)}, u32[]{:S(2)}) async-start(s32[8,48,128]{2,1,0:T(8,128)} %get-tuple-element.30), calls=%async_computation | async-start | bytes 393216 | tf_op jit(solution)/shard_map/all_to_all | solution.py:191
  10.1 1.5 %collective-permute-start = (f32[144,128]{1,0:T(8,128)}, f32[144,128]{1,0:T(8,128)S(1)}, u32[]{:S(2)}, u32[]{:S(2)}) collective-permute-start(f32[144,128]{1,0:T(8,128)} %get-tuple-element.31), channel_id=1, source_target_pairs={{0,1},{1,0},{2,3},{3,2},{4,5},{5,4},{6,7},{7,6},{8,9},{9,8},{10,11... | collective-permute-start | bytes 221192 | tf_op jit(solution)/shard_map/ppermute | solution.py:62
  11.6 3.0 %collective-permute-done.h_ref.l_ref = f32[144,128]{1,0:T(8,128)S(1)} collective-permute-done((f32[144,128]{1,0:T(8,128)}, f32[144,128]{1,0:T(8,128)S(1)}, u32[]{:S(2)}, u32[]{:S(2)}) %collective-permute-start) | collective-permute-done | bytes 73760 | tf_op jit(solution)/shard_map/ppermute | solution.py:62
  14.7 3.4 %all-to-all-done.a_ref = s32[8,48,128]{2,1,0:T(8,128)S(1)} async-done(((s32[8,48,128]{2,1,0:T(8,128)}), s32[8,48,128]{2,1,0:T(8,128)S(1)}, u32[]{:S(2)}, u32[]{:S(2)}) %all-to-all-start) | async-done | bytes 196640 | tf_op jit(solution)/shard_map/all_to_all | solution.py:191
  18.1 1.4 %collective-permute-done.1.b_ref = s32[8,48,128]{2,1,0:T(8,128)S(1)} collective-permute-done((s32[8,48,128]{2,1,0:T(8,128)S(1)}, s32[8,48,128]{2,1,0:T(8,128)S(1)}, u32[]{:S(2)}, u32[]{:S(2)}) %collective-permute-start.1) | collective-permute-done | bytes 196640 | tf_op jit(solution)/shard_map/ppermute | solution.py:196
  19.5 1.2 %unpack_ocean.1 = (f32[2,64,8,128]{3,2,1,0:T(8,128)S(1)}, f32[2,64,8,128]{3,2,1,0:T(8,128)S(1)}, f32[88,128]{1,0:T(8,128)S(1)}) custom-call(s32[8,48,128]{2,1,0:T(8,128)S(1)} %all-to-all-done.a_ref, s32[8,48,128]{2,1,0:T(8,128)S(1)} %collective-permute-done.1.b_ref), custom_call_target="tpu_custom_call" | custom-call | tf_op jit(solution)/shard_map/unpack_ocean/pallas_call | solution.py:31
  20.7 1.6 %collective-permute-start.2 = (f32[88,128]{1,0:T(8,128)S(1)}, f32[88,128]{1,0:T(8,128)S(1)}, u32[]{:S(2)}, u32[]{:S(2)}) collective-permute-start(f32[88,128]{1,0:T(8,128)S(1)} %get-tuple-element.36.o_ref), channel_id=1, source_target_pairs={{0,1},{1,0},{2,3},{3,2},{4,5},{5,4},{6,7},{7,6},{8,9},{9,8},{10,11... | collective-permute-start | bytes 135176 | tf_op jit(solution)/shard_map/ppermute | solution.py:62
  22.3 2.5 %collective-permute-done.2.r_ref = f32[88,128]{1,0:T(8,128)S(1)} collective-permute-done((f32[88,128]{1,0:T(8,128)S(1)}, f32[88,128]{1,0:T(8,128)S(1)}, u32[]{:S(2)}, u32[]{:S(2)}) %collective-permute-start.2) | collective-permute-done | bytes 45088 | tf_op jit(solution)/shard_map/ppermute | solution.py:62
  24.8 0.6 face_speeds.1
  25.5 5.9 %advect_tracers.1 = (f32[4,512,128]{2,1,0:T(8,128)S(1)}, bf16[16,32,512]{2,1,0:T(8,128)(2,1)}) custom-call(f32[4,512,128]{2,1,0:T(8,128)S(1)} %bitcast.20, f32[144,128]{1,0:T(8,128)S(1)} %collective-permute-done.h_ref.l_ref, f32[2,68,8,128]{3,2,1,0:T(8,128)S(1)} %get-tuple-element.37.uv_ref, f32[69,8,128]{2,1,0:T(8,128)S(1)} %get-tuple-element.38.fv_ref), custom_call_target="tpu_custom_call" | custom-call | tf_op jit(solution)/shard_map/advect_tracers/pallas_call | solution.py:31
  31.4 3.7 %all-to-all-start.1 = ((bf16[16,32,512]{2,1,0:T(8,128)(2,1)}), bf16[16,32,512]{2,1,0:T(8,128)(2,1)S(1)}, u32[]{:S(2)}, u32[]{:S(2)}) async-start(bf16[16,32,512]{2,1,0:T(8,128)(2,1)} %get-tuple-element.42), calls=%async_computation.1 | async-start | bytes 1048576 | tf_op jit(solution)/shard_map/all_to_all | solution.py:414
  35.5 4.2 %collective-permute-start.4 = (f32[16,64]{1,0:T(8,128)S(1)}, f32[16,64]{1,0:T(8,128)S(1)}, u32[]{:S(2)}, u32[]{:S(2)}) collective-permute-start(f32[16,64]{1,0:T(8,128)S(1)} %copy-done.7), channel_id=1, source_target_pairs={{2,0},{4,2},{6,4},{8,6},{10,8},{12,10},{14,12},{16,14},{18,16},{20... | collective-permute-start | bytes 12296 | tf_op jit(solution)/shard_map/ppermute | solution.py:417
  40.1 9.1 %collective-permute-done.3.so_ref = f32[16,64]{1,0:T(8,128)S(1)} collective-permute-done((f32[16,64]{1,0:T(8,128)S(1)}, f32[16,64]{1,0:T(8,128)S(1)}, u32[]{:S(2)}, u32[]{:S(2)}) %collective-permute-start.3) | collective-permute-done | bytes 4128 | tf_op jit(solution)/shard_map/ppermute | solution.py:416
  49.2 0.5 all-to-all-done.1.x_ref
  49.7 1.2 %fusion = f16[512,512]{0,1:T(8,128)(2,1)} fusion(bf16[512,512]{1,0:T(8,128)(2,1)S(1)} %spread_coupling.1, bf16[512,512]{1,0:T(8,128)(2,1)S(1)} %bitcast.22), kind=kOutput, calls=%fused_computation.1 | convolution fusion | flops 268959744 | bytes 1572864 | tf_op jit(solution)/shard_map/dot_general | solution.py:513
  50.9 4.2 %all-to-all-start.2 = ((f16[16,32,512]{2,1,0:T(8,128)(2,1)}), f16[16,32,512]{2,1,0:T(8,128)(2,1)S(1)}, u32[]{:S(2)}, u32[]{:S(2)}) async-start(f16[16,32,512]{2,1,0:T(8,128)(2,1)} %bitcast.31), calls=%async_computation.2 | async-start | bytes 1048576 | tf_op jit(solution)/shard_map/all_to_all | solution.py:515
  55.1 1.1 %shade.1 = (f32[8,512]{1,0:T(8,128)S(1)}, f32[8,512]{1,0:T(8,128)S(1)}) custom-call(bf16[16,32,512]{2,1,0:T(8,128)(2,1)S(1)} %all-to-all-done.1.x_ref, s32[64]{0:T(128)S(1)} %copy-done.5, f32[8]{0:T(128)S(1)} %copy-done.6), custom_call_target="tpu_custom_call" | custom-call | tf_op jit(solution)/shard_map/shade/pallas_call | solution.py:31
  56.2 1.6 %collective-permute-start.5 = (f32[8,512]{1,0:T(8,128)S(1)}, f32[8,512]{1,0:T(8,128)S(1)}, u32[]{:S(2)}, u32[]{:S(2)}) collective-permute-start(f32[8,512]{1,0:T(8,128)S(1)} %get-tuple-element.47.cum_ref), channel_id=1, source_target_pairs={{0,1},{1,0},{2,3},{3,2},{4,5},{5,4},{6,7},{7,6},{8,9},{9,8},{10,11... | collective-permute-start | bytes 49160 | tf_op jit(solution)/shard_map/ppermute | solution.py:62
  57.8 1.4 %own_ocean.1 = (f32[8,8,64]{2,1,0:T(8,128)}, f32[8,8,64]{2,1,0:T(8,128)S(1)}, f32[8,8,64]{2,1,0:T(8,128)}, f32[8,8,64]{2,1,0:T(8,128)}) custom-call(f32[8,8,64]{2,1,0:T(8,128)S(1)} %bitcast.25, f32[8,8,64]{2,1,0:T(8,128)S(1)} %bitcast.27, f32[2,544,128]{2,1,0:T(8,128)S(1)} %bitcast.21, f32[552,128]{1,0:T(8,128)S(1)} %bitcast.23, ...), custom_call_target="tpu_custom_call" | custom-call | tf_op jit(solution)/shard_map/own_ocean/pallas_call | solution.py:31
  59.2 0.8 %collective-permute-done.5.r_ref = f32[8,512]{1,0:T(8,128)S(1)} collective-permute-done((f32[8,512]{1,0:T(8,128)S(1)}, f32[8,512]{1,0:T(8,128)S(1)}, u32[]{:S(2)}, u32[]{:S(2)}) %collective-permute-start.5) | collective-permute-done | bytes 16416 | tf_op jit(solution)/shard_map/ppermute | solution.py:62
  60.0 0.8 %heat.1 = f32[8,8,64]{2,1,0:T(8,128)} custom-call(f32[8,512]{1,0:T(8,128)S(1)} %get-tuple-element.46.att_ref, f32[8,512]{1,0:T(8,128)S(1)} %get-tuple-element.47.cum_ref, f32[8,512]{1,0:T(8,128)S(1)} %collective-permute-done.5.r_ref, f32[8,8,64]{2,1,0:T(8,128)S(1)} %get-tuple-element.50.w_ref, s32[8,8,64]{2,1,0:T(8,128)S(1)} %bitcast.29), custom_call_target="tpu_custom_call" | custom-call | tf_op jit(solution)/shard_map/heat/pallas_call | solution.py:31
  60.8 8.8 %all-to-all-done.2 = f16[16,32,512]{2,1,0:T(8,128)(2,1)S(1)} async-done(((f16[16,32,512]{2,1,0:T(8,128)(2,1)}), f16[16,32,512]{2,1,0:T(8,128)(2,1)S(1)}, u32[]{:S(2)}, u32[]{:S(2)}) %all-to-all-start.2) | async-done | bytes 524320 | tf_op jit(solution)/shard_map/all_to_all | solution.py:515
  69.7 1.3 %finish_tracers.1 = f32[4,512,128]{2,1,0:T(8,128)} custom-call(f32[16,32,512]{2,1,0:T(8,128)S(1)} %convert_element_type.11.r_ref, f32[4,512,128]{2,1,0:T(8,128)S(1)} %get-tuple-element.54.a_ref), custom_call_target="tpu_custom_call" | custom-call | tf_op jit(solution)/shard_map/finish_tracers/pallas_call | solution.py:31
  (23 shorter events, 0.9 us)
Async XLA Ops:
  2.7 22.8 %copy-start = (f32[4,64,8,128]{3,2,1,0:T(8,128)S(1)}, f32[4,64,8,128]{3,2,1,0:T(8,128)}, u32[]{:S(2)}) copy-start(f32[4,64,8,128]{3,2,1,0:T(8,128)} %param.14) | copy-start | bytes 3145732
  2.7 15.3 %all-to-all-start = ((s32[8,48,128]{2,1,0:T(8,128)}), s32[8,48,128]{2,1,0:T(8,128)S(1)}, u32[]{:S(2)}, u32[]{:S(2)}) async-start(s32[8,48,128]{2,1,0:T(8,128)} %get-tuple-element.30), calls=%async_computation | async-start | bytes 393216 | tf_op jit(solution)/shard_map/all_to_all | solution.py:191
  10.1 4.6 %collective-permute-start = (f32[144,128]{1,0:T(8,128)}, f32[144,128]{1,0:T(8,128)S(1)}, u32[]{:S(2)}, u32[]{:S(2)}) collective-permute-start(f32[144,128]{1,0:T(8,128)} %get-tuple-element.31), channel_id=1, source_target_pairs={{0,1},{1,0},{2,3},{3,2},{4,5},{5,4},{6,7},{7,6},{8,9},{9,8},{10,11... | collective-permute-start | bytes 221192 | tf_op jit(solution)/shard_map/ppermute | solution.py:62
  18.1 1.4 %collective-permute-start.1 = (s32[8,48,128]{2,1,0:T(8,128)S(1)}, s32[8,48,128]{2,1,0:T(8,128)S(1)}, u32[]{:S(2)}, u32[]{:S(2)}) collective-permute-start(s32[8,48,128]{2,1,0:T(8,128)S(1)} %all-to-all-done.a_ref), channel_id=1, source_target_pairs={{0,2},{2,0},{4,6},{6,4},{8,10},{10,8},{12,14},{14,12},{16,18},{18,... | collective-permute-start | bytes 589832 | tf_op jit(solution)/shard_map/ppermute | solution.py:196
  20.7 4.1 %collective-permute-start.2 = (f32[88,128]{1,0:T(8,128)S(1)}, f32[88,128]{1,0:T(8,128)S(1)}, u32[]{:S(2)}, u32[]{:S(2)}) collective-permute-start(f32[88,128]{1,0:T(8,128)S(1)} %get-tuple-element.36.o_ref), channel_id=1, source_target_pairs={{0,1},{1,0},{2,3},{3,2},{4,5},{5,4},{6,7},{7,6},{8,9},{9,8},{10,11... | collective-permute-start | bytes 135176 | tf_op jit(solution)/shard_map/ppermute | solution.py:62
  31.4 3.8 %copy-start.8 = (f32[16,64]{1,0:T(8,128)S(1)}, f32[16,64]{1,0:T(8,128)}, u32[]{:S(2)}) copy-start(f32[16,64]{1,0:T(8,128)} %get-tuple-element.43) | copy-start | bytes 12292
  31.4 4.1 %copy-start.7 = (f32[16,64]{1,0:T(8,128)S(1)}, f32[16,64]{1,0:T(8,128)}, u32[]{:S(2)}) copy-start(f32[16,64]{1,0:T(8,128)} %get-tuple-element.44) | copy-start | bytes 12292
  31.4 8.2 %copy-start.4 = (bf16[64,64]{1,0:T(8,128)(2,1)S(1)}, bf16[64,64]{1,0:T(8,128)(2,1)}, u32[]{:S(2)}) copy-start(bf16[64,64]{1,0:T(8,128)(2,1)} %c_ref.1) | copy-start | bytes 24580
  31.4 18.2 %all-to-all-start.1 = ((bf16[16,32,512]{2,1,0:T(8,128)(2,1)}), bf16[16,32,512]{2,1,0:T(8,128)(2,1)S(1)}, u32[]{:S(2)}, u32[]{:S(2)}) async-start(bf16[16,32,512]{2,1,0:T(8,128)(2,1)} %get-tuple-element.42), calls=%async_computation.1 | async-start | bytes 1048576 | tf_op jit(solution)/shard_map/all_to_all | solution.py:414
  35.2 14.0 %collective-permute-start.3 = (f32[16,64]{1,0:T(8,128)S(1)}, f32[16,64]{1,0:T(8,128)S(1)}, u32[]{:S(2)}, u32[]{:S(2)}) collective-permute-start(f32[16,64]{1,0:T(8,128)S(1)} %copy-done.8), channel_id=1, source_target_pairs={{0,2},{2,4},{4,6},{6,8},{8,10},{10,12},{12,14},{14,16},{16,18},{18... | collective-permute-start | bytes 12296 | tf_op jit(solution)/shard_map/ppermute | solution.py:416
  35.5 13.7 %collective-permute-start.4 = (f32[16,64]{1,0:T(8,128)S(1)}, f32[16,64]{1,0:T(8,128)S(1)}, u32[]{:S(2)}, u32[]{:S(2)}) collective-permute-start(f32[16,64]{1,0:T(8,128)S(1)} %copy-done.7), channel_id=1, source_target_pairs={{2,0},{4,2},{6,4},{8,6},{10,8},{12,10},{14,12},{16,14},{18,16},{20... | collective-permute-start | bytes 12296 | tf_op jit(solution)/shard_map/ppermute | solution.py:417
  50.9 4.2 %copy-start.5 = (s32[64]{0:T(128)S(1)}, s32[64]{0:T(128)}, u32[]{:S(2)}) copy-start(s32[64]{0:T(128)} %g_ref.1) | copy-start | bytes 772
  50.9 4.2 %copy-start.6 = (f32[8]{0:T(128)S(1)}, f32[8]{0:T(128)}, u32[]{:S(2)}) copy-start(f32[8]{0:T(128)} %k_ref.1) | copy-start | bytes 100
  50.9 18.6 %all-to-all-start.2 = ((f16[16,32,512]{2,1,0:T(8,128)(2,1)}), f16[16,32,512]{2,1,0:T(8,128)(2,1)S(1)}, u32[]{:S(2)}, u32[]{:S(2)}) async-start(f16[16,32,512]{2,1,0:T(8,128)(2,1)} %bitcast.31), calls=%async_computation.2 | async-start | bytes 1048576 | tf_op jit(solution)/shard_map/all_to_all | solution.py:515
  55.1 2.7 %copy-start.1 = (f32[64,8,8]{0,2,1:T(8,128)S(1)}, f32[64,8,8]{0,2,1:T(8,128)}, u32[]{:S(2)}) copy-start(f32[64,8,8]{0,2,1:T(8,128)} %param.9) | copy-start | bytes 49156
  55.1 2.7 %copy-start.2 = (f32[64,8,8]{0,2,1:T(8,128)S(1)}, f32[64,8,8]{0,2,1:T(8,128)}, u32[]{:S(2)}) copy-start(f32[64,8,8]{0,2,1:T(8,128)} %param.10) | copy-start | bytes 49156
  56.2 3.8 %collective-permute-start.5 = (f32[8,512]{1,0:T(8,128)S(1)}, f32[8,512]{1,0:T(8,128)S(1)}, u32[]{:S(2)}, u32[]{:S(2)}) collective-permute-start(f32[8,512]{1,0:T(8,128)S(1)} %get-tuple-element.47.cum_ref), channel_id=1, source_target_pairs={{0,1},{1,0},{2,3},{3,2},{4,5},{5,4},{6,7},{7,6},{8,9},{9,8},{10,11... | collective-permute-start | bytes 49160 | tf_op jit(solution)/shard_map/ppermute | solution.py:62
  57.8 2.2 %copy-start.3 = (s32[64,8,8]{0,2,1:T(8,128)S(1)}, s32[64,8,8]{0,2,1:T(8,128)}, u32[]{:S(2)}) copy-start(s32[64,8,8]{0,2,1:T(8,128)} %param.13) | copy-start | bytes 49156

commit v3 on v2

--- a/solution.py
+++ b/solution.py
@@ -25,9 +25,9 @@
 F32 = jnp.float32
 
 
-def call(kernel, out_shape, args, specs=None, scratch=(), name=None, mib=40):
+def call(kernel, out_shape, args, specs=None, scratch=(), name=None, mib=16, outs=None):
     vmem = pl.BlockSpec(memory_space=pltpu.VMEM)
-    outs = jax.tree.map(lambda _: vmem, out_shape)
+    outs = jax.tree.map(lambda _: vmem, out_shape) if outs is None else outs
     return pl.pallas_call(
         kernel,
         out_shape=out_shape,
@@ -85,6 +85,7 @@
     W, DX = D * XE, D * X
     G = LANES // D
     XL = XE // G
+    RL = LANES // X
 
     def widen(block, dim):
         if H == 0:
@@ -192,7 +193,30 @@
         payload, "trc", split_axis=0, concat_axis=0, tiled=True, axis_index_groups=pairs_apart
     )
     far_outer = exchange_levels(outer)
-    mine, far_outer = lax.optimization_barrier((mine, far_outer))
+
+
+    def rows(k, n=XE):
+        return pl.ds(pl.multiple_of(k * XE, 8), n)
+
+    def widen_levels(c_ref, h_ref, pad, sem):
+        lev = lax.axis_index("lev")
+        copy = pltpu.make_async_copy(c_ref, pad.at[:, pl.ds(4 * XE, W)], sem)
+        copy.start()
+        for t in range(T):
+            outer = h_ref[t * 4 * XE : (t + 1) * 4 * XE]
+            pad[t, 0 : 4 * XE] = jnp.where(lev > 0, outer, 0.0)
+            pad[t, (D + 4) * XE :] = jnp.where(lev < nlev - 1, outer, 0.0)
+        copy.wait()
+
+    pad = call(
+        widen_levels,
+        f32(T, (D + 8) * XE, YG),
+        (species, far_outer),
+        specs=[pl.BlockSpec(memory_space=pl.ANY), pl.BlockSpec(memory_space=pltpu.VMEM)],
+        scratch=(pltpu.SemaphoreType.DMA(()),),
+        name="widen_levels",
+    )
+    mine, pad = lax.optimization_barrier((mine, pad))
     other = lax.ppermute(mine, "trc", [(i, i ^ 1) for i in range(ntrc)])
 
     def plane(ref, i):
@@ -285,7 +309,33 @@
         scratch=(pltpu.VMEM((3, W, YG), F32),),
         name="unpack_ocean",
     )
+    own_levels, pad = lax.optimization_barrier((own_levels, pad))
     far_levels = exchange_levels(own_levels)
+
+    def half_slope(lo, mid, hi):
+        return minmod(0.5 * (mid - lo), 0.5 * (hi - mid))
+
+    def edges(c, axis):
+        d = 0.5 * (shift(c, 1, axis) - c)
+        half = minmod(shift(d, -1, axis), d)
+        return c + half, shift(c - half, 1, axis)
+
+    def slopes(pad, side):
+        def one(k, carry):
+            lo, mid = carry
+            hi = pad[:, rows(k + 2)]
+            half = half_slope(lo, mid, hi)
+            values = edges(mid, 1) + edges(mid, 2) + (mid + half, mid - half)
+            for i, a in enumerate(values):
+                side[i, :, rows(k)] = a
+            return mid, hi
+
+        count = D + 6
+        first = (pad[:, 0:XE], pad[:, XE : 2 * XE])
+        lax.fori_loop(0, count, one, first, unroll=count // 5)
+
+    side = call(slopes, f32(6, T, (D + 6) * XE, YG), (pad,), name="first_slopes")
+    far_levels, side = lax.optimization_barrier((far_levels, side))
 
     def speeds(n_ref, m_ref, o_ref, r_ref, uv_ref, fv_ref):
         lev = lax.axis_index("lev")
@@ -346,68 +396,75 @@
         name="face_speeds",
     )
 
-    def advect(c_ref, h_ref, uv_ref, fv_ref, adv_ref, msg_ref, pad, mid_pad, sem):
-        lev = lax.axis_index("lev")
-        copy = pltpu.make_async_copy(c_ref, pad.at[:, pl.ds(4 * XE, W)], sem)
-        copy.start()
-        for t in range(T):
-            outer = h_ref[t * 4 * XE : (t + 1) * 4 * XE]
-            pad[t, 0 : 4 * XE] = jnp.where(lev > 0, outer, 0.0)
-            pad[t, (D + 4) * XE :] = jnp.where(lev < nlev - 1, outer, 0.0)
-        copy.wait()
-
-        def step(src, dst, first, count):
-            def cells(e):
-                return src[:, pl.ds(pl.multiple_of((e + 2) * XE, 8), XE)]
-
-            def half_slope(lo, mid, hi):
-                return minmod(0.5 * (mid - lo), 0.5 * (hi - mid))
-
-            def down(e, up_cell, lo, mid, hi):
-                half = half_slope(lo, mid, hi)
-                w = level_step * fv_ref[e]
-                return w * jnp.where(w > 0.0, up_cell, mid - half), mid + half
-
-            c0, c1, c2, c3 = (cells(first + k) for k in range(-2, 2))
-            up_cell = c1 + half_slope(c0, c1, c2)
-            flux, up_cell = down(first, up_cell, c1, c2, c3)
-
-            def one(i, carry):
-                e = first + i
-                mid, hi, flux, up_cell = carry
-                nxt = cells(e + 2)
-                flux_next, up_next = down(e + 1, up_cell, mid, hi, nxt)
-                u, v = tracer_step * uv_ref[0, e], tracer_step * uv_ref[1, e]
-                new = mid - (sideways(mid, u[None], 1) + sideways(mid, v[None], 2) + (flux_next - flux))
-                dst[:, pl.ds(pl.multiple_of((e + 2) * XE, 8), XE)] = new
-                return hi, nxt, flux_next, up_next
-
-            lax.fori_loop(0, count, one, (c2, c3, flux, up_cell), unroll=count // 4)
-
-        step(pad, mid_pad, 0, D + 4)
-        step(mid_pad, pad, 2, D)
-        for w in range(DX // LANES):
-            turned = []
-            for t in range(T):
-                rows = []
-                for x in range(w * G, (w + 1) * G):
-                    rows.append(pad[t, pl.ds(4 * XE + H + x, D, stride=XE), :])
-                rows = jnp.concatenate(rows, axis=0)
-                adv_ref[t, w * LANES : (w + 1) * LANES] = rows
-                turned.append(rows.T)
+    def advect(pad, side, uv_ref, fv_ref, adv_ref, msg_any, mid_pad, held, sems):
+        def speeds_at(e):
+            return tracer_step * uv_ref[0, e][None], tracer_step * uv_ref[1, e][None]
+
+        def fall(e, up, low):
+            w = level_step * fv_ref[e]
+            return w * jnp.where(w > 0.0, up, low)
+
+        def first_step(e, flux):
+            k = rows(e + 1)
+            flux_next = fall(e + 1, side[4, :, k], side[5, :, rows(e + 2)])
+            change = flux_next - flux
+            for i, speed in enumerate(speeds_at(e)):
+                f = speed * jnp.where(speed > 0.0, side[2 * i, :, k], side[2 * i + 1, :, k])
+                change = change + (f - shift(f, -1, i + 1))
+            mid_pad[:, rows(e)] = pad[:, rows(e + 2)] - change
+            return flux_next
+
+        flux = fall(0, side[4, :, rows(0)], side[5, :, rows(1)])
+        lax.fori_loop(0, D + 4, first_step, flux, unroll=(D + 4) // 4)
+
+        def second_step(k, carry):
+            mid, hi, up, flux = carry
+            nxt = mid_pad[:, rows(k + 4)]
+            half = half_slope(mid, hi, nxt)
+            flux_next = fall(k + 3, up, hi - half)
+            u, v = speeds_at(k + 2)
+            change = sideways(mid, u, 1) + sideways(mid, v, 2) + (flux_next - flux)
+            adv_ref[:, pl.ds(pl.multiple_of(k * X, 8), X)] = (mid - change)[:, H : H + X]
+            return hi, nxt, hi + half, flux_next
+
+        c = [mid_pad[:, rows(k)] for k in range(4)]
+        half = half_slope(c[1], c[2], c[3])
+        flux = fall(2, c[1] + half_slope(c[0], c[1], c[2]), c[2] - half)
+        def sending(w):
+            here = pl.ds(pl.multiple_of(w * LANES, LANES), LANES)
+            return pltpu.make_async_copy(held.at[w], msg_any.at[:, :, here], sems.at[w])
+
+        def turn(w):
+            here = pl.ds(pl.multiple_of(w * LANES, LANES), LANES)
+            turned = [adv_ref[t, here].T for t in range(T)]
             for d in range(ntrc):
-                rows = [turned[t][d * Y : (d + 1) * Y] for t in range(T)]
-                msg_ref[d, :, w * LANES : (w + 1) * LANES] = jnp.concatenate(rows, axis=0).astype(
-                    jnp.bfloat16
-                )
+                there = [turned[t][d * Y : (d + 1) * Y] for t in range(T)]
+                held[w, d] = jnp.concatenate(there, axis=0).astype(jnp.bfloat16)
+            sending(w).start()
+
+        def block(w, carry):
+            for k in range(RL):
+                carry = second_step(w * RL + k, carry)
+            return carry
+
+        count = DX // LANES
+        lax.fori_loop(0, count, block, (c[2], c[3], c[2] + half, flux))
+        for w in range(count):
+            turn(w)
+        for w in range(count):
+            sending(w).wait()
 
     vmem = pl.BlockSpec(memory_space=pltpu.VMEM)
     advected, message = call(
         advect,
-        (f32(T, DX, YG), jax.ShapeDtypeStruct((ntrc, T * Y, DX), jnp.bfloat16)),
-        (species, far_outer, uv, fv),
-        specs=[pl.BlockSpec(memory_space=pl.ANY)] + [vmem] * 3,
-        scratch=(pltpu.VMEM((T, (D + 8) * XE, YG), F32),) * 2 + (pltpu.SemaphoreType.DMA(()),),
+        (f32(T, DX, YG), pltpu.HBM((ntrc, T * Y, DX), jnp.bfloat16)),
+        (pad, side, uv, fv),
+        scratch=(
+            pltpu.VMEM((T, (D + 4) * XE, YG), F32),
+            pltpu.VMEM((DX // LANES, ntrc, T * Y, LANES), jnp.bfloat16),
+            pltpu.SemaphoreType.DMA((DX // LANES,)),
+        ),
+        outs=(vmem, pl.BlockSpec(memory_space=pltpu.HBM)),
         name="advect_tracers",
     )
     message, lo, hi = lax.optimization_barrier((message, lo, hi))
@@ -523,9 +580,9 @@
         att_ref[...] = att
         lane = lax.broadcasted_iota(jnp.int32, (Y, DX), 1)
         total = att
-        width = 1
-        while width < D:
-            total = total + jnp.where(lane % D < width, 0.0, shift(total, -width, 1))
+        width = X
+        while width < DX:
+            total = total + jnp.where(lane < width, 0.0, shift(total, -width, 1))
             width *= 2
         cum_ref[...] = total
 
@@ -539,38 +596,49 @@
     )
     far_shade = exchange_levels(shaded)
 
-    def heat(att_ref, cum_ref, r_ref, w_ref, m_ref, o_ref):
+    def heat(att_ref, cum_ref, r_ref, w_ref, m_ref, o_ref, turn):
+        lane = lax.broadcasted_iota(jnp.int32, (Y, LANES), 1)
+        keep = (lax.axis_index("lev") > 0) & (lane >= LANES - X)
+        above = jnp.where(keep, r_ref[:, DX - LANES :], 0.0)
+        width = X
+        while width < LANES:
+            above = above + shift(above, width, 1)
+            width *= 2
         att = att_ref[...]
-        path = cum_ref[...] - att
-        caught = 1.0 - jnp.exp(-att)
-        lev = lax.axis_index("lev")
+        path = jnp.concatenate([above] * (DX // LANES), axis=1) + cum_ref[...] - att
+        turn[...] = (jnp.exp(-path) * (1.0 - jnp.exp(-att))).T
         for x in range(X):
-            at = slice(x * D, (x + 1) * D)
-            above = jnp.where(lev > 0, r_ref[:, (x + 1) * D - 1 : (x + 1) * D], 0.0)
-            absorbed = jnp.exp(-(above + path[:, at])) * caught[:, at]
+            absorbed = turn[pl.ds(x, D, stride=X), :].T
             o_ref[x] = w_ref[x] + warming_amount * (m_ref[x].astype(F32) * absorbed)
 
     warmth_final = call(
         heat,
         f32(X, Y, D),
         (attenuation, shaded, far_shade, warmth_moved, jnp.transpose(marine_indicator, (1, 2, 0))),
+        scratch=(pltpu.VMEM((DX, Y), F32),),
         name="heat",
     )
 
-    def finish(r_ref, a_ref, o_ref):
+    def finish(r_ref, a_ref, o_any, o_ref, sems):
+        copies = [pltpu.make_async_copy(o_ref.at[t], o_any.at[t], sems.at[t]) for t in range(T)]
         for t in range(T):
             for w in range(DX // LANES):
                 rows = [
                     r_ref[d, t * Y : (t + 1) * Y, w * LANES : (w + 1) * LANES] for d in range(ntrc)
                 ]
-                turned = (react_step * unit) * jnp.concatenate(rows, axis=0).T
-                for g in range(G):
-                    at = pl.ds(w * G + g, D, stride=X)
-                    rows = slice(g * D, (g + 1) * D)
-                    o_ref[t, at, :] = a_ref[t, w * LANES + g * D : w * LANES + (g + 1) * D] + turned[rows]
+                here = slice(w * LANES, (w + 1) * LANES)
+                o_ref[t, here] = a_ref[t, here] + (react_step * unit) * jnp.concatenate(rows, axis=0).T
+            copies[t].start()
+        for copy in copies:
+            copy.wait()
 
     species_final = call(
-        finish, f32(T, DX, YG), (returned.astype(F32), advected), name="finish_tracers"
+        finish,
+        f32(T, DX, YG),
+        (returned.astype(F32), advected),
+        scratch=(pltpu.VMEM((T, DX, YG), F32), pltpu.SemaphoreType.DMA((T,))),
+        name="finish_tracers",
+        outs=pl.BlockSpec(memory_space=pl.ANY),
     )
     ocean_outputs = (warmth_final, saltiness_final, zonal_speed_final, meridional_speed_final)
     ocean_outputs = tuple(jnp.transpose(a, (2, 0, 1)) for a in ocean_outputs)

time: 71.5 us -> 69.7 us (0.975)
  waiting for transfers between devices: 29.6 us -> 26.3 us
  local copies, waits for them, and re-layouts: 0.05 us -> 1.26 us
    ppermute x3, waiting for transfers between devices: 6.4 us -> 4.59 us  [exchange_levels(): return lax.ppermute(part, 'lev', [(0, 1), (1, 0)])]
    all_to_all x1, waiting for transfers between devices: 3.39 us -> 2.06 us  [shards(): lax.all_to_all(payload, 'trc', split_axis=0, concat_axis=0, tiled=True, a...]
    unnamed x18, local copies, waits for them, and re-layouts: 0.05 us -> 1.26 us
    pallas_call x9 -> x11, Pallas kernels: 14.8 us -> 14.9 us  [call(): pl.pallas_call(kernel, out_shape=out_shape, in_specs=[vmem] * len(args) i...]
  transfers between devices with their start and end apart: 9 -> 9, of which waited for: 8 -> 8; matrix products, arithmetic and copies ran while one was open for 0% -> 0% of each run, Pallas kernels for 5% -> 8%
where the time goes in v3:
time: 69.7 us; the launch traced here: 69.2 us
  waiting for transfers between devices  26.3 us (38%)
  starting transfers between devices  24.6 us (35%)
  Pallas kernels  14.9 us (21%)
  local copies, waits for them, and re-layouts  1.26 us (2%)
  matrix products  1.23 us (2%)
  between operations  0.77 us (1%)
    pallas_call x11, Pallas kernels, call(): pl.pallas_call(kernel, out_shape=out_shape, in_specs=[vmem] * len(args) i...  14.9 us
    ppermute x1, waiting for transfers between devices, shards(): south = lax.ppermute(hi, 'trc', ring)  9.15 us
    all_to_all x1, waiting for transfers between devices, shards(): lax.all_to_all(reaction, 'trc', split_axis=0, concat_axis=0, tiled=True)  8.54 us
    all_to_all x1, starting transfers between devices, shards(): lax.all_to_all(payload, 'trc', split_axis=0, concat_axis=0, tiled=True, a...  7.26 us
    ppermute x3, starting transfers between devices, exchange_levels(): return lax.ppermute(part, 'lev', [(0, 1), (1, 0)])  4.64 us
    ppermute x3, waiting for transfers between devices, exchange_levels(): return lax.ppermute(part, 'lev', [(0, 1), (1, 0)])  4.59 us
    all_to_all x1, starting transfers between devices, shards(): lax.all_to_all(message, 'trc', split_axis=0, concat_axis=0, tiled=True)  4.13 us
    all_to_all x1, starting transfers between devices, shards(): lax.all_to_all(reaction, 'trc', split_axis=0, concat_axis=0, tiled=True)  4.1 us
  transfers between devices with their start and end apart: 9, of which 8 were waited for; matrix products, arithmetic and copies ran while one was open for 0% of the time, Pallas kernels for 8%

profile of v3, /device:TPU:0, one launch (start us, length us, event | category | flops | bytes accessed | tf_op | source)
XLA Modules:
  0.0 69.2 jit_solution(12217441011551678044)
XLA Ops:
  0.6 2.1 %pack_ocean.1 = (s32[8,48,128]{2,1,0:T(8,128)}, f32[16,64]{1,0:T(8,128)}, f32[16,64]{1,0:T(8,128)}, f32[144,128]{1,0:T(8,128)}) custom-call(f32[8,8,64]{2,1,0:T(8,128)} %bitcast.24, f32[8,8,64]{2,1,0:T(8,128)} %bitcast.26, f32[8,8,64]{2,1,0:T(8,128)} %bitcast.32, f32[8,8,64]{2,1,0:T(8,128)} %bitcast.33, s32[8,8,64]{2,1,0:T(8,128)} %bitcast.28, ...), custom_call_target="tpu_custom_call" | custom-call | tf_op jit(solution)/shard_map/pack_ocean/pallas_call | solution.py:31
  2.7 7.3 %all-to-all-start = ((s32[8,48,128]{2,1,0:T(8,128)}), s32[8,48,128]{2,1,0:T(8,128)S(1)}, u32[]{:S(2)}, u32[]{:S(2)}) async-start(s32[8,48,128]{2,1,0:T(8,128)} %get-tuple-element.34), calls=%async_computation | async-start | bytes 393216 | tf_op jit(solution)/shard_map/all_to_all | solution.py:192
  10.0 1.5 %collective-permute-start = (f32[144,128]{1,0:T(8,128)}, f32[144,128]{1,0:T(8,128)S(1)}, u32[]{:S(2)}, u32[]{:S(2)}) collective-permute-start(f32[144,128]{1,0:T(8,128)} %get-tuple-element.35), channel_id=1, source_target_pairs={{0,1},{1,0},{2,3},{3,2},{4,5},{5,4},{6,7},{7,6},{8,9},{9,8},{10,11... | collective-permute-start | bytes 221192 | tf_op jit(solution)/shard_map/ppermute | solution.py:62
  11.5 3.0 %collective-permute-done.h_ref.l_ref = f32[144,128]{1,0:T(8,128)S(1)} collective-permute-done((f32[144,128]{1,0:T(8,128)}, f32[144,128]{1,0:T(8,128)S(1)}, u32[]{:S(2)}, u32[]{:S(2)}) %collective-permute-start) | collective-permute-done | bytes 73760 | tf_op jit(solution)/shard_map/ppermute | solution.py:62
  14.5 1.2 %copy-done = f32[4,64,8,128]{3,2,1,0:T(8,128)S(1)} copy-done((f32[4,64,8,128]{3,2,1,0:T(8,128)S(1)}, f32[4,64,8,128]{3,2,1,0:T(8,128)}, u32[]{:S(2)}) %copy-start) | copy-done | bytes 1048600
  15.9 2.1 %all-to-all-done.a_ref = s32[8,48,128]{2,1,0:T(8,128)S(1)} async-done(((s32[8,48,128]{2,1,0:T(8,128)}), s32[8,48,128]{2,1,0:T(8,128)S(1)}, u32[]{:S(2)}, u32[]{:S(2)}) %all-to-all-start) | async-done | bytes 196640 | tf_op jit(solution)/shard_map/all_to_all | solution.py:192
  17.9 1.4 %collective-permute-done.1.b_ref = s32[8,48,128]{2,1,0:T(8,128)S(1)} collective-permute-done((s32[8,48,128]{2,1,0:T(8,128)S(1)}, s32[8,48,128]{2,1,0:T(8,128)S(1)}, u32[]{:S(2)}, u32[]{:S(2)}) %collective-permute-start.1) | collective-permute-done | bytes 196640 | tf_op jit(solution)/shard_map/ppermute | solution.py:220
  19.4 1.2 %unpack_ocean.1 = (f32[2,64,8,128]{3,2,1,0:T(8,128)S(1)}, f32[2,64,8,128]{3,2,1,0:T(8,128)S(1)}, f32[88,128]{1,0:T(8,128)S(1)}) custom-call(s32[8,48,128]{2,1,0:T(8,128)S(1)} %all-to-all-done.a_ref, s32[8,48,128]{2,1,0:T(8,128)S(1)} %collective-permute-done.1.b_ref), custom_call_target="tpu_custom_call" | custom-call | tf_op jit(solution)/shard_map/unpack_ocean/pallas_call | solution.py:31
  20.6 1.6 %collective-permute-start.2 = (f32[88,128]{1,0:T(8,128)S(1)}, f32[88,128]{1,0:T(8,128)S(1)}, u32[]{:S(2)}, u32[]{:S(2)}) collective-permute-start(f32[88,128]{1,0:T(8,128)S(1)} %get-tuple-element.40.o_ref), channel_id=1, source_target_pairs={{0,1},{1,0},{2,3},{3,2},{4,5},{5,4},{6,7},{7,6},{8,9},{9,8},{10,11... | collective-permute-start | bytes 135176 | tf_op jit(solution)/shard_map/ppermute | solution.py:62
  22.1 1.8 %first_slopes.1.side = f32[6,4,560,128]{3,2,1,0:T(8,128)S(1)} custom-call(f32[4,576,128]{2,1,0:T(8,128)S(1)} %widen_levels.1.pad), custom_call_target="tpu_custom_call" | custom-call | tf_op jit(solution)/shard_map/first_slopes/pallas_call | solution.py:31
  23.9 0.7 %collective-permute-done.2.r_ref = f32[88,128]{1,0:T(8,128)S(1)} collective-permute-done((f32[88,128]{1,0:T(8,128)S(1)}, f32[88,128]{1,0:T(8,128)S(1)}, u32[]{:S(2)}, u32[]{:S(2)}) %collective-permute-start.2) | collective-permute-done | bytes 45088 | tf_op jit(solution)/shard_map/ppermute | solution.py:62
  25.3 4.1 %advect_tracers.1 = (f32[4,512,128]{2,1,0:T(8,128)S(1)}, bf16[16,32,512]{2,1,0:T(8,128)(2,1)}) custom-call(f32[4,576,128]{2,1,0:T(8,128)S(1)} %widen_levels.1.pad, f32[6,4,560,128]{3,2,1,0:T(8,128)S(1)} %first_slopes.1.side, f32[2,68,8,128]{3,2,1,0:T(8,128)S(1)} %get-tuple-element.45.uv_ref, f32[69,8,128]{2,1,0:T(8,128)S(1)} %get-tuple-element.46.fv_ref), custom_call_target="tpu_custom_call" | custom-call | tf_op jit(solution)/shard_map/advect_tracers/pallas_call | solution.py:31
  29.4 4.1 %all-to-all-start.1 = ((bf16[16,32,512]{2,1,0:T(8,128)(2,1)}), bf16[16,32,512]{2,1,0:T(8,128)(2,1)S(1)}, u32[]{:S(2)}, u32[]{:S(2)}) async-start(bf16[16,32,512]{2,1,0:T(8,128)(2,1)} %get-tuple-element.50), calls=%async_computation.1 | async-start | bytes 1048576 | tf_op jit(solution)/shard_map/all_to_all | solution.py:471
  34.0 4.0 %collective-permute-start.4 = (f32[16,64]{1,0:T(8,128)S(1)}, f32[16,64]{1,0:T(8,128)S(1)}, u32[]{:S(2)}, u32[]{:S(2)}) collective-permute-start(f32[16,64]{1,0:T(8,128)S(1)} %copy-done.7), channel_id=1, source_target_pairs={{2,0},{4,2},{6,4},{8,6},{10,8},{12,10},{14,12},{16,14},{18,16},{20... | collective-permute-start | bytes 12296 | tf_op jit(solution)/shard_map/ppermute | solution.py:474
  38.5 9.1 %collective-permute-done.3.so_ref = f32[16,64]{1,0:T(8,128)S(1)} collective-permute-done((f32[16,64]{1,0:T(8,128)S(1)}, f32[16,64]{1,0:T(8,128)S(1)}, u32[]{:S(2)}, u32[]{:S(2)}) %collective-permute-start.3) | collective-permute-done | bytes 4128 | tf_op jit(solution)/shard_map/ppermute | solution.py:473
  48.1 1.2 %fusion = f16[512,512]{0,1:T(8,128)(2,1)} fusion(bf16[512,512]{1,0:T(8,128)(2,1)S(1)} %spread_coupling.1, bf16[512,512]{1,0:T(8,128)(2,1)S(1)} %bitcast.22), kind=kOutput, calls=%fused_computation.1 | convolution fusion | flops 268959744 | bytes 1572864 | tf_op jit(solution)/shard_map/dot_general | solution.py:570
  49.4 4.1 %all-to-all-start.2 = ((f16[16,32,512]{2,1,0:T(8,128)(2,1)}), f16[16,32,512]{2,1,0:T(8,128)(2,1)S(1)}, u32[]{:S(2)}, u32[]{:S(2)}) async-start(f16[16,32,512]{2,1,0:T(8,128)(2,1)} %bitcast.31), calls=%async_computation.2 | async-start | bytes 1048576 | tf_op jit(solution)/shard_map/all_to_all | solution.py:572
  53.5 1.0 %shade.1 = (f32[8,512]{1,0:T(8,128)S(1)}, f32[8,512]{1,0:T(8,128)S(1)}) custom-call(bf16[16,32,512]{2,1,0:T(8,128)(2,1)S(1)} %all-to-all-done.1.x_ref, s32[64]{0:T(128)S(1)} %copy-done.5, f32[8]{0:T(128)S(1)} %copy-done.6), custom_call_target="tpu_custom_call" | custom-call | tf_op jit(solution)/shard_map/shade/pallas_call | solution.py:31
  54.5 1.5 %collective-permute-start.5 = (f32[8,512]{1,0:T(8,128)S(1)}, f32[8,512]{1,0:T(8,128)S(1)}, u32[]{:S(2)}, u32[]{:S(2)}) collective-permute-start(f32[8,512]{1,0:T(8,128)S(1)} %get-tuple-element.55.cum_ref), channel_id=1, source_target_pairs={{0,1},{1,0},{2,3},{3,2},{4,5},{5,4},{6,7},{7,6},{8,9},{9,8},{10,11... | collective-permute-start | bytes 49160 | tf_op jit(solution)/shard_map/ppermute | solution.py:62
  56.0 1.4 %own_ocean.1 = (f32[8,8,64]{2,1,0:T(8,128)}, f32[8,8,64]{2,1,0:T(8,128)S(1)}, f32[8,8,64]{2,1,0:T(8,128)}, f32[8,8,64]{2,1,0:T(8,128)}) custom-call(f32[8,8,64]{2,1,0:T(8,128)S(1)} %bitcast.25, f32[8,8,64]{2,1,0:T(8,128)S(1)} %bitcast.27, f32[2,544,128]{2,1,0:T(8,128)S(1)} %bitcast.21, f32[552,128]{1,0:T(8,128)S(1)} %bitcast.23, ...), custom_call_target="tpu_custom_call" | custom-call | tf_op jit(solution)/shard_map/own_ocean/pallas_call | solution.py:31
  57.4 0.8 %collective-permute-done.5.r_ref = f32[8,512]{1,0:T(8,128)S(1)} collective-permute-done((f32[8,512]{1,0:T(8,128)S(1)}, f32[8,512]{1,0:T(8,128)S(1)}, u32[]{:S(2)}, u32[]{:S(2)}) %collective-permute-start.5) | collective-permute-done | bytes 16416 | tf_op jit(solution)/shard_map/ppermute | solution.py:62
  58.2 1.2 %heat.1 = f32[8,8,64]{2,1,0:T(8,128)} custom-call(f32[8,512]{1,0:T(8,128)S(1)} %get-tuple-element.54.att_ref, f32[8,512]{1,0:T(8,128)S(1)} %get-tuple-element.55.cum_ref, f32[8,512]{1,0:T(8,128)S(1)} %collective-permute-done.5.r_ref, f32[8,8,64]{2,1,0:T(8,128)S(1)} %get-tuple-element.58.w_ref, s32[8,8,64]{2,1,0:T(8,128)S(1)} %bitcast.29), custom_call_target="tpu_custom_call" | custom-call | tf_op jit(solution)/shard_map/heat/pallas_call | solution.py:31
  59.4 8.5 %all-to-all-done.2 = f16[16,32,512]{2,1,0:T(8,128)(2,1)S(1)} async-done(((f16[16,32,512]{2,1,0:T(8,128)(2,1)}), f16[16,32,512]{2,1,0:T(8,128)(2,1)S(1)}, u32[]{:S(2)}, u32[]{:S(2)}) %all-to-all-start.2) | async-done | bytes 524320 | tf_op jit(solution)/shard_map/all_to_all | solution.py:572
  68.1 1.1 %finish_tracers.1 = f32[4,512,128]{2,1,0:T(8,128)} custom-call(f32[16,32,512]{2,1,0:T(8,128)S(1)} %convert_element_type.11.r_ref, f32[4,512,128]{2,1,0:T(8,128)S(1)} %get-tuple-element.62.a_ref), custom_call_target="tpu_custom_call" | custom-call | tf_op jit(solution)/shard_map/finish_tracers/pallas_call | solution.py:31
  (25 shorter events, 2.2 us)
Async XLA Ops:
  2.7 15.2 %all-to-all-start = ((s32[8,48,128]{2,1,0:T(8,128)}), s32[8,48,128]{2,1,0:T(8,128)S(1)}, u32[]{:S(2)}, u32[]{:S(2)}) async-start(s32[8,48,128]{2,1,0:T(8,128)} %get-tuple-element.34), calls=%async_computation | async-start | bytes 393216 | tf_op jit(solution)/shard_map/all_to_all | solution.py:192
  10.0 4.6 %collective-permute-start = (f32[144,128]{1,0:T(8,128)}, f32[144,128]{1,0:T(8,128)S(1)}, u32[]{:S(2)}, u32[]{:S(2)}) collective-permute-start(f32[144,128]{1,0:T(8,128)} %get-tuple-element.35), channel_id=1, source_target_pairs={{0,1},{1,0},{2,3},{3,2},{4,5},{5,4},{6,7},{7,6},{8,9},{9,8},{10,11... | collective-permute-start | bytes 221192 | tf_op jit(solution)/shard_map/ppermute | solution.py:62
  14.5 1.2 %copy-start = (f32[4,64,8,128]{3,2,1,0:T(8,128)S(1)}, f32[4,64,8,128]{3,2,1,0:T(8,128)}, u32[]{:S(2)}) copy-start(f32[4,64,8,128]{3,2,1,0:T(8,128)} %param.14) | copy-start | bytes 3145732
  17.9 1.4 %collective-permute-start.1 = (s32[8,48,128]{2,1,0:T(8,128)S(1)}, s32[8,48,128]{2,1,0:T(8,128)S(1)}, u32[]{:S(2)}, u32[]{:S(2)}) collective-permute-start(s32[8,48,128]{2,1,0:T(8,128)S(1)} %all-to-all-done.a_ref), channel_id=1, source_target_pairs={{0,2},{2,0},{4,6},{6,4},{8,10},{10,8},{12,14},{14,12},{16,18},{18,... | collective-permute-start | bytes 589832 | tf_op jit(solution)/shard_map/ppermute | solution.py:220
  20.6 4.1 %collective-permute-start.2 = (f32[88,128]{1,0:T(8,128)S(1)}, f32[88,128]{1,0:T(8,128)S(1)}, u32[]{:S(2)}, u32[]{:S(2)}) collective-permute-start(f32[88,128]{1,0:T(8,128)S(1)} %get-tuple-element.40.o_ref), channel_id=1, source_target_pairs={{0,1},{1,0},{2,3},{3,2},{4,5},{5,4},{6,7},{7,6},{8,9},{9,8},{10,11... | collective-permute-start | bytes 135176 | tf_op jit(solution)/shard_map/ppermute | solution.py:62
  23.9 9.7 %copy-start.8 = (f32[16,64]{1,0:T(8,128)S(1)}, f32[16,64]{1,0:T(8,128)}, u32[]{:S(2)}) copy-start(f32[16,64]{1,0:T(8,128)} %get-tuple-element.51) | copy-start | bytes 12292
  23.9 10.1 %copy-start.7 = (f32[16,64]{1,0:T(8,128)S(1)}, f32[16,64]{1,0:T(8,128)}, u32[]{:S(2)}) copy-start(f32[16,64]{1,0:T(8,128)} %get-tuple-element.52) | copy-start | bytes 12292
  23.9 14.2 %copy-start.4 = (bf16[64,64]{1,0:T(8,128)(2,1)S(1)}, bf16[64,64]{1,0:T(8,128)(2,1)}, u32[]{:S(2)}) copy-start(bf16[64,64]{1,0:T(8,128)(2,1)} %c_ref.1) | copy-start | bytes 24580
  25.3 28.2 %copy-start.5 = (s32[64]{0:T(128)S(1)}, s32[64]{0:T(128)}, u32[]{:S(2)}) copy-start(s32[64]{0:T(128)} %g_ref.1) | copy-start | bytes 772
  25.3 28.2 %copy-start.6 = (f32[8]{0:T(128)S(1)}, f32[8]{0:T(128)}, u32[]{:S(2)}) copy-start(f32[8]{0:T(128)} %k_ref.1) | copy-start | bytes 100
  25.3 30.7 %copy-start.1 = (f32[64,8,8]{0,2,1:T(8,128)S(1)}, f32[64,8,8]{0,2,1:T(8,128)}, u32[]{:S(2)}) copy-start(f32[64,8,8]{0,2,1:T(8,128)} %param.9) | copy-start | bytes 49156
  25.3 30.7 %copy-start.2 = (f32[64,8,8]{0,2,1:T(8,128)S(1)}, f32[64,8,8]{0,2,1:T(8,128)}, u32[]{:S(2)}) copy-start(f32[64,8,8]{0,2,1:T(8,128)} %param.10) | copy-start | bytes 49156
  25.3 32.9 %copy-start.3 = (s32[64,8,8]{0,2,1:T(8,128)S(1)}, s32[64,8,8]{0,2,1:T(8,128)}, u32[]{:S(2)}) copy-start(s32[64,8,8]{0,2,1:T(8,128)} %param.13) | copy-start | bytes 49156
  29.4 18.7 %all-to-all-start.1 = ((bf16[16,32,512]{2,1,0:T(8,128)(2,1)}), bf16[16,32,512]{2,1,0:T(8,128)(2,1)S(1)}, u32[]{:S(2)}, u32[]{:S(2)}) async-start(bf16[16,32,512]{2,1,0:T(8,128)(2,1)} %get-tuple-element.50), calls=%async_computation.1 | async-start | bytes 1048576 | tf_op jit(solution)/shard_map/all_to_all | solution.py:471
  33.6 14.1 %collective-permute-start.3 = (f32[16,64]{1,0:T(8,128)S(1)}, f32[16,64]{1,0:T(8,128)S(1)}, u32[]{:S(2)}, u32[]{:S(2)}) collective-permute-start(f32[16,64]{1,0:T(8,128)S(1)} %copy-done.8), channel_id=1, source_target_pairs={{0,2},{2,4},{4,6},{6,8},{8,10},{10,12},{12,14},{14,16},{16,18},{18... | collective-permute-start | bytes 12296 | tf_op jit(solution)/shard_map/ppermute | solution.py:473
  34.0 13.6 %collective-permute-start.4 = (f32[16,64]{1,0:T(8,128)S(1)}, f32[16,64]{1,0:T(8,128)S(1)}, u32[]{:S(2)}, u32[]{:S(2)}) collective-permute-start(f32[16,64]{1,0:T(8,128)S(1)} %copy-done.7), channel_id=1, source_target_pairs={{2,0},{4,2},{6,4},{8,6},{10,8},{12,10},{14,12},{16,14},{18,16},{20... | collective-permute-start | bytes 12296 | tf_op jit(solution)/shard_map/ppermute | solution.py:474
  49.4 18.6 %all-to-all-start.2 = ((f16[16,32,512]{2,1,0:T(8,128)(2,1)}), f16[16,32,512]{2,1,0:T(8,128)(2,1)S(1)}, u32[]{:S(2)}, u32[]{:S(2)}) async-start(f16[16,32,512]{2,1,0:T(8,128)(2,1)} %bitcast.31), calls=%async_computation.2 | async-start | bytes 1048576 | tf_op jit(solution)/shard_map/all_to_all | solution.py:572
  54.5 3.8 %collective-permute-start.5 = (f32[8,512]{1,0:T(8,128)S(1)}, f32[8,512]{1,0:T(8,128)S(1)}, u32[]{:S(2)}, u32[]{:S(2)}) collective-permute-start(f32[8,512]{1,0:T(8,128)S(1)} %get-tuple-element.55.cum_ref), channel_id=1, source_target_pairs={{0,1},{1,0},{2,3},{3,2},{4,5},{5,4},{6,7},{7,6},{8,9},{9,8},{10,11... | collective-permute-start | bytes 49160 | tf_op jit(solution)/shard_map/ppermute | solution.py:62

commit v4 on v3

--- a/solution.py
+++ b/solution.py
@@ -139,7 +139,7 @@
         density = jnp.where(sea, 0.8 * s - 0.2 * t, 0.0)
         numbers, halves = 0, []
         for i, a in enumerate((density, held[2], held[3])):
-            most = jnp.max(jnp.abs(a))
+            most = jnp.max(jnp.abs(a), axis=(0, 1, 2), keepdims=True)[0]
             unit, number = tops[i], 0
             for k in range(1, SCALES + 1):
                 fits = most <= tops[i] * 2.0**-k
@@ -293,7 +293,7 @@
             return total, tuple(a + b for a, b in zip(sums, parts))
 
         zero = jnp.zeros((XE, YG), F32)
-        total, sums = lax.fori_loop(0, D, one, (zero, (zero,) * 4), unroll=16)
+        total, sums = lax.fori_loop(0, D, one, (zero, (zero,) * 4), unroll=D // 2)
         for i, a in enumerate((total,) + sums):
             l_ref[i * XE : (i + 1) * XE] = a
         first = jnp.where(lax.axis_index("lev") == 0, D - 2, 0)
@@ -383,20 +383,15 @@
             fv_ref[k + 2] = total
             return total
 
-        total = lax.fori_loop(0, D, climb, below, unroll=16)
+        total = lax.fori_loop(0, D, climb, below, unroll=D)
         fv_ref[2] = jnp.where(lev == 0, 0.0, total)
         for e in (1, 0):
             total = total + divergence(e)
             fv_ref[e] = total
 
-    uv, fv = call(
-        speeds,
-        (f32(2, D + 4, XE, YG), f32(D + 5, XE, YG)),
-        (near_uv, masks, own_levels, far_levels),
-        name="face_speeds",
-    )
-
-    def advect(pad, side, uv_ref, fv_ref, adv_ref, msg_any, mid_pad, held, sems):
+    def advect(n_ref, m_ref, o_ref, r_ref, pad, side, adv_ref, msg_any, uv_ref, fv_ref, mid_pad, held, sems):
+        speeds(n_ref, m_ref, o_ref, r_ref, uv_ref, fv_ref)
+
         def speeds_at(e):
             return tracer_step * uv_ref[0, e][None], tracer_step * uv_ref[1, e][None]
 
@@ -415,21 +410,28 @@
             return flux_next
 
         flux = fall(0, side[4, :, rows(0)], side[5, :, rows(1)])
-        lax.fori_loop(0, D + 4, first_step, flux, unroll=(D + 4) // 4)
+        lax.fori_loop(0, D + 4, first_step, flux, unroll=(D + 4) // 2)
 
         def second_step(k, carry):
+            B = 16
+            here = mid_pad[:, rows(k + 2, B * XE)].reshape(T, B, XE, YG)
+            u = tracer_step * uv_ref[0, pl.ds(k + 2, B)]
+            v = tracer_step * uv_ref[1, pl.ds(k + 2, B)]
+            flat = sideways(here, v, 3) + sideways(here, u, 2)
             mid, hi, up, flux = carry
-            nxt = mid_pad[:, rows(k + 4)]
-            half = half_slope(mid, hi, nxt)
-            flux_next = fall(k + 3, up, hi - half)
-            u, v = speeds_at(k + 2)
-            change = sideways(mid, u, 1) + sideways(mid, v, 2) + (flux_next - flux)
-            adv_ref[:, pl.ds(pl.multiple_of(k * X, 8), X)] = (mid - change)[:, H : H + X]
-            return hi, nxt, hi + half, flux_next
+            for j in range(B):
+                nxt = mid_pad[:, rows(k + j + 4)]
+                half = half_slope(mid, hi, nxt)
+                flux_next = fall(k + j + 3, up, hi - half)
+                new = mid - (flat[:, j] + (flux_next - flux))
+                adv_ref[:, pl.ds(pl.multiple_of((k + j) * X, 8), X)] = new[:, H : H + X]
+                mid, hi, up, flux = hi, nxt, hi + half, flux_next
+            return mid, hi, up, flux
 
         c = [mid_pad[:, rows(k)] for k in range(4)]
         half = half_slope(c[1], c[2], c[3])
         flux = fall(2, c[1] + half_slope(c[0], c[1], c[2]), c[2] - half)
+
         def sending(w):
             here = pl.ds(pl.multiple_of(w * LANES, LANES), LANES)
             return pltpu.make_async_copy(held.at[w], msg_any.at[:, :, here], sems.at[w])
@@ -443,28 +445,29 @@
             sending(w).start()
 
         def block(w, carry):
-            for k in range(RL):
+            for k in range(0, RL, 16):
                 carry = second_step(w * RL + k, carry)
             return carry
 
         count = DX // LANES
-        lax.fori_loop(0, count, block, (c[2], c[3], c[2] + half, flux))
+        lax.fori_loop(0, count, block, (c[2], c[3], c[2] + half, flux), unroll=2)
         for w in range(count):
             turn(w)
         for w in range(count):
             sending(w).wait()
 
     vmem = pl.BlockSpec(memory_space=pltpu.VMEM)
-    advected, message = call(
+    advected, message, uv, fv = call(
         advect,
-        (f32(T, DX, YG), pltpu.HBM((ntrc, T * Y, DX), jnp.bfloat16)),
-        (pad, side, uv, fv),
+        (f32(T, DX, YG), pltpu.HBM((ntrc, T * Y, DX), jnp.bfloat16))
+        + (f32(2, D + 4, XE, YG), f32(D + 5, XE, YG)),
+        (near_uv, masks, own_levels, far_levels, pad, side),
         scratch=(
             pltpu.VMEM((T, (D + 4) * XE, YG), F32),
             pltpu.VMEM((DX // LANES, ntrc, T * Y, LANES), jnp.bfloat16),
             pltpu.SemaphoreType.DMA((DX // LANES,)),
         ),
-        outs=(vmem, pl.BlockSpec(memory_space=pltpu.HBM)),
+        outs=(vmem, pl.BlockSpec(memory_space=pltpu.HBM), vmem, vmem),
         name="advect_tracers",
     )
     message, lo, hi = lax.optimization_barrier((message, lo, hi))

time: 69.7 us -> 68.6 us (0.984)
  Pallas kernels: 14.9 us -> 13.8 us
    pallas_call x11 -> x10, Pallas kernels: 14.9 us -> 13.8 us  [call(): pl.pallas_call(kernel, out_shape=out_shape, in_specs=[vmem] * len(args) i...]
where the time goes in v4:
time: 68.6 us; the launch traced here: 68.1 us
  waiting for transfers between devices  26.3 us (38%)
  starting transfers between devices  24.6 us (36%)
  Pallas kernels  13.8 us (20%)
  local copies, waits for them, and re-layouts  1.26 us (2%)
  matrix products  1.23 us (2%)
  between operations  0.77 us (1%)
    pallas_call x10, Pallas kernels, call(): pl.pallas_call(kernel, out_shape=out_shape, in_specs=[vmem] * len(args) i...  13.8 us
    ppermute x1, waiting for transfers between devices, shards(): south = lax.ppermute(hi, 'trc', ring)  9.15 us
    all_to_all x1, waiting for transfers between devices, shards(): lax.all_to_all(reaction, 'trc', split_axis=0, concat_axis=0, tiled=True)  8.55 us
    all_to_all x1, starting transfers between devices, shards(): lax.all_to_all(payload, 'trc', split_axis=0, concat_axis=0, tiled=True, a...  7.26 us
    ppermute x3, starting transfers between devices, exchange_levels(): return lax.ppermute(part, 'lev', [(0, 1), (1, 0)])  4.64 us
    ppermute x3, waiting for transfers between devices, exchange_levels(): return lax.ppermute(part, 'lev', [(0, 1), (1, 0)])  4.57 us
    all_to_all x1, starting transfers between devices, shards(): lax.all_to_all(message, 'trc', split_axis=0, concat_axis=0, tiled=True)  4.13 us
    all_to_all x1, starting transfers between devices, shards(): lax.all_to_all(reaction, 'trc', split_axis=0, concat_axis=0, tiled=True)  4.1 us
  transfers between devices with their start and end apart: 9, of which 8 were waited for; matrix products, arithmetic and copies ran while one was open for 0% of the time, Pallas kernels for 8%

profile of v4, /device:TPU:0, one launch (start us, length us, event | category | flops | bytes accessed | tf_op | source)
XLA Modules:
  0.0 68.1 jit_solution(15670313707966016231)
XLA Ops:
  0.6 1.9 %pack_ocean.1 = (s32[8,48,128]{2,1,0:T(8,128)}, f32[16,64]{1,0:T(8,128)}, f32[16,64]{1,0:T(8,128)}, f32[144,128]{1,0:T(8,128)}) custom-call(f32[8,8,64]{2,1,0:T(8,128)} %bitcast.24, f32[8,8,64]{2,1,0:T(8,128)} %bitcast.26, f32[8,8,64]{2,1,0:T(8,128)} %bitcast.32, f32[8,8,64]{2,1,0:T(8,128)} %bitcast.33, s32[8,8,64]{2,1,0:T(8,128)} %bitcast.28, ...), custom_call_target="tpu_custom_call" | custom-call | tf_op jit(solution)/shard_map/pack_ocean/pallas_call | solution.py:31
  2.5 7.3 %all-to-all-start = ((s32[8,48,128]{2,1,0:T(8,128)}), s32[8,48,128]{2,1,0:T(8,128)S(1)}, u32[]{:S(2)}, u32[]{:S(2)}) async-start(s32[8,48,128]{2,1,0:T(8,128)} %get-tuple-element.34), calls=%async_computation | async-start | bytes 393216 | tf_op jit(solution)/shard_map/all_to_all | solution.py:192
  9.8 1.5 %collective-permute-start = (f32[144,128]{1,0:T(8,128)}, f32[144,128]{1,0:T(8,128)S(1)}, u32[]{:S(2)}, u32[]{:S(2)}) collective-permute-start(f32[144,128]{1,0:T(8,128)} %get-tuple-element.35), channel_id=1, source_target_pairs={{0,1},{1,0},{2,3},{3,2},{4,5},{5,4},{6,7},{7,6},{8,9},{9,8},{10,11... | collective-permute-start | bytes 221192 | tf_op jit(solution)/shard_map/ppermute | solution.py:62
  11.3 3.0 %collective-permute-done.h_ref.l_ref = f32[144,128]{1,0:T(8,128)S(1)} collective-permute-done((f32[144,128]{1,0:T(8,128)}, f32[144,128]{1,0:T(8,128)S(1)}, u32[]{:S(2)}, u32[]{:S(2)}) %collective-permute-start) | collective-permute-done | bytes 73760 | tf_op jit(solution)/shard_map/ppermute | solution.py:62
  14.4 1.2 %copy-done = f32[4,64,8,128]{3,2,1,0:T(8,128)S(1)} copy-done((f32[4,64,8,128]{3,2,1,0:T(8,128)S(1)}, f32[4,64,8,128]{3,2,1,0:T(8,128)}, u32[]{:S(2)}) %copy-start) | copy-done | bytes 1048600
  15.7 2.1 %all-to-all-done.a_ref = s32[8,48,128]{2,1,0:T(8,128)S(1)} async-done(((s32[8,48,128]{2,1,0:T(8,128)}), s32[8,48,128]{2,1,0:T(8,128)S(1)}, u32[]{:S(2)}, u32[]{:S(2)}) %all-to-all-start) | async-done | bytes 196640 | tf_op jit(solution)/shard_map/all_to_all | solution.py:192
  17.8 1.4 %collective-permute-done.1.b_ref = s32[8,48,128]{2,1,0:T(8,128)S(1)} collective-permute-done((s32[8,48,128]{2,1,0:T(8,128)S(1)}, s32[8,48,128]{2,1,0:T(8,128)S(1)}, u32[]{:S(2)}, u32[]{:S(2)}) %collective-permute-start.1) | collective-permute-done | bytes 196640 | tf_op jit(solution)/shard_map/ppermute | solution.py:220
  19.2 1.0 %unpack_ocean.1 = (f32[2,64,8,128]{3,2,1,0:T(8,128)S(1)}, f32[2,64,8,128]{3,2,1,0:T(8,128)S(1)}, f32[88,128]{1,0:T(8,128)S(1)}) custom-call(s32[8,48,128]{2,1,0:T(8,128)S(1)} %all-to-all-done.a_ref, s32[8,48,128]{2,1,0:T(8,128)S(1)} %collective-permute-done.1.b_ref), custom_call_target="tpu_custom_call" | custom-call | tf_op jit(solution)/shard_map/unpack_ocean/pallas_call | solution.py:31
  20.2 1.6 %collective-permute-start.2 = (f32[88,128]{1,0:T(8,128)S(1)}, f32[88,128]{1,0:T(8,128)S(1)}, u32[]{:S(2)}, u32[]{:S(2)}) collective-permute-start(f32[88,128]{1,0:T(8,128)S(1)} %get-tuple-element.41.o_ref), channel_id=1, source_target_pairs={{0,1},{1,0},{2,3},{3,2},{4,5},{5,4},{6,7},{7,6},{8,9},{9,8},{10,11... | collective-permute-start | bytes 135176 | tf_op jit(solution)/shard_map/ppermute | solution.py:62
  21.8 1.8 %first_slopes.1.side = f32[6,4,560,128]{3,2,1,0:T(8,128)S(1)} custom-call(f32[4,576,128]{2,1,0:T(8,128)S(1)} %widen_levels.1.pad), custom_call_target="tpu_custom_call" | custom-call | tf_op jit(solution)/shard_map/first_slopes/pallas_call | solution.py:31
  23.7 0.7 %collective-permute-done.2.r_ref = f32[88,128]{1,0:T(8,128)S(1)} collective-permute-done((f32[88,128]{1,0:T(8,128)S(1)}, f32[88,128]{1,0:T(8,128)S(1)}, u32[]{:S(2)}, u32[]{:S(2)}) %collective-permute-start.2) | collective-permute-done | bytes 45088 | tf_op jit(solution)/shard_map/ppermute | solution.py:62
  24.4 4.0 %advect_tracers.1 = (f32[4,512,128]{2,1,0:T(8,128)S(1)}, bf16[16,32,512]{2,1,0:T(8,128)(2,1)}, f32[2,68,8,128]{3,2,1,0:T(8,128)S(1)}, f32[69,8,128]{2,1,0:T(8,128)S(1)}) custom-call(f32[2,64,8,128]{3,2,1,0:T(8,128)S(1)} %get-tuple-element.37.n_ref, f32[2,64,8,128]{3,2,1,0:T(8,128)S(1)} %get-tuple-element.38.m_ref, f32[88,128]{1,0:T(8,128)S(1)} %get-tuple-element.41.o_ref, ...), custom_call_target="tpu_custom_call" | custom-call | tf_op jit(solution)/shard_map/advect_tracers/pallas_call | solution.py:31
  28.3 4.1 %all-to-all-start.1 = ((bf16[16,32,512]{2,1,0:T(8,128)(2,1)}), bf16[16,32,512]{2,1,0:T(8,128)(2,1)S(1)}, u32[]{:S(2)}, u32[]{:S(2)}) async-start(bf16[16,32,512]{2,1,0:T(8,128)(2,1)} %get-tuple-element.48), calls=%async_computation.1 | async-start | bytes 1048576 | tf_op jit(solution)/shard_map/all_to_all | solution.py:474
  32.9 4.0 %collective-permute-start.4 = (f32[16,64]{1,0:T(8,128)S(1)}, f32[16,64]{1,0:T(8,128)S(1)}, u32[]{:S(2)}, u32[]{:S(2)}) collective-permute-start(f32[16,64]{1,0:T(8,128)S(1)} %copy-done.7), channel_id=1, source_target_pairs={{2,0},{4,2},{6,4},{8,6},{10,8},{12,10},{14,12},{16,14},{18,16},{20... | collective-permute-start | bytes 12296 | tf_op jit(solution)/shard_map/ppermute | solution.py:477
  37.4 9.1 %collective-permute-done.3.so_ref = f32[16,64]{1,0:T(8,128)S(1)} collective-permute-done((f32[16,64]{1,0:T(8,128)S(1)}, f32[16,64]{1,0:T(8,128)S(1)}, u32[]{:S(2)}, u32[]{:S(2)}) %collective-permute-start.3) | collective-permute-done | bytes 4128 | tf_op jit(solution)/shard_map/ppermute | solution.py:476
  47.0 1.2 %fusion = f16[512,512]{0,1:T(8,128)(2,1)} fusion(bf16[512,512]{1,0:T(8,128)(2,1)S(1)} %spread_coupling.1, bf16[512,512]{1,0:T(8,128)(2,1)S(1)} %bitcast.21), kind=kOutput, calls=%fused_computation.1 | convolution fusion | flops 268959744 | bytes 1572864 | tf_op jit(solution)/shard_map/dot_general | solution.py:573
  48.2 4.1 %all-to-all-start.2 = ((f16[16,32,512]{2,1,0:T(8,128)(2,1)}), f16[16,32,512]{2,1,0:T(8,128)(2,1)S(1)}, u32[]{:S(2)}, u32[]{:S(2)}) async-start(f16[16,32,512]{2,1,0:T(8,128)(2,1)} %bitcast.31), calls=%async_computation.2 | async-start | bytes 1048576 | tf_op jit(solution)/shard_map/all_to_all | solution.py:575
  52.4 1.0 %shade.1 = (f32[8,512]{1,0:T(8,128)S(1)}, f32[8,512]{1,0:T(8,128)S(1)}) custom-call(bf16[16,32,512]{2,1,0:T(8,128)(2,1)S(1)} %all-to-all-done.1.x_ref, s32[64]{0:T(128)S(1)} %copy-done.5, f32[8]{0:T(128)S(1)} %copy-done.6), custom_call_target="tpu_custom_call" | custom-call | tf_op jit(solution)/shard_map/shade/pallas_call | solution.py:31
  53.3 1.5 %collective-permute-start.5 = (f32[8,512]{1,0:T(8,128)S(1)}, f32[8,512]{1,0:T(8,128)S(1)}, u32[]{:S(2)}, u32[]{:S(2)}) collective-permute-start(f32[8,512]{1,0:T(8,128)S(1)} %get-tuple-element.53.cum_ref), channel_id=1, source_target_pairs={{0,1},{1,0},{2,3},{3,2},{4,5},{5,4},{6,7},{7,6},{8,9},{9,8},{10,11... | collective-permute-start | bytes 49160 | tf_op jit(solution)/shard_map/ppermute | solution.py:62
  54.9 1.4 %own_ocean.1 = (f32[8,8,64]{2,1,0:T(8,128)}, f32[8,8,64]{2,1,0:T(8,128)S(1)}, f32[8,8,64]{2,1,0:T(8,128)}, f32[8,8,64]{2,1,0:T(8,128)}) custom-call(f32[8,8,64]{2,1,0:T(8,128)S(1)} %bitcast.25, f32[8,8,64]{2,1,0:T(8,128)S(1)} %bitcast.27, f32[2,544,128]{2,1,0:T(8,128)S(1)} %bitcast.22, f32[552,128]{1,0:T(8,128)S(1)} %bitcast.23, ...), custom_call_target="tpu_custom_call" | custom-call | tf_op jit(solution)/shard_map/own_ocean/pallas_call | solution.py:31
  56.3 0.8 %collective-permute-done.5.r_ref = f32[8,512]{1,0:T(8,128)S(1)} collective-permute-done((f32[8,512]{1,0:T(8,128)S(1)}, f32[8,512]{1,0:T(8,128)S(1)}, u32[]{:S(2)}, u32[]{:S(2)}) %collective-permute-start.5) | collective-permute-done | bytes 16416 | tf_op jit(solution)/shard_map/ppermute | solution.py:62
  57.1 1.2 %heat.1 = f32[8,8,64]{2,1,0:T(8,128)} custom-call(f32[8,512]{1,0:T(8,128)S(1)} %get-tuple-element.52.att_ref, f32[8,512]{1,0:T(8,128)S(1)} %get-tuple-element.53.cum_ref, f32[8,512]{1,0:T(8,128)S(1)} %collective-permute-done.5.r_ref, f32[8,8,64]{2,1,0:T(8,128)S(1)} %get-tuple-element.58.w_ref, s32[8,8,64]{2,1,0:T(8,128)S(1)} %bitcast.29), custom_call_target="tpu_custom_call" | custom-call | tf_op jit(solution)/shard_map/heat/pallas_call | solution.py:31
  58.3 8.6 %all-to-all-done.2 = f16[16,32,512]{2,1,0:T(8,128)(2,1)S(1)} async-done(((f16[16,32,512]{2,1,0:T(8,128)(2,1)}), f16[16,32,512]{2,1,0:T(8,128)(2,1)S(1)}, u32[]{:S(2)}, u32[]{:S(2)}) %all-to-all-start.2) | async-done | bytes 524320 | tf_op jit(solution)/shard_map/all_to_all | solution.py:575
  66.9 1.1 %finish_tracers.1 = f32[4,512,128]{2,1,0:T(8,128)} custom-call(f32[16,32,512]{2,1,0:T(8,128)S(1)} %convert_element_type.11.r_ref, f32[4,512,128]{2,1,0:T(8,128)S(1)} %get-tuple-element.62.a_ref), custom_call_target="tpu_custom_call" | custom-call | tf_op jit(solution)/shard_map/finish_tracers/pallas_call | solution.py:31
  (24 shorter events, 1.6 us)
Async XLA Ops:
  2.5 15.2 %all-to-all-start = ((s32[8,48,128]{2,1,0:T(8,128)}), s32[8,48,128]{2,1,0:T(8,128)S(1)}, u32[]{:S(2)}, u32[]{:S(2)}) async-start(s32[8,48,128]{2,1,0:T(8,128)} %get-tuple-element.34), calls=%async_computation | async-start | bytes 393216 | tf_op jit(solution)/shard_map/all_to_all | solution.py:192
  9.8 4.6 %collective-permute-start = (f32[144,128]{1,0:T(8,128)}, f32[144,128]{1,0:T(8,128)S(1)}, u32[]{:S(2)}, u32[]{:S(2)}) collective-permute-start(f32[144,128]{1,0:T(8,128)} %get-tuple-element.35), channel_id=1, source_target_pairs={{0,1},{1,0},{2,3},{3,2},{4,5},{5,4},{6,7},{7,6},{8,9},{9,8},{10,11... | collective-permute-start | bytes 221192 | tf_op jit(solution)/shard_map/ppermute | solution.py:62
  14.4 1.2 %copy-start = (f32[4,64,8,128]{3,2,1,0:T(8,128)S(1)}, f32[4,64,8,128]{3,2,1,0:T(8,128)}, u32[]{:S(2)}) copy-start(f32[4,64,8,128]{3,2,1,0:T(8,128)} %param.14) | copy-start | bytes 3145732
  17.8 1.4 %collective-permute-start.1 = (s32[8,48,128]{2,1,0:T(8,128)S(1)}, s32[8,48,128]{2,1,0:T(8,128)S(1)}, u32[]{:S(2)}, u32[]{:S(2)}) collective-permute-start(s32[8,48,128]{2,1,0:T(8,128)S(1)} %all-to-all-done.a_ref), channel_id=1, source_target_pairs={{0,2},{2,0},{4,6},{6,4},{8,10},{10,8},{12,14},{14,12},{16,18},{18,... | collective-permute-start | bytes 589832 | tf_op jit(solution)/shard_map/ppermute | solution.py:220
  20.2 4.1 %collective-permute-start.2 = (f32[88,128]{1,0:T(8,128)S(1)}, f32[88,128]{1,0:T(8,128)S(1)}, u32[]{:S(2)}, u32[]{:S(2)}) collective-permute-start(f32[88,128]{1,0:T(8,128)S(1)} %get-tuple-element.41.o_ref), channel_id=1, source_target_pairs={{0,1},{1,0},{2,3},{3,2},{4,5},{5,4},{6,7},{7,6},{8,9},{9,8},{10,11... | collective-permute-start | bytes 135176 | tf_op jit(solution)/shard_map/ppermute | solution.py:62
  23.6 8.9 %copy-start.8 = (f32[16,64]{1,0:T(8,128)S(1)}, f32[16,64]{1,0:T(8,128)}, u32[]{:S(2)}) copy-start(f32[16,64]{1,0:T(8,128)} %get-tuple-element.49) | copy-start | bytes 12292
  23.6 9.3 %copy-start.7 = (f32[16,64]{1,0:T(8,128)S(1)}, f32[16,64]{1,0:T(8,128)}, u32[]{:S(2)}) copy-start(f32[16,64]{1,0:T(8,128)} %get-tuple-element.50) | copy-start | bytes 12292
  23.6 13.4 %copy-start.4 = (bf16[64,64]{1,0:T(8,128)(2,1)S(1)}, bf16[64,64]{1,0:T(8,128)(2,1)}, u32[]{:S(2)}) copy-start(bf16[64,64]{1,0:T(8,128)(2,1)} %c_ref.1) | copy-start | bytes 24580
  23.6 28.7 %copy-start.5 = (s32[64]{0:T(128)S(1)}, s32[64]{0:T(128)}, u32[]{:S(2)}) copy-start(s32[64]{0:T(128)} %g_ref.1) | copy-start | bytes 772
  23.7 28.7 %copy-start.6 = (f32[8]{0:T(128)S(1)}, f32[8]{0:T(128)}, u32[]{:S(2)}) copy-start(f32[8]{0:T(128)} %k_ref.1) | copy-start | bytes 100
  24.4 30.5 %copy-start.1 = (f32[64,8,8]{0,2,1:T(8,128)S(1)}, f32[64,8,8]{0,2,1:T(8,128)}, u32[]{:S(2)}) copy-start(f32[64,8,8]{0,2,1:T(8,128)} %param.9) | copy-start | bytes 49156
  24.4 30.5 %copy-start.2 = (f32[64,8,8]{0,2,1:T(8,128)S(1)}, f32[64,8,8]{0,2,1:T(8,128)}, u32[]{:S(2)}) copy-start(f32[64,8,8]{0,2,1:T(8,128)} %param.10) | copy-start | bytes 49156
  24.4 32.7 %copy-start.3 = (s32[64,8,8]{0,2,1:T(8,128)S(1)}, s32[64,8,8]{0,2,1:T(8,128)}, u32[]{:S(2)}) copy-start(s32[64,8,8]{0,2,1:T(8,128)} %param.13) | copy-start | bytes 49156
  28.3 18.7 %all-to-all-start.1 = ((bf16[16,32,512]{2,1,0:T(8,128)(2,1)}), bf16[16,32,512]{2,1,0:T(8,128)(2,1)S(1)}, u32[]{:S(2)}, u32[]{:S(2)}) async-start(bf16[16,32,512]{2,1,0:T(8,128)(2,1)} %get-tuple-element.48), calls=%async_computation.1 | async-start | bytes 1048576 | tf_op jit(solution)/shard_map/all_to_all | solution.py:474
  32.5 14.1 %collective-permute-start.3 = (f32[16,64]{1,0:T(8,128)S(1)}, f32[16,64]{1,0:T(8,128)S(1)}, u32[]{:S(2)}, u32[]{:S(2)}) collective-permute-start(f32[16,64]{1,0:T(8,128)S(1)} %copy-done.8), channel_id=1, source_target_pairs={{0,2},{2,4},{4,6},{6,8},{8,10},{10,12},{12,14},{14,16},{16,18},{18... | collective-permute-start | bytes 12296 | tf_op jit(solution)/shard_map/ppermute | solution.py:476
  32.9 13.6 %collective-permute-start.4 = (f32[16,64]{1,0:T(8,128)S(1)}, f32[16,64]{1,0:T(8,128)S(1)}, u32[]{:S(2)}, u32[]{:S(2)}) collective-permute-start(f32[16,64]{1,0:T(8,128)S(1)} %copy-done.7), channel_id=1, source_target_pairs={{2,0},{4,2},{6,4},{8,6},{10,8},{12,10},{14,12},{16,14},{18,16},{20... | collective-permute-start | bytes 12296 | tf_op jit(solution)/shard_map/ppermute | solution.py:477
  48.2 18.6 %all-to-all-start.2 = ((f16[16,32,512]{2,1,0:T(8,128)(2,1)}), f16[16,32,512]{2,1,0:T(8,128)(2,1)S(1)}, u32[]{:S(2)}, u32[]{:S(2)}) async-start(f16[16,32,512]{2,1,0:T(8,128)(2,1)} %bitcast.31), calls=%async_computation.2 | async-start | bytes 1048576 | tf_op jit(solution)/shard_map/all_to_all | solution.py:575
  53.3 3.8 %collective-permute-start.5 = (f32[8,512]{1,0:T(8,128)S(1)}, f32[8,512]{1,0:T(8,128)S(1)}, u32[]{:S(2)}, u32[]{:S(2)}) collective-permute-start(f32[8,512]{1,0:T(8,128)S(1)} %get-tuple-element.53.cum_ref), channel_id=1, source_target_pairs={{0,1},{1,0},{2,3},{3,2},{4,5},{5,4},{6,7},{7,6},{8,9},{9,8},{10,11... | collective-permute-start | bytes 49160 | tf_op jit(solution)/shard_map/ppermute | solution.py:62

commit v5 on v4

--- a/solution.py
+++ b/solution.py
@@ -389,7 +389,7 @@
             total = total + divergence(e)
             fv_ref[e] = total
 
-    def advect(n_ref, m_ref, o_ref, r_ref, pad, side, adv_ref, msg_any, uv_ref, fv_ref, mid_pad, held, sems):
+    def advect(n_ref, m_ref, o_ref, r_ref, pad, side, adv_ref, msg_any, uv_ref, fv_ref, mid_pad, part, held, sems):
         speeds(n_ref, m_ref, o_ref, r_ref, uv_ref, fv_ref)
 
         def speeds_at(e):
@@ -413,18 +413,17 @@
         lax.fori_loop(0, D + 4, first_step, flux, unroll=(D + 4) // 2)
 
         def second_step(k, carry):
-            B = 16
+            B = RL
             here = mid_pad[:, rows(k + 2, B * XE)].reshape(T, B, XE, YG)
             u = tracer_step * uv_ref[0, pl.ds(k + 2, B)]
-            v = tracer_step * uv_ref[1, pl.ds(k + 2, B)]
-            flat = sideways(here, v, 3) + sideways(here, u, 2)
+            flat = sideways(here, u, 2)
             mid, hi, up, flux = carry
             for j in range(B):
                 nxt = mid_pad[:, rows(k + j + 4)]
                 half = half_slope(mid, hi, nxt)
                 flux_next = fall(k + j + 3, up, hi - half)
                 new = mid - (flat[:, j] + (flux_next - flux))
-                adv_ref[:, pl.ds(pl.multiple_of((k + j) * X, 8), X)] = new[:, H : H + X]
+                part[:, pl.ds(pl.multiple_of((k + j) * X, 8), X)] = new[:, H : H + X]
                 mid, hi, up, flux = hi, nxt, hi + half, flux_next
             return mid, hi, up, flux
 
@@ -437,20 +436,27 @@
             return pltpu.make_async_copy(held.at[w], msg_any.at[:, :, here], sems.at[w])
 
         def turn(w):
-            here = pl.ds(pl.multiple_of(w * LANES, LANES), LANES)
-            turned = [adv_ref[t, here].T for t in range(T)]
+            here = pl.ds(w * LANES, LANES)
+
+            def turned(a):
+                return a.reshape(RL, XE, YG)[:, H : H + X].reshape(LANES, YG).T
+
+            v = turned(tracer_step * uv_ref[1, pl.ds(w * RL + 2, RL)])
+            new = []
+            for t in range(T):
+                c = turned(mid_pad[t, rows(w * RL + 2, RL * XE)])
+                new.append(part[t, here].T - sideways(c, v, 0))
+                adv_ref[t, :, here] = new[t]
             for d in range(ntrc):
-                there = [turned[t][d * Y : (d + 1) * Y] for t in range(T)]
+                there = [new[t][d * Y : (d + 1) * Y] for t in range(T)]
                 held[w, d] = jnp.concatenate(there, axis=0).astype(jnp.bfloat16)
             sending(w).start()
 
         def block(w, carry):
-            for k in range(0, RL, 16):
-                carry = second_step(w * RL + k, carry)
-            return carry
+            return second_step(w * RL, carry)
 
         count = DX // LANES
-        lax.fori_loop(0, count, block, (c[2], c[3], c[2] + half, flux), unroll=2)
+        lax.fori_loop(0, count, block, (c[2], c[3], c[2] + half, flux))
         for w in range(count):
             turn(w)
         for w in range(count):
@@ -459,11 +465,12 @@
     vmem = pl.BlockSpec(memory_space=pltpu.VMEM)
     advected, message, uv, fv = call(
         advect,
-        (f32(T, DX, YG), pltpu.HBM((ntrc, T * Y, DX), jnp.bfloat16))
+        (f32(T, YG, DX), pltpu.HBM((ntrc, T * Y, DX), jnp.bfloat16))
         + (f32(2, D + 4, XE, YG), f32(D + 5, XE, YG)),
         (near_uv, masks, own_levels, far_levels, pad, side),
         scratch=(
             pltpu.VMEM((T, (D + 4) * XE, YG), F32),
+            pltpu.VMEM((T, DX, YG), F32),
             pltpu.VMEM((DX // LANES, ntrc, T * Y, LANES), jnp.bfloat16),
             pltpu.SemaphoreType.DMA((DX // LANES,)),
         ),
@@ -630,7 +637,7 @@
                     r_ref[d, t * Y : (t + 1) * Y, w * LANES : (w + 1) * LANES] for d in range(ntrc)
                 ]
                 here = slice(w * LANES, (w + 1) * LANES)
-                o_ref[t, here] = a_ref[t, here] + (react_step * unit) * jnp.concatenate(rows, axis=0).T
+                o_ref[t, here] = (a_ref[t, :, here] + (react_step * unit) * jnp.concatenate(rows, axis=0)).T
             copies[t].start()
         for copy in copies:
             copy.wait()

time: 68.6 us -> 68.2 us (level)
  transfers between devices with their start and end apart: 9 -> 9, of which waited for: 8 -> 8; matrix products, arithmetic and copies ran while one was open for 0% -> 0% of each run, Pallas kernels for 8% -> 9%
where the time goes in v5:
time: 68.2 us; the launch traced here: 67.7 us
  waiting for transfers between devices  26.3 us (39%)
  starting transfers between devices  24.6 us (36%)
  Pallas kernels  13.4 us (20%)
  local copies, waits for them, and re-layouts  1.26 us (2%)
  matrix products  1.23 us (2%)
  between operations  0.77 us (1%)
    pallas_call x10, Pallas kernels, call(): pl.pallas_call(kernel, out_shape=out_shape, in_specs=[vmem] * len(args) i...  13.4 us
    ppermute x1, waiting for transfers between devices, shards(): south = lax.ppermute(hi, 'trc', ring)  9.15 us
    all_to_all x1, waiting for transfers between devices, shards(): lax.all_to_all(reaction, 'trc', split_axis=0, concat_axis=0, tiled=True)  8.55 us
    all_to_all x1, starting transfers between devices, shards(): lax.all_to_all(payload, 'trc', split_axis=0, concat_axis=0, tiled=True, a...  7.26 us
    ppermute x3, starting transfers between devices, exchange_levels(): return lax.ppermute(part, 'lev', [(0, 1), (1, 0)])  4.64 us
    ppermute x3, waiting for transfers between devices, exchange_levels(): return lax.ppermute(part, 'lev', [(0, 1), (1, 0)])  4.57 us
    all_to_all x1, starting transfers between devices, shards(): lax.all_to_all(message, 'trc', split_axis=0, concat_axis=0, tiled=True)  4.13 us
    all_to_all x1, starting transfers between devices, shards(): lax.all_to_all(reaction, 'trc', split_axis=0, concat_axis=0, tiled=True)  4.1 us
  transfers between devices with their start and end apart: 9, of which 8 were waited for; matrix products, arithmetic and copies ran while one was open for 0% of the time, Pallas kernels for 9%

profile of v5, /device:TPU:0, one launch (start us, length us, event | category | flops | bytes accessed | tf_op | source)
XLA Modules:
  0.0 67.7 jit_solution(4711638630967348228)
XLA Ops:
  0.6 1.9 %pack_ocean.1 = (s32[8,48,128]{2,1,0:T(8,128)}, f32[16,64]{1,0:T(8,128)}, f32[16,64]{1,0:T(8,128)}, f32[144,128]{1,0:T(8,128)}) custom-call(f32[8,8,64]{2,1,0:T(8,128)} %bitcast.24, f32[8,8,64]{2,1,0:T(8,128)} %bitcast.26, f32[8,8,64]{2,1,0:T(8,128)} %bitcast.32, f32[8,8,64]{2,1,0:T(8,128)} %bitcast.33, s32[8,8,64]{2,1,0:T(8,128)} %bitcast.28, ...), custom_call_target="tpu_custom_call" | custom-call | tf_op jit(solution)/shard_map/pack_ocean/pallas_call | solution.py:31
  2.5 7.3 %all-to-all-start = ((s32[8,48,128]{2,1,0:T(8,128)}), s32[8,48,128]{2,1,0:T(8,128)S(1)}, u32[]{:S(2)}, u32[]{:S(2)}) async-start(s32[8,48,128]{2,1,0:T(8,128)} %get-tuple-element.34), calls=%async_computation | async-start | bytes 393216 | tf_op jit(solution)/shard_map/all_to_all | solution.py:192
  9.8 1.5 %collective-permute-start = (f32[144,128]{1,0:T(8,128)}, f32[144,128]{1,0:T(8,128)S(1)}, u32[]{:S(2)}, u32[]{:S(2)}) collective-permute-start(f32[144,128]{1,0:T(8,128)} %get-tuple-element.35), channel_id=1, source_target_pairs={{0,1},{1,0},{2,3},{3,2},{4,5},{5,4},{6,7},{7,6},{8,9},{9,8},{10,11... | collective-permute-start | bytes 221192 | tf_op jit(solution)/shard_map/ppermute | solution.py:62
  11.3 3.0 %collective-permute-done.h_ref.l_ref = f32[144,128]{1,0:T(8,128)S(1)} collective-permute-done((f32[144,128]{1,0:T(8,128)}, f32[144,128]{1,0:T(8,128)S(1)}, u32[]{:S(2)}, u32[]{:S(2)}) %collective-permute-start) | collective-permute-done | bytes 73760 | tf_op jit(solution)/shard_map/ppermute | solution.py:62
  14.4 1.2 %copy-done = f32[4,64,8,128]{3,2,1,0:T(8,128)S(1)} copy-done((f32[4,64,8,128]{3,2,1,0:T(8,128)S(1)}, f32[4,64,8,128]{3,2,1,0:T(8,128)}, u32[]{:S(2)}) %copy-start) | copy-done | bytes 1048600
  15.7 2.1 %all-to-all-done.a_ref = s32[8,48,128]{2,1,0:T(8,128)S(1)} async-done(((s32[8,48,128]{2,1,0:T(8,128)}), s32[8,48,128]{2,1,0:T(8,128)S(1)}, u32[]{:S(2)}, u32[]{:S(2)}) %all-to-all-start) | async-done | bytes 196640 | tf_op jit(solution)/shard_map/all_to_all | solution.py:192
  17.8 1.4 %collective-permute-done.1.b_ref = s32[8,48,128]{2,1,0:T(8,128)S(1)} collective-permute-done((s32[8,48,128]{2,1,0:T(8,128)S(1)}, s32[8,48,128]{2,1,0:T(8,128)S(1)}, u32[]{:S(2)}, u32[]{:S(2)}) %collective-permute-start.1) | collective-permute-done | bytes 196640 | tf_op jit(solution)/shard_map/ppermute | solution.py:220
  19.2 1.0 %unpack_ocean.1 = (f32[2,64,8,128]{3,2,1,0:T(8,128)S(1)}, f32[2,64,8,128]{3,2,1,0:T(8,128)S(1)}, f32[88,128]{1,0:T(8,128)S(1)}) custom-call(s32[8,48,128]{2,1,0:T(8,128)S(1)} %all-to-all-done.a_ref, s32[8,48,128]{2,1,0:T(8,128)S(1)} %collective-permute-done.1.b_ref), custom_call_target="tpu_custom_call" | custom-call | tf_op jit(solution)/shard_map/unpack_ocean/pallas_call | solution.py:31
  20.2 1.6 %collective-permute-start.2 = (f32[88,128]{1,0:T(8,128)S(1)}, f32[88,128]{1,0:T(8,128)S(1)}, u32[]{:S(2)}, u32[]{:S(2)}) collective-permute-start(f32[88,128]{1,0:T(8,128)S(1)} %get-tuple-element.41.o_ref), channel_id=1, source_target_pairs={{0,1},{1,0},{2,3},{3,2},{4,5},{5,4},{6,7},{7,6},{8,9},{9,8},{10,11... | collective-permute-start | bytes 135176 | tf_op jit(solution)/shard_map/ppermute | solution.py:62
  21.8 1.8 %first_slopes.1.side = f32[6,4,560,128]{3,2,1,0:T(8,128)S(1)} custom-call(f32[4,576,128]{2,1,0:T(8,128)S(1)} %widen_levels.1.pad), custom_call_target="tpu_custom_call" | custom-call | tf_op jit(solution)/shard_map/first_slopes/pallas_call | solution.py:31
  23.7 0.7 %collective-permute-done.2.r_ref = f32[88,128]{1,0:T(8,128)S(1)} collective-permute-done((f32[88,128]{1,0:T(8,128)S(1)}, f32[88,128]{1,0:T(8,128)S(1)}, u32[]{:S(2)}, u32[]{:S(2)}) %collective-permute-start.2) | collective-permute-done | bytes 45088 | tf_op jit(solution)/shard_map/ppermute | solution.py:62
  24.4 3.5 %advect_tracers.1 = (f32[4,128,512]{2,1,0:T(8,128)S(1)}, bf16[16,32,512]{2,1,0:T(8,128)(2,1)}, f32[2,68,8,128]{3,2,1,0:T(8,128)S(1)}, f32[69,8,128]{2,1,0:T(8,128)S(1)}) custom-call(f32[2,64,8,128]{3,2,1,0:T(8,128)S(1)} %get-tuple-element.37.n_ref, f32[2,64,8,128]{3,2,1,0:T(8,128)S(1)} %get-tuple-element.38.m_ref, f32[88,128]{1,0:T(8,128)S(1)} %get-tuple-element.41.o_ref, ...), custom_call_target="tpu_custom_call" | custom-call | tf_op jit(solution)/shard_map/advect_tracers/pallas_call | solution.py:31
  27.9 4.1 %all-to-all-start.1 = ((bf16[16,32,512]{2,1,0:T(8,128)(2,1)}), bf16[16,32,512]{2,1,0:T(8,128)(2,1)S(1)}, u32[]{:S(2)}, u32[]{:S(2)}) async-start(bf16[16,32,512]{2,1,0:T(8,128)(2,1)} %get-tuple-element.48), calls=%async_computation.1 | async-start | bytes 1048576 | tf_op jit(solution)/shard_map/all_to_all | solution.py:481
  32.5 4.0 %collective-permute-start.4 = (f32[16,64]{1,0:T(8,128)S(1)}, f32[16,64]{1,0:T(8,128)S(1)}, u32[]{:S(2)}, u32[]{:S(2)}) collective-permute-start(f32[16,64]{1,0:T(8,128)S(1)} %copy-done.7), channel_id=1, source_target_pairs={{2,0},{4,2},{6,4},{8,6},{10,8},{12,10},{14,12},{16,14},{18,16},{20... | collective-permute-start | bytes 12296 | tf_op jit(solution)/shard_map/ppermute | solution.py:484
  36.9 9.1 %collective-permute-done.3.so_ref = f32[16,64]{1,0:T(8,128)S(1)} collective-permute-done((f32[16,64]{1,0:T(8,128)S(1)}, f32[16,64]{1,0:T(8,128)S(1)}, u32[]{:S(2)}, u32[]{:S(2)}) %collective-permute-start.3) | collective-permute-done | bytes 4128 | tf_op jit(solution)/shard_map/ppermute | solution.py:483
  46.6 1.2 %fusion = f16[512,512]{0,1:T(8,128)(2,1)} fusion(bf16[512,512]{1,0:T(8,128)(2,1)S(1)} %spread_coupling.1, bf16[512,512]{1,0:T(8,128)(2,1)S(1)} %bitcast.21), kind=kOutput, calls=%fused_computation.1 | convolution fusion | flops 268959744 | bytes 1572864 | tf_op jit(solution)/shard_map/dot_general | solution.py:580
  47.8 4.1 %all-to-all-start.2 = ((f16[16,32,512]{2,1,0:T(8,128)(2,1)}), f16[16,32,512]{2,1,0:T(8,128)(2,1)S(1)}, u32[]{:S(2)}, u32[]{:S(2)}) async-start(f16[16,32,512]{2,1,0:T(8,128)(2,1)} %bitcast.31), calls=%async_computation.2 | async-start | bytes 1048576 | tf_op jit(solution)/shard_map/all_to_all | solution.py:582
  51.9 1.0 %shade.1 = (f32[8,512]{1,0:T(8,128)S(1)}, f32[8,512]{1,0:T(8,128)S(1)}) custom-call(bf16[16,32,512]{2,1,0:T(8,128)(2,1)S(1)} %all-to-all-done.1.x_ref, s32[64]{0:T(128)S(1)} %copy-done.5, f32[8]{0:T(128)S(1)} %copy-done.6), custom_call_target="tpu_custom_call" | custom-call | tf_op jit(solution)/shard_map/shade/pallas_call | solution.py:31
  52.9 1.5 %collective-permute-start.5 = (f32[8,512]{1,0:T(8,128)S(1)}, f32[8,512]{1,0:T(8,128)S(1)}, u32[]{:S(2)}, u32[]{:S(2)}) collective-permute-start(f32[8,512]{1,0:T(8,128)S(1)} %get-tuple-element.53.cum_ref), channel_id=1, source_target_pairs={{0,1},{1,0},{2,3},{3,2},{4,5},{5,4},{6,7},{7,6},{8,9},{9,8},{10,11... | collective-permute-start | bytes 49160 | tf_op jit(solution)/shard_map/ppermute | solution.py:62
  54.5 1.4 %own_ocean.1 = (f32[8,8,64]{2,1,0:T(8,128)}, f32[8,8,64]{2,1,0:T(8,128)S(1)}, f32[8,8,64]{2,1,0:T(8,128)}, f32[8,8,64]{2,1,0:T(8,128)}) custom-call(f32[8,8,64]{2,1,0:T(8,128)S(1)} %bitcast.25, f32[8,8,64]{2,1,0:T(8,128)S(1)} %bitcast.27, f32[2,544,128]{2,1,0:T(8,128)S(1)} %bitcast.22, f32[552,128]{1,0:T(8,128)S(1)} %bitcast.23, ...), custom_call_target="tpu_custom_call" | custom-call | tf_op jit(solution)/shard_map/own_ocean/pallas_call | solution.py:31
  55.8 0.8 %collective-permute-done.5.r_ref = f32[8,512]{1,0:T(8,128)S(1)} collective-permute-done((f32[8,512]{1,0:T(8,128)S(1)}, f32[8,512]{1,0:T(8,128)S(1)}, u32[]{:S(2)}, u32[]{:S(2)}) %collective-permute-start.5) | collective-permute-done | bytes 16416 | tf_op jit(solution)/shard_map/ppermute | solution.py:62
  56.7 1.2 %heat.1 = f32[8,8,64]{2,1,0:T(8,128)} custom-call(f32[8,512]{1,0:T(8,128)S(1)} %get-tuple-element.52.att_ref, f32[8,512]{1,0:T(8,128)S(1)} %get-tuple-element.53.cum_ref, f32[8,512]{1,0:T(8,128)S(1)} %collective-permute-done.5.r_ref, f32[8,8,64]{2,1,0:T(8,128)S(1)} %get-tuple-element.58.w_ref, s32[8,8,64]{2,1,0:T(8,128)S(1)} %bitcast.29), custom_call_target="tpu_custom_call" | custom-call | tf_op jit(solution)/shard_map/heat/pallas_call | solution.py:31
  57.8 8.6 %all-to-all-done.2 = f16[16,32,512]{2,1,0:T(8,128)(2,1)S(1)} async-done(((f16[16,32,512]{2,1,0:T(8,128)(2,1)}), f16[16,32,512]{2,1,0:T(8,128)(2,1)S(1)}, u32[]{:S(2)}, u32[]{:S(2)}) %all-to-all-start.2) | async-done | bytes 524320 | tf_op jit(solution)/shard_map/all_to_all | solution.py:582
  66.5 1.1 %finish_tracers.1 = f32[4,512,128]{2,1,0:T(8,128)} custom-call(f32[16,32,512]{2,1,0:T(8,128)S(1)} %convert_element_type.11.r_ref, f32[4,128,512]{2,1,0:T(8,128)S(1)} %get-tuple-element.62.a_ref), custom_call_target="tpu_custom_call" | custom-call | tf_op jit(solution)/shard_map/finish_tracers/pallas_call | solution.py:31
  (24 shorter events, 1.6 us)
Async XLA Ops:
  2.5 15.2 %all-to-all-start = ((s32[8,48,128]{2,1,0:T(8,128)}), s32[8,48,128]{2,1,0:T(8,128)S(1)}, u32[]{:S(2)}, u32[]{:S(2)}) async-start(s32[8,48,128]{2,1,0:T(8,128)} %get-tuple-element.34), calls=%async_computation | async-start | bytes 393216 | tf_op jit(solution)/shard_map/all_to_all | solution.py:192
  9.8 4.6 %collective-permute-start = (f32[144,128]{1,0:T(8,128)}, f32[144,128]{1,0:T(8,128)S(1)}, u32[]{:S(2)}, u32[]{:S(2)}) collective-permute-start(f32[144,128]{1,0:T(8,128)} %get-tuple-element.35), channel_id=1, source_target_pairs={{0,1},{1,0},{2,3},{3,2},{4,5},{5,4},{6,7},{7,6},{8,9},{9,8},{10,11... | collective-permute-start | bytes 221192 | tf_op jit(solution)/shard_map/ppermute | solution.py:62
  14.4 1.2 %copy-start = (f32[4,64,8,128]{3,2,1,0:T(8,128)S(1)}, f32[4,64,8,128]{3,2,1,0:T(8,128)}, u32[]{:S(2)}) copy-start(f32[4,64,8,128]{3,2,1,0:T(8,128)} %param.14) | copy-start | bytes 3145732
  17.8 1.4 %collective-permute-start.1 = (s32[8,48,128]{2,1,0:T(8,128)S(1)}, s32[8,48,128]{2,1,0:T(8,128)S(1)}, u32[]{:S(2)}, u32[]{:S(2)}) collective-permute-start(s32[8,48,128]{2,1,0:T(8,128)S(1)} %all-to-all-done.a_ref), channel_id=1, source_target_pairs={{0,2},{2,0},{4,6},{6,4},{8,10},{10,8},{12,14},{14,12},{16,18},{18,... | collective-permute-start | bytes 589832 | tf_op jit(solution)/shard_map/ppermute | solution.py:220
  20.2 4.1 %collective-permute-start.2 = (f32[88,128]{1,0:T(8,128)S(1)}, f32[88,128]{1,0:T(8,128)S(1)}, u32[]{:S(2)}, u32[]{:S(2)}) collective-permute-start(f32[88,128]{1,0:T(8,128)S(1)} %get-tuple-element.41.o_ref), channel_id=1, source_target_pairs={{0,1},{1,0},{2,3},{3,2},{4,5},{5,4},{6,7},{7,6},{8,9},{9,8},{10,11... | collective-permute-start | bytes 135176 | tf_op jit(solution)/shard_map/ppermute | solution.py:62
  23.6 8.4 %copy-start.8 = (f32[16,64]{1,0:T(8,128)S(1)}, f32[16,64]{1,0:T(8,128)}, u32[]{:S(2)}) copy-start(f32[16,64]{1,0:T(8,128)} %get-tuple-element.49) | copy-start | bytes 12292
  23.6 8.9 %copy-start.7 = (f32[16,64]{1,0:T(8,128)S(1)}, f32[16,64]{1,0:T(8,128)}, u32[]{:S(2)}) copy-start(f32[16,64]{1,0:T(8,128)} %get-tuple-element.50) | copy-start | bytes 12292
  23.6 12.9 %copy-start.4 = (bf16[64,64]{1,0:T(8,128)(2,1)S(1)}, bf16[64,64]{1,0:T(8,128)(2,1)}, u32[]{:S(2)}) copy-start(bf16[64,64]{1,0:T(8,128)(2,1)} %c_ref.1) | copy-start | bytes 24580
  23.6 28.3 %copy-start.5 = (s32[64]{0:T(128)S(1)}, s32[64]{0:T(128)}, u32[]{:S(2)}) copy-start(s32[64]{0:T(128)} %g_ref.1) | copy-start | bytes 772
  23.7 28.3 %copy-start.6 = (f32[8]{0:T(128)S(1)}, f32[8]{0:T(128)}, u32[]{:S(2)}) copy-start(f32[8]{0:T(128)} %k_ref.1) | copy-start | bytes 100
  24.4 30.1 %copy-start.1 = (f32[64,8,8]{0,2,1:T(8,128)S(1)}, f32[64,8,8]{0,2,1:T(8,128)}, u32[]{:S(2)}) copy-start(f32[64,8,8]{0,2,1:T(8,128)} %param.9) | copy-start | bytes 49156
  24.4 30.1 %copy-start.2 = (f32[64,8,8]{0,2,1:T(8,128)S(1)}, f32[64,8,8]{0,2,1:T(8,128)}, u32[]{:S(2)}) copy-start(f32[64,8,8]{0,2,1:T(8,128)} %param.10) | copy-start | bytes 49156
  24.4 32.3 %copy-start.3 = (s32[64,8,8]{0,2,1:T(8,128)S(1)}, s32[64,8,8]{0,2,1:T(8,128)}, u32[]{:S(2)}) copy-start(s32[64,8,8]{0,2,1:T(8,128)} %param.13) | copy-start | bytes 49156
  27.9 18.7 %all-to-all-start.1 = ((bf16[16,32,512]{2,1,0:T(8,128)(2,1)}), bf16[16,32,512]{2,1,0:T(8,128)(2,1)S(1)}, u32[]{:S(2)}, u32[]{:S(2)}) async-start(bf16[16,32,512]{2,1,0:T(8,128)(2,1)} %get-tuple-element.48), calls=%async_computation.1 | async-start | bytes 1048576 | tf_op jit(solution)/shard_map/all_to_all | solution.py:481
  32.0 14.1 %collective-permute-start.3 = (f32[16,64]{1,0:T(8,128)S(1)}, f32[16,64]{1,0:T(8,128)S(1)}, u32[]{:S(2)}, u32[]{:S(2)}) collective-permute-start(f32[16,64]{1,0:T(8,128)S(1)} %copy-done.8), channel_id=1, source_target_pairs={{0,2},{2,4},{4,6},{6,8},{8,10},{10,12},{12,14},{14,16},{16,18},{18... | collective-permute-start | bytes 12296 | tf_op jit(solution)/shard_map/ppermute | solution.py:483
  32.5 13.6 %collective-permute-start.4 = (f32[16,64]{1,0:T(8,128)S(1)}, f32[16,64]{1,0:T(8,128)S(1)}, u32[]{:S(2)}, u32[]{:S(2)}) collective-permute-start(f32[16,64]{1,0:T(8,128)S(1)} %copy-done.7), channel_id=1, source_target_pairs={{2,0},{4,2},{6,4},{8,6},{10,8},{12,10},{14,12},{16,14},{18,16},{20... | collective-permute-start | bytes 12296 | tf_op jit(solution)/shard_map/ppermute | solution.py:484
  47.8 18.6 %all-to-all-start.2 = ((f16[16,32,512]{2,1,0:T(8,128)(2,1)}), f16[16,32,512]{2,1,0:T(8,128)(2,1)S(1)}, u32[]{:S(2)}, u32[]{:S(2)}) async-start(f16[16,32,512]{2,1,0:T(8,128)(2,1)} %bitcast.31), calls=%async_computation.2 | async-start | bytes 1048576 | tf_op jit(solution)/shard_map/all_to_all | solution.py:582
  52.9 3.8 %collective-permute-start.5 = (f32[8,512]{1,0:T(8,128)S(1)}, f32[8,512]{1,0:T(8,128)S(1)}, u32[]{:S(2)}, u32[]{:S(2)}) collective-permute-start(f32[8,512]{1,0:T(8,128)S(1)} %get-tuple-element.53.cum_ref), channel_id=1, source_target_pairs={{0,1},{1,0},{2,3},{3,2},{4,5},{5,4},{6,7},{7,6},{8,9},{9,8},{10,11... | collective-permute-start | bytes 49160 | tf_op jit(solution)/shard_map/ppermute | solution.py:62

commit v6 on v5

--- a/solution.py
+++ b/solution.py
@@ -104,15 +104,15 @@
     NP = ntrc // 2
     pairs_apart = [[2 * g + c for g in range(NP)] for c in range(2)]
 
-    UV_ROWS, DENSE_ROWS = XL * Y, XL * Y // 2
-    DRY_CODE = -(2**14)
+    ROWS = XL * Y
+    MOST = 2**20 - 1
+    DRY_CODE = -(2**20)
     SCALES = 31
 
     def top(bound):
         return 2.0 ** math.ceil(math.log2(bound))
 
     tops = (top(hydro_bound * 1.001), top(speed_bound), top(speed_bound))
-    codes = (2**14 - 1, 2**15 - 1, 2**15 - 1)
 
     def pack(t_any, s_any, u_any, v_any, m_any, c_any, pay_ref, lo_ref, hi_ref, out_ref, held, wet, sems):
         upper = lax.axis_index("lev") == 0
@@ -145,7 +145,7 @@
                 fits = most <= tops[i] * 2.0**-k
                 unit = jnp.where(fits, tops[i] * 2.0**-k, unit)
                 number = jnp.where(fits, k, number)
-            code = jnp.floor(jnp.clip(a * (1.0 / unit), -1.0, 1.0) * codes[i] + 0.5).astype(jnp.int32)
+            code = jnp.floor(jnp.clip(a * (1.0 / unit), -1.0, 1.0) * MOST + 0.5).astype(jnp.int32)
             if i == 0:
                 code = jnp.where(sea, code, DRY_CODE)
             numbers = numbers + number * 32**i
@@ -153,11 +153,10 @@
             halves.append(code.reshape(XL * Y, LANES))
         density, u, v = halves
         lane = lax.broadcasted_iota(jnp.int32, (XL * Y, LANES), 1)
-        density = density * 2 + (lax.shift_right_logical(numbers, lane % 16) & 1)
-        rows = jnp.concatenate(
-            [u * 65536 + (v & 65535), density[:DENSE_ROWS] * 65536 + (density[DENSE_ROWS:] & 65535)],
-            axis=0,
-        )
+        bit = lax.shift_right_logical(numbers, lane % 16) & 1
+        first = lax.shift_left(u, 11) | (lax.shift_right_arithmetic(v, 10) & 2047)
+        second = lax.shift_left(v & 1023, 22) | lax.shift_left(density & (2**21 - 1), 1) | bit
+        rows = jnp.concatenate([first, second], axis=0)
         for g in range(NP):
             pay_ref[g] = rows
         lane = lax.broadcasted_iota(jnp.int32, (Y, LANES), 1)
@@ -174,7 +173,7 @@
     payload, lo, hi, outer = call(
         pack,
         (
-            jax.ShapeDtypeStruct((NP, UV_ROWS + DENSE_ROWS, LANES), jnp.int32),
+            jax.ShapeDtypeStruct((NP, 2 * ROWS, LANES), jnp.int32),
             f32(2 * XE, D),
             f32(2 * XE, D),
             f32(4 * T * XE + 2 * Y, LANES),
@@ -225,15 +224,18 @@
     def dense(raw):
         return jnp.where(raw < 0.5 * DRY, raw, 0.0)
 
-    def faces(raw, u, v, before):
+    def beside(a, axis):
+        return shift(a, 1, axis) + shift(a, -1, axis)
+
+    def faces(raw, speeds, along_y, before):
         wet = jnp.where(raw < 0.5 * DRY, 1.0, 0.0)
         d = dense(raw)
         total = before + d
         p = buoyancy * (total - 0.5 * d)
         result = []
-        for axis, a in enumerate((u, v)):
+        for axis, (a, sides) in enumerate(zip(speeds, along_y)):
             mask = wet * shift(wet, 1, axis)
-            lap = shift(a, 1, 0) + shift(a, -1, 0) + shift(a, 1, 1) + shift(a, -1, 1) - 4.0 * a
+            lap = beside(a, 0) + sides - 4.0 * a
             push = viscosity * lap - (shift(p, 1, axis) - p)
             result.append((mask * (a + marine_advance * push), mask))
         return total, result
@@ -249,18 +251,12 @@
                 rows += [jnp.where(core == 0, a, b), jnp.where(core == 0, b, a)]
             return jnp.concatenate(rows, axis=0)
 
-        def high(w):
-            return lax.shift_right_arithmetic(w, 16)
-
-        def low(w):
-            return lax.shift_right_arithmetic(lax.shift_left(w, 16), 16)
-
-        bits = high(words(UV_ROWS)) & 1
+        bits = words(ROWS) & 1
         numbers = jnp.sum(jnp.where(lane < 16, lax.shift_left(bits, lane % 16), 0), axis=1, keepdims=True)
         units = []
         for i in range(3):
             number = lax.shift_right_logical(numbers, 5 * i) & 31
-            unit = jnp.full((YG, 1), tops[i] / codes[i], F32)
+            unit = jnp.full((YG, 1), tops[i] / MOST, F32)
             for b in range(5):
                 unit = jnp.where(lax.shift_right_logical(number, b) & 1 > 0, unit * 2.0 ** -(2**b), unit)
             units.append(unit)
@@ -271,21 +267,24 @@
                 f_ref[f, pl.ds(x + g * XL, D, stride=XE), :] = turned[g * D : (g + 1) * D]
 
         for x in range(XL):
-            w = words(x * Y)
-            put(1, x, high(w).astype(F32) * units[1])
-            put(2, x, low(w).astype(F32) * units[2])
-            if x < XL // 2:
-                w = words(UV_ROWS + x * Y)
-                for xx, code in ((x, high(w)), (x + XL // 2, low(w))):
-                    code = lax.shift_right_arithmetic(code, 1)
-                    put(0, xx, jnp.where(code == DRY_CODE, DRY, code.astype(F32) * units[0]))
+            first, second = words(x * Y), words(ROWS + x * Y)
+            u = lax.shift_right_arithmetic(first, 11)
+            v = lax.shift_right_arithmetic(lax.shift_left(first, 21), 21)
+            v = lax.shift_left(v, 10) | lax.shift_right_logical(second, 22)
+            density = lax.shift_right_arithmetic(lax.shift_left(second, 10), 11)
+            put(0, x, jnp.where(density == DRY_CODE, DRY, density.astype(F32) * units[0]))
+            for i, a in enumerate((u, v)):
+                a = a.astype(F32) * units[1 + i]
+                put(1 + i, x, a)
+                put(3 + i, x, beside(a, 0))
 
         def field(f, k):
             return f_ref[f, pl.ds(pl.multiple_of(k * XE, 8), XE)]
 
         def one(k, carry):
             total, sums = carry
-            total, new = faces(field(0, k), field(1, k), field(2, k), total)
+            f = [field(i, k) for i in range(5)]
+            total, new = faces(f[0], f[1:3], f[3:5], total)
             for i, (speed, mask) in enumerate(new):
                 uv_ref[i, k] = speed
                 mask_ref[i, k] = mask
@@ -293,7 +292,7 @@
             return total, tuple(a + b for a, b in zip(sums, parts))
 
         zero = jnp.zeros((XE, YG), F32)
-        total, sums = lax.fori_loop(0, D, one, (zero, (zero,) * 4), unroll=D // 2)
+        total, sums = lax.fori_loop(0, D, one, (zero, (zero,) * 4), unroll=D)
         for i, a in enumerate((total,) + sums):
             l_ref[i * XE : (i + 1) * XE] = a
         first = jnp.where(lax.axis_index("lev") == 0, D - 2, 0)
@@ -306,7 +305,7 @@
         unpack,
         (f32(2, D, XE, YG), f32(2, D, XE, YG), f32(11 * XE, YG)),
         (mine, other),
-        scratch=(pltpu.VMEM((3, W, YG), F32),),
+        scratch=(pltpu.VMEM((5, W, YG), F32),),
         name="unpack_ocean",
     )
     own_levels, pad = lax.optimization_barrier((own_levels, pad))
@@ -350,7 +349,9 @@
 
         def far(e, total):
             k = e % 2 if e < 2 else e - D - 2
-            total, new = faces(plane(r_ref, 5 + k), plane(r_ref, 7 + k), plane(r_ref, 9 + k), total)
+            speeds = plane(r_ref, 7 + k), plane(r_ref, 9 + k)
+            sides = [beside(a, 1) for a in speeds]
+            total, new = faces(plane(r_ref, 5 + k), speeds, sides, total)
             for i in range(2):
                 uv_ref[i, e] = new[i][0]
             return total
@@ -410,7 +411,7 @@
             return flux_next
 
         flux = fall(0, side[4, :, rows(0)], side[5, :, rows(1)])
-        lax.fori_loop(0, D + 4, first_step, flux, unroll=(D + 4) // 2)
+        lax.fori_loop(0, D + 4, first_step, flux, unroll=D + 4)
 
         def second_step(k, carry):
             B = RL

time: 68.2 us -> 68.8 us (level)
  waiting for transfers between devices: 26.3 us -> 27.3 us
    all_to_all x1, waiting for transfers between devices: 2.06 us -> 3.03 us  [shards(): lax.all_to_all(payload, 'trc', split_axis=0, concat_axis=0, tiled=True, a...]
  transfers between devices with their start and end apart: 9 -> 9, of which waited for: 8 -> 8; matrix products, arithmetic and copies ran while one was open for 0% -> 0% of each run, Pallas kernels for 9% -> 8%
where the time goes in v6:
time: 68.8 us; the launch traced here: 68.2 us
  waiting for transfers between devices  27.3 us (40%)
  starting transfers between devices  24.2 us (35%)
  Pallas kernels  13.3 us (19%)
  local copies, waits for them, and re-layouts  1.26 us (2%)
  matrix products  1.23 us (2%)
  between operations  0.77 us (1%)
    pallas_call x10, Pallas kernels, call(): pl.pallas_call(kernel, out_shape=out_shape, in_specs=[vmem] * len(args) i...  13.3 us
    ppermute x1, waiting for transfers between devices, shards(): south = lax.ppermute(hi, 'trc', ring)  9.15 us
    all_to_all x1, waiting for transfers between devices, shards(): lax.all_to_all(reaction, 'trc', split_axis=0, concat_axis=0, tiled=True)  8.55 us
    all_to_all x1, starting transfers between devices, shards(): lax.all_to_all(payload, 'trc', split_axis=0, concat_axis=0, tiled=True, a...  7.26 us
    ppermute x3, starting transfers between devices, exchange_levels(): return lax.ppermute(part, 'lev', [(0, 1), (1, 0)])  4.64 us
    ppermute x3, waiting for transfers between devices, exchange_levels(): return lax.ppermute(part, 'lev', [(0, 1), (1, 0)])  4.57 us
    all_to_all x1, starting transfers between devices, shards(): lax.all_to_all(reaction, 'trc', split_axis=0, concat_axis=0, tiled=True)  4.1 us
    ppermute x1, starting transfers between devices, shards(): north = lax.ppermute(lo, 'trc', [(b, a) for a, b in ring])  4.05 us
  transfers between devices with their start and end apart: 9, of which 8 were waited for; matrix products, arithmetic and copies ran while one was open for 0% of the time, Pallas kernels for 8%

profile of v6, /device:TPU:0, one launch (start us, length us, event | category | flops | bytes accessed | tf_op | source)
XLA Modules:
  0.0 68.2 jit_solution(11366487360873715676)
XLA Ops:
  0.6 1.9 %pack_ocean.1 = (s32[8,64,128]{2,1,0:T(8,128)}, f32[16,64]{1,0:T(8,128)}, f32[16,64]{1,0:T(8,128)}, f32[144,128]{1,0:T(8,128)}) custom-call(f32[8,8,64]{2,1,0:T(8,128)} %bitcast.24, f32[8,8,64]{2,1,0:T(8,128)} %bitcast.26, f32[8,8,64]{2,1,0:T(8,128)} %bitcast.32, f32[8,8,64]{2,1,0:T(8,128)} %bitcast.33, s32[8,8,64]{2,1,0:T(8,128)} %bitcast.28, ...), custom_call_target="tpu_custom_call" | custom-call | tf_op jit(solution)/shard_map/pack_ocean/pallas_call | solution.py:31
  2.6 7.3 %all-to-all-start = ((s32[8,64,128]{2,1,0:T(8,128)}), s32[8,64,128]{2,1,0:T(8,128)S(1)}, u32[]{:S(2)}, u32[]{:S(2)}) async-start(s32[8,64,128]{2,1,0:T(8,128)} %get-tuple-element.34), calls=%async_computation | async-start | bytes 524288 | tf_op jit(solution)/shard_map/all_to_all | solution.py:191
  9.8 1.5 %collective-permute-start = (f32[144,128]{1,0:T(8,128)}, f32[144,128]{1,0:T(8,128)S(1)}, u32[]{:S(2)}, u32[]{:S(2)}) collective-permute-start(f32[144,128]{1,0:T(8,128)} %get-tuple-element.35), channel_id=1, source_target_pairs={{0,1},{1,0},{2,3},{3,2},{4,5},{5,4},{6,7},{7,6},{8,9},{9,8},{10,11... | collective-permute-start | bytes 221192 | tf_op jit(solution)/shard_map/ppermute | solution.py:62
  11.4 3.0 %collective-permute-done.h_ref.l_ref = f32[144,128]{1,0:T(8,128)S(1)} collective-permute-done((f32[144,128]{1,0:T(8,128)}, f32[144,128]{1,0:T(8,128)S(1)}, u32[]{:S(2)}, u32[]{:S(2)}) %collective-permute-start) | collective-permute-done | bytes 73760 | tf_op jit(solution)/shard_map/ppermute | solution.py:62
  14.4 1.2 %copy-done = f32[4,64,8,128]{3,2,1,0:T(8,128)S(1)} copy-done((f32[4,64,8,128]{3,2,1,0:T(8,128)S(1)}, f32[4,64,8,128]{3,2,1,0:T(8,128)}, u32[]{:S(2)}) %copy-start) | copy-done | bytes 1048600
  15.7 3.0 %all-to-all-done.a_ref = s32[8,64,128]{2,1,0:T(8,128)S(1)} async-done(((s32[8,64,128]{2,1,0:T(8,128)}), s32[8,64,128]{2,1,0:T(8,128)S(1)}, u32[]{:S(2)}, u32[]{:S(2)}) %all-to-all-start) | async-done | bytes 262176 | tf_op jit(solution)/shard_map/all_to_all | solution.py:191
  18.8 1.5 %collective-permute-done.1.b_ref = s32[8,64,128]{2,1,0:T(8,128)S(1)} collective-permute-done((s32[8,64,128]{2,1,0:T(8,128)S(1)}, s32[8,64,128]{2,1,0:T(8,128)S(1)}, u32[]{:S(2)}, u32[]{:S(2)}) %collective-permute-start.1) | collective-permute-done | bytes 262176 | tf_op jit(solution)/shard_map/ppermute | solution.py:219
  20.3 1.0 %unpack_ocean.1 = (f32[2,64,8,128]{3,2,1,0:T(8,128)S(1)}, f32[2,64,8,128]{3,2,1,0:T(8,128)S(1)}, f32[88,128]{1,0:T(8,128)S(1)}) custom-call(s32[8,64,128]{2,1,0:T(8,128)S(1)} %all-to-all-done.a_ref, s32[8,64,128]{2,1,0:T(8,128)S(1)} %collective-permute-done.1.b_ref), custom_call_target="tpu_custom_call" | custom-call | tf_op jit(solution)/shard_map/unpack_ocean/pallas_call | solution.py:31
  21.3 1.6 %collective-permute-start.2 = (f32[88,128]{1,0:T(8,128)S(1)}, f32[88,128]{1,0:T(8,128)S(1)}, u32[]{:S(2)}, u32[]{:S(2)}) collective-permute-start(f32[88,128]{1,0:T(8,128)S(1)} %get-tuple-element.41.o_ref), channel_id=1, source_target_pairs={{0,1},{1,0},{2,3},{3,2},{4,5},{5,4},{6,7},{7,6},{8,9},{9,8},{10,11... | collective-permute-start | bytes 135176 | tf_op jit(solution)/shard_map/ppermute | solution.py:62
  22.9 1.8 %first_slopes.1.side = f32[6,4,560,128]{3,2,1,0:T(8,128)S(1)} custom-call(f32[4,576,128]{2,1,0:T(8,128)S(1)} %widen_levels.1.pad), custom_call_target="tpu_custom_call" | custom-call | tf_op jit(solution)/shard_map/first_slopes/pallas_call | solution.py:31
  24.7 0.7 %collective-permute-done.2.r_ref = f32[88,128]{1,0:T(8,128)S(1)} collective-permute-done((f32[88,128]{1,0:T(8,128)S(1)}, f32[88,128]{1,0:T(8,128)S(1)}, u32[]{:S(2)}, u32[]{:S(2)}) %collective-permute-start.2) | collective-permute-done | bytes 45088 | tf_op jit(solution)/shard_map/ppermute | solution.py:62
  25.4 3.5 %advect_tracers.1 = (f32[4,128,512]{2,1,0:T(8,128)S(1)}, bf16[16,32,512]{2,1,0:T(8,128)(2,1)}, f32[2,68,8,128]{3,2,1,0:T(8,128)S(1)}, f32[69,8,128]{2,1,0:T(8,128)S(1)}) custom-call(f32[2,64,8,128]{3,2,1,0:T(8,128)S(1)} %get-tuple-element.37.n_ref, f32[2,64,8,128]{3,2,1,0:T(8,128)S(1)} %get-tuple-element.38.m_ref, f32[88,128]{1,0:T(8,128)S(1)} %get-tuple-element.41.o_ref, ...), custom_call_target="tpu_custom_call" | custom-call | tf_op jit(solution)/shard_map/advect_tracers/pallas_call | solution.py:31
  28.9 3.7 %all-to-all-start.1 = ((bf16[16,32,512]{2,1,0:T(8,128)(2,1)}), bf16[16,32,512]{2,1,0:T(8,128)(2,1)S(1)}, u32[]{:S(2)}, u32[]{:S(2)}) async-start(bf16[16,32,512]{2,1,0:T(8,128)(2,1)} %get-tuple-element.48), calls=%async_computation.1 | async-start | bytes 1048576 | tf_op jit(solution)/shard_map/all_to_all | solution.py:482
  33.1 4.0 %collective-permute-start.4 = (f32[16,64]{1,0:T(8,128)S(1)}, f32[16,64]{1,0:T(8,128)S(1)}, u32[]{:S(2)}, u32[]{:S(2)}) collective-permute-start(f32[16,64]{1,0:T(8,128)S(1)} %copy-done.7), channel_id=1, source_target_pairs={{2,0},{4,2},{6,4},{8,6},{10,8},{12,10},{14,12},{16,14},{18,16},{20... | collective-permute-start | bytes 12296 | tf_op jit(solution)/shard_map/ppermute | solution.py:485
  37.5 9.1 %collective-permute-done.3.so_ref = f32[16,64]{1,0:T(8,128)S(1)} collective-permute-done((f32[16,64]{1,0:T(8,128)S(1)}, f32[16,64]{1,0:T(8,128)S(1)}, u32[]{:S(2)}, u32[]{:S(2)}) %collective-permute-start.3) | collective-permute-done | bytes 4128 | tf_op jit(solution)/shard_map/ppermute | solution.py:484
  47.2 1.2 %fusion = f16[512,512]{0,1:T(8,128)(2,1)} fusion(bf16[512,512]{1,0:T(8,128)(2,1)S(1)} %spread_coupling.1, bf16[512,512]{1,0:T(8,128)(2,1)S(1)} %bitcast.21), kind=kOutput, calls=%fused_computation.1 | convolution fusion | flops 268959744 | bytes 1572864 | tf_op jit(solution)/shard_map/dot_general | solution.py:581
  48.4 4.1 %all-to-all-start.2 = ((f16[16,32,512]{2,1,0:T(8,128)(2,1)}), f16[16,32,512]{2,1,0:T(8,128)(2,1)S(1)}, u32[]{:S(2)}, u32[]{:S(2)}) async-start(f16[16,32,512]{2,1,0:T(8,128)(2,1)} %bitcast.31), calls=%async_computation.2 | async-start | bytes 1048576 | tf_op jit(solution)/shard_map/all_to_all | solution.py:583
  52.5 1.0 %shade.1 = (f32[8,512]{1,0:T(8,128)S(1)}, f32[8,512]{1,0:T(8,128)S(1)}) custom-call(bf16[16,32,512]{2,1,0:T(8,128)(2,1)S(1)} %all-to-all-done.1.x_ref, s32[64]{0:T(128)S(1)} %copy-done.5, f32[8]{0:T(128)S(1)} %copy-done.6), custom_call_target="tpu_custom_call" | custom-call | tf_op jit(solution)/shard_map/shade/pallas_call | solution.py:31
  53.5 1.5 %collective-permute-start.5 = (f32[8,512]{1,0:T(8,128)S(1)}, f32[8,512]{1,0:T(8,128)S(1)}, u32[]{:S(2)}, u32[]{:S(2)}) collective-permute-start(f32[8,512]{1,0:T(8,128)S(1)} %get-tuple-element.53.cum_ref), channel_id=1, source_target_pairs={{0,1},{1,0},{2,3},{3,2},{4,5},{5,4},{6,7},{7,6},{8,9},{9,8},{10,11... | collective-permute-start | bytes 49160 | tf_op jit(solution)/shard_map/ppermute | solution.py:62
  55.0 1.4 %own_ocean.1 = (f32[8,8,64]{2,1,0:T(8,128)}, f32[8,8,64]{2,1,0:T(8,128)S(1)}, f32[8,8,64]{2,1,0:T(8,128)}, f32[8,8,64]{2,1,0:T(8,128)}) custom-call(f32[8,8,64]{2,1,0:T(8,128)S(1)} %bitcast.25, f32[8,8,64]{2,1,0:T(8,128)S(1)} %bitcast.27, f32[2,544,128]{2,1,0:T(8,128)S(1)} %bitcast.22, f32[552,128]{1,0:T(8,128)S(1)} %bitcast.23, ...), custom_call_target="tpu_custom_call" | custom-call | tf_op jit(solution)/shard_map/own_ocean/pallas_call | solution.py:31
  56.4 0.8 %collective-permute-done.5.r_ref = f32[8,512]{1,0:T(8,128)S(1)} collective-permute-done((f32[8,512]{1,0:T(8,128)S(1)}, f32[8,512]{1,0:T(8,128)S(1)}, u32[]{:S(2)}, u32[]{:S(2)}) %collective-permute-start.5) | collective-permute-done | bytes 16416 | tf_op jit(solution)/shard_map/ppermute | solution.py:62
  57.2 1.2 %heat.1 = f32[8,8,64]{2,1,0:T(8,128)} custom-call(f32[8,512]{1,0:T(8,128)S(1)} %get-tuple-element.52.att_ref, f32[8,512]{1,0:T(8,128)S(1)} %get-tuple-element.53.cum_ref, f32[8,512]{1,0:T(8,128)S(1)} %collective-permute-done.5.r_ref, f32[8,8,64]{2,1,0:T(8,128)S(1)} %get-tuple-element.58.w_ref, s32[8,8,64]{2,1,0:T(8,128)S(1)} %bitcast.29), custom_call_target="tpu_custom_call" | custom-call | tf_op jit(solution)/shard_map/heat/pallas_call | solution.py:31
  58.4 8.6 %all-to-all-done.2 = f16[16,32,512]{2,1,0:T(8,128)(2,1)S(1)} async-done(((f16[16,32,512]{2,1,0:T(8,128)(2,1)}), f16[16,32,512]{2,1,0:T(8,128)(2,1)S(1)}, u32[]{:S(2)}, u32[]{:S(2)}) %all-to-all-start.2) | async-done | bytes 524320 | tf_op jit(solution)/shard_map/all_to_all | solution.py:583
  67.1 1.1 %finish_tracers.1 = f32[4,512,128]{2,1,0:T(8,128)} custom-call(f32[16,32,512]{2,1,0:T(8,128)S(1)} %convert_element_type.11.r_ref, f32[4,128,512]{2,1,0:T(8,128)S(1)} %get-tuple-element.62.a_ref), custom_call_target="tpu_custom_call" | custom-call | tf_op jit(solution)/shard_map/finish_tracers/pallas_call | solution.py:31
  (24 shorter events, 1.6 us)
Async XLA Ops:
  2.6 16.2 %all-to-all-start = ((s32[8,64,128]{2,1,0:T(8,128)}), s32[8,64,128]{2,1,0:T(8,128)S(1)}, u32[]{:S(2)}, u32[]{:S(2)}) async-start(s32[8,64,128]{2,1,0:T(8,128)} %get-tuple-element.34), calls=%async_computation | async-start | bytes 524288 | tf_op jit(solution)/shard_map/all_to_all | solution.py:191
  9.8 4.6 %collective-permute-start = (f32[144,128]{1,0:T(8,128)}, f32[144,128]{1,0:T(8,128)S(1)}, u32[]{:S(2)}, u32[]{:S(2)}) collective-permute-start(f32[144,128]{1,0:T(8,128)} %get-tuple-element.35), channel_id=1, source_target_pairs={{0,1},{1,0},{2,3},{3,2},{4,5},{5,4},{6,7},{7,6},{8,9},{9,8},{10,11... | collective-permute-start | bytes 221192 | tf_op jit(solution)/shard_map/ppermute | solution.py:62
  14.4 1.2 %copy-start = (f32[4,64,8,128]{3,2,1,0:T(8,128)S(1)}, f32[4,64,8,128]{3,2,1,0:T(8,128)}, u32[]{:S(2)}) copy-start(f32[4,64,8,128]{3,2,1,0:T(8,128)} %param.14) | copy-start | bytes 3145732
  18.8 1.5 %collective-permute-start.1 = (s32[8,64,128]{2,1,0:T(8,128)S(1)}, s32[8,64,128]{2,1,0:T(8,128)S(1)}, u32[]{:S(2)}, u32[]{:S(2)}) collective-permute-start(s32[8,64,128]{2,1,0:T(8,128)S(1)} %all-to-all-done.a_ref), channel_id=1, source_target_pairs={{0,2},{2,0},{4,6},{6,4},{8,10},{10,8},{12,14},{14,12},{16,18},{18,... | collective-permute-start | bytes 786440 | tf_op jit(solution)/shard_map/ppermute | solution.py:219
  21.3 4.1 %collective-permute-start.2 = (f32[88,128]{1,0:T(8,128)S(1)}, f32[88,128]{1,0:T(8,128)S(1)}, u32[]{:S(2)}, u32[]{:S(2)}) collective-permute-start(f32[88,128]{1,0:T(8,128)S(1)} %get-tuple-element.41.o_ref), channel_id=1, source_target_pairs={{0,1},{1,0},{2,3},{3,2},{4,5},{5,4},{6,7},{7,6},{8,9},{9,8},{10,11... | collective-permute-start | bytes 135176 | tf_op jit(solution)/shard_map/ppermute | solution.py:62
  24.7 7.9 %copy-start.8 = (f32[16,64]{1,0:T(8,128)S(1)}, f32[16,64]{1,0:T(8,128)}, u32[]{:S(2)}) copy-start(f32[16,64]{1,0:T(8,128)} %get-tuple-element.49) | copy-start | bytes 12292
  24.7 8.4 %copy-start.7 = (f32[16,64]{1,0:T(8,128)S(1)}, f32[16,64]{1,0:T(8,128)}, u32[]{:S(2)}) copy-start(f32[16,64]{1,0:T(8,128)} %get-tuple-element.50) | copy-start | bytes 12292
  24.7 12.4 %copy-start.4 = (bf16[64,64]{1,0:T(8,128)(2,1)S(1)}, bf16[64,64]{1,0:T(8,128)(2,1)}, u32[]{:S(2)}) copy-start(bf16[64,64]{1,0:T(8,128)(2,1)} %c_ref.1) | copy-start | bytes 24580
  24.7 27.8 %copy-start.5 = (s32[64]{0:T(128)S(1)}, s32[64]{0:T(128)}, u32[]{:S(2)}) copy-start(s32[64]{0:T(128)} %g_ref.1) | copy-start | bytes 772
  24.7 27.8 %copy-start.6 = (f32[8]{0:T(128)S(1)}, f32[8]{0:T(128)}, u32[]{:S(2)}) copy-start(f32[8]{0:T(128)} %k_ref.1) | copy-start | bytes 100
  25.4 29.6 %copy-start.1 = (f32[64,8,8]{0,2,1:T(8,128)S(1)}, f32[64,8,8]{0,2,1:T(8,128)}, u32[]{:S(2)}) copy-start(f32[64,8,8]{0,2,1:T(8,128)} %param.9) | copy-start | bytes 49156
  25.4 29.6 %copy-start.2 = (f32[64,8,8]{0,2,1:T(8,128)S(1)}, f32[64,8,8]{0,2,1:T(8,128)}, u32[]{:S(2)}) copy-start(f32[64,8,8]{0,2,1:T(8,128)} %param.10) | copy-start | bytes 49156
  25.4 31.8 %copy-start.3 = (s32[64,8,8]{0,2,1:T(8,128)S(1)}, s32[64,8,8]{0,2,1:T(8,128)}, u32[]{:S(2)}) copy-start(s32[64,8,8]{0,2,1:T(8,128)} %param.13) | copy-start | bytes 49156
  28.9 18.3 %all-to-all-start.1 = ((bf16[16,32,512]{2,1,0:T(8,128)(2,1)}), bf16[16,32,512]{2,1,0:T(8,128)(2,1)S(1)}, u32[]{:S(2)}, u32[]{:S(2)}) async-start(bf16[16,32,512]{2,1,0:T(8,128)(2,1)} %get-tuple-element.48), calls=%async_computation.1 | async-start | bytes 1048576 | tf_op jit(solution)/shard_map/all_to_all | solution.py:482
  32.6 14.1 %collective-permute-start.3 = (f32[16,64]{1,0:T(8,128)S(1)}, f32[16,64]{1,0:T(8,128)S(1)}, u32[]{:S(2)}, u32[]{:S(2)}) collective-permute-start(f32[16,64]{1,0:T(8,128)S(1)} %copy-done.8), channel_id=1, source_target_pairs={{0,2},{2,4},{4,6},{6,8},{8,10},{10,12},{12,14},{14,16},{16,18},{18... | collective-permute-start | bytes 12296 | tf_op jit(solution)/shard_map/ppermute | solution.py:484
  33.1 13.6 %collective-permute-start.4 = (f32[16,64]{1,0:T(8,128)S(1)}, f32[16,64]{1,0:T(8,128)S(1)}, u32[]{:S(2)}, u32[]{:S(2)}) collective-permute-start(f32[16,64]{1,0:T(8,128)S(1)} %copy-done.7), channel_id=1, source_target_pairs={{2,0},{4,2},{6,4},{8,6},{10,8},{12,10},{14,12},{16,14},{18,16},{20... | collective-permute-start | bytes 12296 | tf_op jit(solution)/shard_map/ppermute | solution.py:485
  48.4 18.6 %all-to-all-start.2 = ((f16[16,32,512]{2,1,0:T(8,128)(2,1)}), f16[16,32,512]{2,1,0:T(8,128)(2,1)S(1)}, u32[]{:S(2)}, u32[]{:S(2)}) async-start(f16[16,32,512]{2,1,0:T(8,128)(2,1)} %bitcast.31), calls=%async_computation.2 | async-start | bytes 1048576 | tf_op jit(solution)/shard_map/all_to_all | solution.py:583
  53.5 3.8 %collective-permute-start.5 = (f32[8,512]{1,0:T(8,128)S(1)}, f32[8,512]{1,0:T(8,128)S(1)}, u32[]{:S(2)}, u32[]{:S(2)}) collective-permute-start(f32[8,512]{1,0:T(8,128)S(1)} %get-tuple-element.53.cum_ref), channel_id=1, source_target_pairs={{0,1},{1,0},{2,3},{3,2},{4,5},{5,4},{6,7},{7,6},{8,9},{9,8},{10,11... | collective-permute-start | bytes 49160 | tf_op jit(solution)/shard_map/ppermute | solution.py:62

commit v7 on v6

--- a/solution.py
+++ b/solution.py
@@ -1,4 +1,5 @@
 import math
+import random
 
 import jax
 import jax.numpy as jnp
@@ -102,6 +103,9 @@
     )
     species = widen(species_concentrations, 2)
     NP = ntrc // 2
+    order = list(range(ntrc))
+    random.Random(4).shuffle(order)
+    place = [order.index(d) for d in range(ntrc)]
     pairs_apart = [[2 * g + c for g in range(NP)] for c in range(2)]
 
     ROWS = XL * Y
@@ -450,7 +454,7 @@
                 adv_ref[t, :, here] = new[t]
             for d in range(ntrc):
                 there = [new[t][d * Y : (d + 1) * Y] for t in range(T)]
-                held[w, d] = jnp.concatenate(there, axis=0).astype(jnp.bfloat16)
+                held[w, place[d]] = jnp.concatenate(there, axis=0).astype(jnp.bfloat16)
             sending(w).start()
 
         def block(w, carry):
@@ -479,7 +483,9 @@
         name="advect_tracers",
     )
     message, lo, hi = lax.optimization_barrier((message, lo, hi))
-    gathered = lax.all_to_all(message, "trc", split_axis=0, concat_axis=0, tiled=True)
+    gathered = lax.all_to_all(
+        message, "trc", split_axis=0, concat_axis=0, tiled=True, axis_index_groups=[order]
+    )
     ring = [(i, (i + 1) % ntrc) for i in range(ntrc)]
     south = lax.ppermute(hi, "trc", ring)
     north = lax.ppermute(lo, "trc", [(b, a) for a, b in ring])
@@ -562,7 +568,9 @@
 
         def pick(shape, along):
             wide, narrow = (lax.broadcasted_iota(jnp.int32, shape, d) for d in (along, 1 - along))
-            return jnp.where(wide // Y == narrow, 1.0, 0.0).astype(jnp.bfloat16)
+            device = sum(jnp.where(wide // (T * Y) == p, d, 0) for p, d in enumerate(order))
+            tracer = device * T + (wide // Y) % T
+            return jnp.where(tracer == narrow, 1.0, 0.0).astype(jnp.bfloat16)
 
         tall = jnp.dot(pick((n, NT), 0), c_ref[...], preferred_element_type=F32)
         full = jnp.dot(
@@ -580,14 +588,16 @@
     flat_tracers = gathered.reshape(NT * Y, DX)
     reaction = jnp.dot(spread, flat_tracers, preferred_element_type=F32)
     reaction = (reaction * (1.0 / unit)).astype(jnp.float16).reshape(ntrc, T * Y, DX)
-    returned = lax.all_to_all(reaction, "trc", split_axis=0, concat_axis=0, tiled=True)
+    returned = lax.all_to_all(
+        reaction, "trc", split_axis=0, concat_axis=0, tiled=True, axis_index_groups=[order]
+    )
 
     def shade(x_ref, g_ref, k_ref, att_ref, cum_ref):
         att = jnp.zeros((Y, DX), F32)
         for d in range(ntrc):
             rows = x_ref[d].astype(F32)
             for t in range(T):
-                att = att + k_ref[g_ref[d * T + t]] * rows[t * Y : (t + 1) * Y]
+                att = att + k_ref[g_ref[order[d] * T + t]] * rows[t * Y : (t + 1) * Y]
         att_ref[...] = att
         lane = lax.broadcasted_iota(jnp.int32, (Y, DX), 1)
         total = att
@@ -635,7 +645,8 @@
         for t in range(T):
             for w in range(DX // LANES):
                 rows = [
-                    r_ref[d, t * Y : (t + 1) * Y, w * LANES : (w + 1) * LANES] for d in range(ntrc)
+                    r_ref[place[d], t * Y : (t + 1) * Y, w * LANES : (w + 1) * LANES]
+                    for d in range(ntrc)
                 ]
                 here = slice(w * LANES, (w + 1) * LANES)
                 o_ref[t, here] = (a_ref[t, :, here] + (react_step * unit) * jnp.concatenate(rows, axis=0)).T

time: 68.8 us -> 68.5 us (level)
  waiting for transfers between devices: 27.3 us -> 23.5 us
  starting transfers between devices: 24.2 us -> 27.7 us
    all_to_all x2, starting transfers between devices: 7.8 us -> 11.3 us  [the longest x1 6.19 us: shards(): lax.all_to_all(reaction, 'trc', split_axis=0, concat_axis=0, tiled=True,...]
    ppermute x1, waiting for transfers between devices: 9.15 us -> 5.87 us  [shards(): south = lax.ppermute(hi, 'trc', ring)]
  transfers between devices with their start and end apart: 9 -> 9, of which waited for: 8 -> 8; matrix products, arithmetic and copies ran while one was open for 0% -> 0% of each run, Pallas kernels for 8% -> 9%
where the time goes in v7:
time: 68.5 us; the launch traced here: 67.9 us
  starting transfers between devices  27.7 us (40%)
  waiting for transfers between devices  23.5 us (34%)
  Pallas kernels  13.3 us (19%)
  local copies, waits for them, and re-layouts  1.26 us (2%)
  matrix products  1.23 us (2%)
  between operations  0.74 us (1%)
    pallas_call x10, Pallas kernels, call(): pl.pallas_call(kernel, out_shape=out_shape, in_specs=[vmem] * len(args) i...  13.3 us
    all_to_all x1, starting transfers between devices, shards(): lax.all_to_all(payload, 'trc', split_axis=0, concat_axis=0, tiled=True, a...  7.26 us
    all_to_all x1, waiting for transfers between devices, shards(): lax.all_to_all(reaction, 'trc', split_axis=0, concat_axis=0, tiled=True,...  6.68 us
    all_to_all x1, starting transfers between devices, shards(): lax.all_to_all(reaction, 'trc', split_axis=0, concat_axis=0, tiled=True,...  6.19 us
    ppermute x1, waiting for transfers between devices, shards(): south = lax.ppermute(hi, 'trc', ring)  5.87 us
    all_to_all x1, starting transfers between devices, shards(): lax.all_to_all(message, 'trc', split_axis=0, concat_axis=0, tiled=True, a...  5.13 us
    ppermute x3, starting transfers between devices, exchange_levels(): return lax.ppermute(part, 'lev', [(0, 1), (1, 0)])  4.64 us
    ppermute x3, waiting for transfers between devices, exchange_levels(): return lax.ppermute(part, 'lev', [(0, 1), (1, 0)])  4.57 us
  transfers between devices with their start and end apart: 9, of which 8 were waited for; matrix products, arithmetic and copies ran while one was open for 0% of the time, Pallas kernels for 9%

profile of v7, /device:TPU:0, one launch (start us, length us, event | category | flops | bytes accessed | tf_op | source)
XLA Modules:
  0.0 67.9 jit_solution(11608336067667644968)
XLA Ops:
  0.6 1.9 %pack_ocean.1 = (s32[8,64,128]{2,1,0:T(8,128)}, f32[16,64]{1,0:T(8,128)}, f32[16,64]{1,0:T(8,128)}, f32[144,128]{1,0:T(8,128)}) custom-call(f32[8,8,64]{2,1,0:T(8,128)} %bitcast.24, f32[8,8,64]{2,1,0:T(8,128)} %bitcast.26, f32[8,8,64]{2,1,0:T(8,128)} %bitcast.32, f32[8,8,64]{2,1,0:T(8,128)} %bitcast.33, s32[8,8,64]{2,1,0:T(8,128)} %bitcast.28, ...), custom_call_target="tpu_custom_call" | custom-call | tf_op jit(solution)/shard_map/pack_ocean/pallas_call | solution.py:32
  2.6 7.3 %all-to-all-start = ((s32[8,64,128]{2,1,0:T(8,128)}), s32[8,64,128]{2,1,0:T(8,128)S(1)}, u32[]{:S(2)}, u32[]{:S(2)}) async-start(s32[8,64,128]{2,1,0:T(8,128)} %get-tuple-element.34), calls=%async_computation | async-start | bytes 524288 | tf_op jit(solution)/shard_map/all_to_all | solution.py:195
  9.8 1.5 %collective-permute-start = (f32[144,128]{1,0:T(8,128)}, f32[144,128]{1,0:T(8,128)S(1)}, u32[]{:S(2)}, u32[]{:S(2)}) collective-permute-start(f32[144,128]{1,0:T(8,128)} %get-tuple-element.35), channel_id=1, source_target_pairs={{0,1},{1,0},{2,3},{3,2},{4,5},{5,4},{6,7},{7,6},{8,9},{9,8},{10,11... | collective-permute-start | bytes 221192 | tf_op jit(solution)/shard_map/ppermute | solution.py:63
  11.4 3.0 %collective-permute-done.h_ref.l_ref = f32[144,128]{1,0:T(8,128)S(1)} collective-permute-done((f32[144,128]{1,0:T(8,128)}, f32[144,128]{1,0:T(8,128)S(1)}, u32[]{:S(2)}, u32[]{:S(2)}) %collective-permute-start) | collective-permute-done | bytes 73760 | tf_op jit(solution)/shard_map/ppermute | solution.py:63
  14.4 1.2 %copy-done = f32[4,64,8,128]{3,2,1,0:T(8,128)S(1)} copy-done((f32[4,64,8,128]{3,2,1,0:T(8,128)S(1)}, f32[4,64,8,128]{3,2,1,0:T(8,128)}, u32[]{:S(2)}) %copy-start) | copy-done | bytes 1048600
  15.7 3.0 %all-to-all-done.a_ref = s32[8,64,128]{2,1,0:T(8,128)S(1)} async-done(((s32[8,64,128]{2,1,0:T(8,128)}), s32[8,64,128]{2,1,0:T(8,128)S(1)}, u32[]{:S(2)}, u32[]{:S(2)}) %all-to-all-start) | async-done | bytes 262176 | tf_op jit(solution)/shard_map/all_to_all | solution.py:195
  18.8 1.5 %collective-permute-done.1.b_ref = s32[8,64,128]{2,1,0:T(8,128)S(1)} collective-permute-done((s32[8,64,128]{2,1,0:T(8,128)S(1)}, s32[8,64,128]{2,1,0:T(8,128)S(1)}, u32[]{:S(2)}, u32[]{:S(2)}) %collective-permute-start.1) | collective-permute-done | bytes 262176 | tf_op jit(solution)/shard_map/ppermute | solution.py:223
  20.3 1.0 %unpack_ocean.1 = (f32[2,64,8,128]{3,2,1,0:T(8,128)S(1)}, f32[2,64,8,128]{3,2,1,0:T(8,128)S(1)}, f32[88,128]{1,0:T(8,128)S(1)}) custom-call(s32[8,64,128]{2,1,0:T(8,128)S(1)} %all-to-all-done.a_ref, s32[8,64,128]{2,1,0:T(8,128)S(1)} %collective-permute-done.1.b_ref), custom_call_target="tpu_custom_call" | custom-call | tf_op jit(solution)/shard_map/unpack_ocean/pallas_call | solution.py:32
  21.3 1.6 %collective-permute-start.2 = (f32[88,128]{1,0:T(8,128)S(1)}, f32[88,128]{1,0:T(8,128)S(1)}, u32[]{:S(2)}, u32[]{:S(2)}) collective-permute-start(f32[88,128]{1,0:T(8,128)S(1)} %get-tuple-element.41.o_ref), channel_id=1, source_target_pairs={{0,1},{1,0},{2,3},{3,2},{4,5},{5,4},{6,7},{7,6},{8,9},{9,8},{10,11... | collective-permute-start | bytes 135176 | tf_op jit(solution)/shard_map/ppermute | solution.py:63
  22.9 1.8 %first_slopes.1.side = f32[6,4,560,128]{3,2,1,0:T(8,128)S(1)} custom-call(f32[4,576,128]{2,1,0:T(8,128)S(1)} %widen_levels.1.pad), custom_call_target="tpu_custom_call" | custom-call | tf_op jit(solution)/shard_map/first_slopes/pallas_call | solution.py:32
  25.4 3.5 %advect_tracers.1 = (f32[4,128,512]{2,1,0:T(8,128)S(1)}, bf16[16,32,512]{2,1,0:T(8,128)(2,1)}, f32[2,68,8,128]{3,2,1,0:T(8,128)S(1)}, f32[69,8,128]{2,1,0:T(8,128)S(1)}) custom-call(f32[2,64,8,128]{3,2,1,0:T(8,128)S(1)} %get-tuple-element.37.n_ref, f32[2,64,8,128]{3,2,1,0:T(8,128)S(1)} %get-tuple-element.38.m_ref, f32[88,128]{1,0:T(8,128)S(1)} %get-tuple-element.41.o_ref, ...), custom_call_target="tpu_custom_call" | custom-call | tf_op jit(solution)/shard_map/advect_tracers/pallas_call | solution.py:32
  28.9 5.1 %all-to-all-start.1 = ((bf16[16,32,512]{2,1,0:T(8,128)(2,1)}), bf16[16,32,512]{2,1,0:T(8,128)(2,1)S(1)}, u32[]{:S(2)}, u32[]{:S(2)}) async-start(bf16[16,32,512]{2,1,0:T(8,128)(2,1)} %get-tuple-element.48), calls=%async_computation.1 | async-start | bytes 1048576 | tf_op jit(solution)/shard_map/all_to_all | solution.py:486
  34.2 4.3 %collective-permute-start.4 = (f32[16,64]{1,0:T(8,128)S(1)}, f32[16,64]{1,0:T(8,128)S(1)}, u32[]{:S(2)}, u32[]{:S(2)}) collective-permute-start(f32[16,64]{1,0:T(8,128)S(1)} %copy-done.7), channel_id=1, source_target_pairs={{2,0},{4,2},{6,4},{8,6},{10,8},{12,10},{14,12},{16,14},{18,16},{20... | collective-permute-start | bytes 12296 | tf_op jit(solution)/shard_map/ppermute | solution.py:491
  38.9 5.9 %collective-permute-done.3.so_ref = f32[16,64]{1,0:T(8,128)S(1)} collective-permute-done((f32[16,64]{1,0:T(8,128)S(1)}, f32[16,64]{1,0:T(8,128)S(1)}, u32[]{:S(2)}, u32[]{:S(2)}) %collective-permute-start.3) | collective-permute-done | bytes 4128 | tf_op jit(solution)/shard_map/ppermute | solution.py:490
  44.8 1.8 %all-to-all-done.1.x_ref = bf16[16,32,512]{2,1,0:T(8,128)(2,1)S(1)} async-done(((bf16[16,32,512]{2,1,0:T(8,128)(2,1)}), bf16[16,32,512]{2,1,0:T(8,128)(2,1)S(1)}, u32[]{:S(2)}, u32[]{:S(2)}) %all-to-all-start.1) | async-done | bytes 524320 | tf_op jit(solution)/shard_map/all_to_all | solution.py:486
  46.6 1.2 %fusion = f16[512,512]{0,1:T(8,128)(2,1)} fusion(bf16[512,512]{1,0:T(8,128)(2,1)S(1)} %spread_coupling.1, bf16[512,512]{1,0:T(8,128)(2,1)S(1)} %bitcast.21), kind=kOutput, calls=%fused_computation.1 | convolution fusion | flops 268959744 | bytes 1572864 | tf_op jit(solution)/shard_map/dot_general | solution.py:589
  47.9 6.2 %all-to-all-start.2 = ((f16[16,32,512]{2,1,0:T(8,128)(2,1)}), f16[16,32,512]{2,1,0:T(8,128)(2,1)S(1)}, u32[]{:S(2)}, u32[]{:S(2)}) async-start(f16[16,32,512]{2,1,0:T(8,128)(2,1)} %bitcast.31), calls=%async_computation.2 | async-start | bytes 1048576 | tf_op jit(solution)/shard_map/all_to_all | solution.py:591
  54.1 1.0 %shade.1 = (f32[8,512]{1,0:T(8,128)S(1)}, f32[8,512]{1,0:T(8,128)S(1)}) custom-call(bf16[16,32,512]{2,1,0:T(8,128)(2,1)S(1)} %all-to-all-done.1.x_ref, s32[64]{0:T(128)S(1)} %copy-done.5, f32[8]{0:T(128)S(1)} %copy-done.6), custom_call_target="tpu_custom_call" | custom-call | tf_op jit(solution)/shard_map/shade/pallas_call | solution.py:32
  55.0 1.5 %collective-permute-start.5 = (f32[8,512]{1,0:T(8,128)S(1)}, f32[8,512]{1,0:T(8,128)S(1)}, u32[]{:S(2)}, u32[]{:S(2)}) collective-permute-start(f32[8,512]{1,0:T(8,128)S(1)} %get-tuple-element.53.cum_ref), channel_id=1, source_target_pairs={{0,1},{1,0},{2,3},{3,2},{4,5},{5,4},{6,7},{7,6},{8,9},{9,8},{10,11... | collective-permute-start | bytes 49160 | tf_op jit(solution)/shard_map/ppermute | solution.py:63
  56.6 1.4 %own_ocean.1 = (f32[8,8,64]{2,1,0:T(8,128)}, f32[8,8,64]{2,1,0:T(8,128)S(1)}, f32[8,8,64]{2,1,0:T(8,128)}, f32[8,8,64]{2,1,0:T(8,128)}) custom-call(f32[8,8,64]{2,1,0:T(8,128)S(1)} %bitcast.25, f32[8,8,64]{2,1,0:T(8,128)S(1)} %bitcast.27, f32[2,544,128]{2,1,0:T(8,128)S(1)} %bitcast.22, f32[552,128]{1,0:T(8,128)S(1)} %bitcast.23, ...), custom_call_target="tpu_custom_call" | custom-call | tf_op jit(solution)/shard_map/own_ocean/pallas_call | solution.py:32
  58.0 0.8 %collective-permute-done.5.r_ref = f32[8,512]{1,0:T(8,128)S(1)} collective-permute-done((f32[8,512]{1,0:T(8,128)S(1)}, f32[8,512]{1,0:T(8,128)S(1)}, u32[]{:S(2)}, u32[]{:S(2)}) %collective-permute-start.5) | collective-permute-done | bytes 16416 | tf_op jit(solution)/shard_map/ppermute | solution.py:63
  58.8 1.2 %heat.1 = f32[8,8,64]{2,1,0:T(8,128)} custom-call(f32[8,512]{1,0:T(8,128)S(1)} %get-tuple-element.52.att_ref, f32[8,512]{1,0:T(8,128)S(1)} %get-tuple-element.53.cum_ref, f32[8,512]{1,0:T(8,128)S(1)} %collective-permute-done.5.r_ref, f32[8,8,64]{2,1,0:T(8,128)S(1)} %get-tuple-element.58.w_ref, s32[8,8,64]{2,1,0:T(8,128)S(1)} %bitcast.29), custom_call_target="tpu_custom_call" | custom-call | tf_op jit(solution)/shard_map/heat/pallas_call | solution.py:32
  60.0 6.7 %all-to-all-done.2 = f16[16,32,512]{2,1,0:T(8,128)(2,1)S(1)} async-done(((f16[16,32,512]{2,1,0:T(8,128)(2,1)}), f16[16,32,512]{2,1,0:T(8,128)(2,1)S(1)}, u32[]{:S(2)}, u32[]{:S(2)}) %all-to-all-start.2) | async-done | bytes 524320 | tf_op jit(solution)/shard_map/all_to_all | solution.py:591
  66.8 1.1 %finish_tracers.1 = f32[4,512,128]{2,1,0:T(8,128)} custom-call(f32[16,32,512]{2,1,0:T(8,128)S(1)} %convert_element_type.11.r_ref, f32[4,128,512]{2,1,0:T(8,128)S(1)} %get-tuple-element.62.a_ref), custom_call_target="tpu_custom_call" | custom-call | tf_op jit(solution)/shard_map/finish_tracers/pallas_call | solution.py:32
  (24 shorter events, 1.6 us)
Async XLA Ops:
  2.6 16.2 %all-to-all-start = ((s32[8,64,128]{2,1,0:T(8,128)}), s32[8,64,128]{2,1,0:T(8,128)S(1)}, u32[]{:S(2)}, u32[]{:S(2)}) async-start(s32[8,64,128]{2,1,0:T(8,128)} %get-tuple-element.34), calls=%async_computation | async-start | bytes 524288 | tf_op jit(solution)/shard_map/all_to_all | solution.py:195
  9.8 4.6 %collective-permute-start = (f32[144,128]{1,0:T(8,128)}, f32[144,128]{1,0:T(8,128)S(1)}, u32[]{:S(2)}, u32[]{:S(2)}) collective-permute-start(f32[144,128]{1,0:T(8,128)} %get-tuple-element.35), channel_id=1, source_target_pairs={{0,1},{1,0},{2,3},{3,2},{4,5},{5,4},{6,7},{7,6},{8,9},{9,8},{10,11... | collective-permute-start | bytes 221192 | tf_op jit(solution)/shard_map/ppermute | solution.py:63
  14.4 1.2 %copy-start = (f32[4,64,8,128]{3,2,1,0:T(8,128)S(1)}, f32[4,64,8,128]{3,2,1,0:T(8,128)}, u32[]{:S(2)}) copy-start(f32[4,64,8,128]{3,2,1,0:T(8,128)} %param.14) | copy-start | bytes 3145732
  18.8 1.5 %collective-permute-start.1 = (s32[8,64,128]{2,1,0:T(8,128)S(1)}, s32[8,64,128]{2,1,0:T(8,128)S(1)}, u32[]{:S(2)}, u32[]{:S(2)}) collective-permute-start(s32[8,64,128]{2,1,0:T(8,128)S(1)} %all-to-all-done.a_ref), channel_id=1, source_target_pairs={{0,2},{2,0},{4,6},{6,4},{8,10},{10,8},{12,14},{14,12},{16,18},{18,... | collective-permute-start | bytes 786440 | tf_op jit(solution)/shard_map/ppermute | solution.py:223
  21.3 4.1 %collective-permute-start.2 = (f32[88,128]{1,0:T(8,128)S(1)}, f32[88,128]{1,0:T(8,128)S(1)}, u32[]{:S(2)}, u32[]{:S(2)}) collective-permute-start(f32[88,128]{1,0:T(8,128)S(1)} %get-tuple-element.41.o_ref), channel_id=1, source_target_pairs={{0,1},{1,0},{2,3},{3,2},{4,5},{5,4},{6,7},{7,6},{8,9},{9,8},{10,11... | collective-permute-start | bytes 135176 | tf_op jit(solution)/shard_map/ppermute | solution.py:63
  24.7 9.3 %copy-start.8 = (f32[16,64]{1,0:T(8,128)S(1)}, f32[16,64]{1,0:T(8,128)}, u32[]{:S(2)}) copy-start(f32[16,64]{1,0:T(8,128)} %get-tuple-element.49) | copy-start | bytes 12292
  24.7 9.6 %copy-start.7 = (f32[16,64]{1,0:T(8,128)S(1)}, f32[16,64]{1,0:T(8,128)}, u32[]{:S(2)}) copy-start(f32[16,64]{1,0:T(8,128)} %get-tuple-element.50) | copy-start | bytes 12292
  24.7 13.8 %copy-start.4 = (bf16[64,64]{1,0:T(8,128)(2,1)S(1)}, bf16[64,64]{1,0:T(8,128)(2,1)}, u32[]{:S(2)}) copy-start(bf16[64,64]{1,0:T(8,128)(2,1)} %c_ref.1) | copy-start | bytes 24580
  24.7 29.4 %copy-start.5 = (s32[64]{0:T(128)S(1)}, s32[64]{0:T(128)}, u32[]{:S(2)}) copy-start(s32[64]{0:T(128)} %g_ref.1) | copy-start | bytes 772
  24.7 29.4 %copy-start.6 = (f32[8]{0:T(128)S(1)}, f32[8]{0:T(128)}, u32[]{:S(2)}) copy-start(f32[8]{0:T(128)} %k_ref.1) | copy-start | bytes 100
  25.4 31.2 %copy-start.1 = (f32[64,8,8]{0,2,1:T(8,128)S(1)}, f32[64,8,8]{0,2,1:T(8,128)}, u32[]{:S(2)}) copy-start(f32[64,8,8]{0,2,1:T(8,128)} %param.9) | copy-start | bytes 49156
  25.4 31.2 %copy-start.2 = (f32[64,8,8]{0,2,1:T(8,128)S(1)}, f32[64,8,8]{0,2,1:T(8,128)}, u32[]{:S(2)}) copy-start(f32[64,8,8]{0,2,1:T(8,128)} %param.10) | copy-start | bytes 49156
  25.4 33.4 %copy-start.3 = (s32[64,8,8]{0,2,1:T(8,128)S(1)}, s32[64,8,8]{0,2,1:T(8,128)}, u32[]{:S(2)}) copy-start(s32[64,8,8]{0,2,1:T(8,128)} %param.13) | copy-start | bytes 49156
  28.9 17.7 %all-to-all-start.1 = ((bf16[16,32,512]{2,1,0:T(8,128)(2,1)}), bf16[16,32,512]{2,1,0:T(8,128)(2,1)S(1)}, u32[]{:S(2)}, u32[]{:S(2)}) async-start(bf16[16,32,512]{2,1,0:T(8,128)(2,1)} %get-tuple-element.48), calls=%async_computation.1 | async-start | bytes 1048576 | tf_op jit(solution)/shard_map/all_to_all | solution.py:486
  34.0 10.8 %collective-permute-start.3 = (f32[16,64]{1,0:T(8,128)S(1)}, f32[16,64]{1,0:T(8,128)S(1)}, u32[]{:S(2)}, u32[]{:S(2)}) collective-permute-start(f32[16,64]{1,0:T(8,128)S(1)} %copy-done.8), channel_id=1, source_target_pairs={{0,2},{2,4},{4,6},{6,8},{8,10},{10,12},{12,14},{14,16},{16,18},{18... | collective-permute-start | bytes 12296 | tf_op jit(solution)/shard_map/ppermute | solution.py:490
  34.2 10.6 %collective-permute-start.4 = (f32[16,64]{1,0:T(8,128)S(1)}, f32[16,64]{1,0:T(8,128)S(1)}, u32[]{:S(2)}, u32[]{:S(2)}) collective-permute-start(f32[16,64]{1,0:T(8,128)S(1)} %copy-done.7), channel_id=1, source_target_pairs={{2,0},{4,2},{6,4},{8,6},{10,8},{12,10},{14,12},{16,14},{18,16},{20... | collective-permute-start | bytes 12296 | tf_op jit(solution)/shard_map/ppermute | solution.py:491
  47.9 18.8 %all-to-all-start.2 = ((f16[16,32,512]{2,1,0:T(8,128)(2,1)}), f16[16,32,512]{2,1,0:T(8,128)(2,1)S(1)}, u32[]{:S(2)}, u32[]{:S(2)}) async-start(f16[16,32,512]{2,1,0:T(8,128)(2,1)} %bitcast.31), calls=%async_computation.2 | async-start | bytes 1048576 | tf_op jit(solution)/shard_map/all_to_all | solution.py:591
  55.0 3.8 %collective-permute-start.5 = (f32[8,512]{1,0:T(8,128)S(1)}, f32[8,512]{1,0:T(8,128)S(1)}, u32[]{:S(2)}, u32[]{:S(2)}) collective-permute-start(f32[8,512]{1,0:T(8,128)S(1)} %get-tuple-element.53.cum_ref), channel_id=1, source_target_pairs={{0,1},{1,0},{2,3},{3,2},{4,5},{5,4},{6,7},{7,6},{8,9},{9,8},{10,11... | collective-permute-start | bytes 49160 | tf_op jit(solution)/shard_map/ppermute | solution.py:63

commit v8 on v7

--- a/solution.py
+++ b/solution.py
@@ -106,6 +106,9 @@
     order = list(range(ntrc))
     random.Random(4).shuffle(order)
     place = [order.index(d) for d in range(ntrc)]
+    back = list(range(ntrc))
+    random.Random(3).shuffle(back)
+    back_place = [back.index(d) for d in range(ntrc)]
     pairs_apart = [[2 * g + c for g in range(NP)] for c in range(2)]
 
     ROWS = XL * Y
@@ -568,7 +571,7 @@
 
         def pick(shape, along):
             wide, narrow = (lax.broadcasted_iota(jnp.int32, shape, d) for d in (along, 1 - along))
-            device = sum(jnp.where(wide // (T * Y) == p, d, 0) for p, d in enumerate(order))
+            device = sum(jnp.where(wide // (T * Y) == p, d, 0) for p, d in enumerate((back, order)[along]))
             tracer = device * T + (wide // Y) % T
             return jnp.where(tracer == narrow, 1.0, 0.0).astype(jnp.bfloat16)
 
@@ -589,7 +592,7 @@
     reaction = jnp.dot(spread, flat_tracers, preferred_element_type=F32)
     reaction = (reaction * (1.0 / unit)).astype(jnp.float16).reshape(ntrc, T * Y, DX)
     returned = lax.all_to_all(
-        reaction, "trc", split_axis=0, concat_axis=0, tiled=True, axis_index_groups=[order]
+        reaction, "trc", split_axis=0, concat_axis=0, tiled=True, axis_index_groups=[back]
     )
 
     def shade(x_ref, g_ref, k_ref, att_ref, cum_ref):
@@ -645,7 +648,7 @@
         for t in range(T):
             for w in range(DX // LANES):
                 rows = [
-                    r_ref[place[d], t * Y : (t + 1) * Y, w * LANES : (w + 1) * LANES]
+                    r_ref[back_place[d], t * Y : (t + 1) * Y, w * LANES : (w + 1) * LANES]
                     for d in range(ntrc)
                 ]
                 here = slice(w * LANES, (w + 1) * LANES)

time: 68.5 us -> 68.2 us (level)
  starting transfers between devices: 27.7 us -> 26.2 us
  waiting for transfers between devices: 23.5 us -> 24.8 us
    all_to_all x1, starting transfers between devices: 6.19 us -> 4.65 us  [shards(): lax.all_to_all(reaction, 'trc', split_axis=0, concat_axis=0, tiled=True,...]
    all_to_all x1, waiting for transfers between devices: 6.68 us -> 7.99 us  [shards(): lax.all_to_all(reaction, 'trc', split_axis=0, concat_axis=0, tiled=True,...]
where the time goes in v8:
time: 68.2 us; the launch traced here: 67.7 us
  starting transfers between devices  26.2 us (38%)
  waiting for transfers between devices  24.8 us (36%)
  Pallas kernels  13.3 us (20%)
  local copies, waits for them, and re-layouts  1.26 us (2%)
  matrix products  1.23 us (2%)
  between operations  0.74 us (1%)
    pallas_call x10, Pallas kernels, call(): pl.pallas_call(kernel, out_shape=out_shape, in_specs=[vmem] * len(args) i...  13.3 us
    all_to_all x1, waiting for transfers between devices, shards(): lax.all_to_all(reaction, 'trc', split_axis=0, concat_axis=0, tiled=True,...  7.99 us
    all_to_all x1, starting transfers between devices, shards(): lax.all_to_all(payload, 'trc', split_axis=0, concat_axis=0, tiled=True, a...  7.26 us
    ppermute x1, waiting for transfers between devices, shards(): south = lax.ppermute(hi, 'trc', ring)  5.87 us
    all_to_all x1, starting transfers between devices, shards(): lax.all_to_all(message, 'trc', split_axis=0, concat_axis=0, tiled=True, a...  5.13 us
    all_to_all x1, starting transfers between devices, shards(): lax.all_to_all(reaction, 'trc', split_axis=0, concat_axis=0, tiled=True,...  4.65 us
    ppermute x3, starting transfers between devices, exchange_levels(): return lax.ppermute(part, 'lev', [(0, 1), (1, 0)])  4.64 us
    ppermute x3, waiting for transfers between devices, exchange_levels(): return lax.ppermute(part, 'lev', [(0, 1), (1, 0)])  4.57 us
  transfers between devices with their start and end apart: 9, of which 8 were waited for; matrix products, arithmetic and copies ran while one was open for 0% of the time, Pallas kernels for 9%

profile of v8, /device:TPU:0, one launch (start us, length us, event | category | flops | bytes accessed | tf_op | source)
XLA Modules:
  0.0 67.7 jit_solution(10694991283374111748)
XLA Ops:
  0.6 1.9 %pack_ocean.1 = (s32[8,64,128]{2,1,0:T(8,128)}, f32[16,64]{1,0:T(8,128)}, f32[16,64]{1,0:T(8,128)}, f32[144,128]{1,0:T(8,128)}) custom-call(f32[8,8,64]{2,1,0:T(8,128)} %bitcast.24, f32[8,8,64]{2,1,0:T(8,128)} %bitcast.26, f32[8,8,64]{2,1,0:T(8,128)} %bitcast.32, f32[8,8,64]{2,1,0:T(8,128)} %bitcast.33, s32[8,8,64]{2,1,0:T(8,128)} %bitcast.28, ...), custom_call_target="tpu_custom_call" | custom-call | tf_op jit(solution)/shard_map/pack_ocean/pallas_call | solution.py:32
  2.6 7.3 %all-to-all-start = ((s32[8,64,128]{2,1,0:T(8,128)}), s32[8,64,128]{2,1,0:T(8,128)S(1)}, u32[]{:S(2)}, u32[]{:S(2)}) async-start(s32[8,64,128]{2,1,0:T(8,128)} %get-tuple-element.34), calls=%async_computation | async-start | bytes 524288 | tf_op jit(solution)/shard_map/all_to_all | solution.py:198
  9.8 1.5 %collective-permute-start = (f32[144,128]{1,0:T(8,128)}, f32[144,128]{1,0:T(8,128)S(1)}, u32[]{:S(2)}, u32[]{:S(2)}) collective-permute-start(f32[144,128]{1,0:T(8,128)} %get-tuple-element.35), channel_id=1, source_target_pairs={{0,1},{1,0},{2,3},{3,2},{4,5},{5,4},{6,7},{7,6},{8,9},{9,8},{10,11... | collective-permute-start | bytes 221192 | tf_op jit(solution)/shard_map/ppermute | solution.py:63
  11.4 3.0 %collective-permute-done.h_ref.l_ref = f32[144,128]{1,0:T(8,128)S(1)} collective-permute-done((f32[144,128]{1,0:T(8,128)}, f32[144,128]{1,0:T(8,128)S(1)}, u32[]{:S(2)}, u32[]{:S(2)}) %collective-permute-start) | collective-permute-done | bytes 73760 | tf_op jit(solution)/shard_map/ppermute | solution.py:63
  14.4 1.2 %copy-done = f32[4,64,8,128]{3,2,1,0:T(8,128)S(1)} copy-done((f32[4,64,8,128]{3,2,1,0:T(8,128)S(1)}, f32[4,64,8,128]{3,2,1,0:T(8,128)}, u32[]{:S(2)}) %copy-start) | copy-done | bytes 1048600
  15.7 3.0 %all-to-all-done.a_ref = s32[8,64,128]{2,1,0:T(8,128)S(1)} async-done(((s32[8,64,128]{2,1,0:T(8,128)}), s32[8,64,128]{2,1,0:T(8,128)S(1)}, u32[]{:S(2)}, u32[]{:S(2)}) %all-to-all-start) | async-done | bytes 262176 | tf_op jit(solution)/shard_map/all_to_all | solution.py:198
  18.8 1.5 %collective-permute-done.1.b_ref = s32[8,64,128]{2,1,0:T(8,128)S(1)} collective-permute-done((s32[8,64,128]{2,1,0:T(8,128)S(1)}, s32[8,64,128]{2,1,0:T(8,128)S(1)}, u32[]{:S(2)}, u32[]{:S(2)}) %collective-permute-start.1) | collective-permute-done | bytes 262176 | tf_op jit(solution)/shard_map/ppermute | solution.py:226
  20.3 1.0 %unpack_ocean.1 = (f32[2,64,8,128]{3,2,1,0:T(8,128)S(1)}, f32[2,64,8,128]{3,2,1,0:T(8,128)S(1)}, f32[88,128]{1,0:T(8,128)S(1)}) custom-call(s32[8,64,128]{2,1,0:T(8,128)S(1)} %all-to-all-done.a_ref, s32[8,64,128]{2,1,0:T(8,128)S(1)} %collective-permute-done.1.b_ref), custom_call_target="tpu_custom_call" | custom-call | tf_op jit(solution)/shard_map/unpack_ocean/pallas_call | solution.py:32
  21.3 1.6 %collective-permute-start.2 = (f32[88,128]{1,0:T(8,128)S(1)}, f32[88,128]{1,0:T(8,128)S(1)}, u32[]{:S(2)}, u32[]{:S(2)}) collective-permute-start(f32[88,128]{1,0:T(8,128)S(1)} %get-tuple-element.41.o_ref), channel_id=1, source_target_pairs={{0,1},{1,0},{2,3},{3,2},{4,5},{5,4},{6,7},{7,6},{8,9},{9,8},{10,11... | collective-permute-start | bytes 135176 | tf_op jit(solution)/shard_map/ppermute | solution.py:63
  22.9 1.8 %first_slopes.1.side = f32[6,4,560,128]{3,2,1,0:T(8,128)S(1)} custom-call(f32[4,576,128]{2,1,0:T(8,128)S(1)} %widen_levels.1.pad), custom_call_target="tpu_custom_call" | custom-call | tf_op jit(solution)/shard_map/first_slopes/pallas_call | solution.py:32
  25.4 3.5 %advect_tracers.1 = (f32[4,128,512]{2,1,0:T(8,128)S(1)}, bf16[16,32,512]{2,1,0:T(8,128)(2,1)}, f32[2,68,8,128]{3,2,1,0:T(8,128)S(1)}, f32[69,8,128]{2,1,0:T(8,128)S(1)}) custom-call(f32[2,64,8,128]{3,2,1,0:T(8,128)S(1)} %get-tuple-element.37.n_ref, f32[2,64,8,128]{3,2,1,0:T(8,128)S(1)} %get-tuple-element.38.m_ref, f32[88,128]{1,0:T(8,128)S(1)} %get-tuple-element.41.o_ref, ...), custom_call_target="tpu_custom_call" | custom-call | tf_op jit(solution)/shard_map/advect_tracers/pallas_call | solution.py:32
  28.9 5.1 %all-to-all-start.1 = ((bf16[16,32,512]{2,1,0:T(8,128)(2,1)}), bf16[16,32,512]{2,1,0:T(8,128)(2,1)S(1)}, u32[]{:S(2)}, u32[]{:S(2)}) async-start(bf16[16,32,512]{2,1,0:T(8,128)(2,1)} %get-tuple-element.48), calls=%async_computation.1 | async-start | bytes 1048576 | tf_op jit(solution)/shard_map/all_to_all | solution.py:489
  34.2 4.3 %collective-permute-start.4 = (f32[16,64]{1,0:T(8,128)S(1)}, f32[16,64]{1,0:T(8,128)S(1)}, u32[]{:S(2)}, u32[]{:S(2)}) collective-permute-start(f32[16,64]{1,0:T(8,128)S(1)} %copy-done.7), channel_id=1, source_target_pairs={{2,0},{4,2},{6,4},{8,6},{10,8},{12,10},{14,12},{16,14},{18,16},{20... | collective-permute-start | bytes 12296 | tf_op jit(solution)/shard_map/ppermute | solution.py:494
  38.9 5.9 %collective-permute-done.3.so_ref = f32[16,64]{1,0:T(8,128)S(1)} collective-permute-done((f32[16,64]{1,0:T(8,128)S(1)}, f32[16,64]{1,0:T(8,128)S(1)}, u32[]{:S(2)}, u32[]{:S(2)}) %collective-permute-start.3) | collective-permute-done | bytes 4128 | tf_op jit(solution)/shard_map/ppermute | solution.py:493
  44.8 1.8 %all-to-all-done.1.x_ref = bf16[16,32,512]{2,1,0:T(8,128)(2,1)S(1)} async-done(((bf16[16,32,512]{2,1,0:T(8,128)(2,1)}), bf16[16,32,512]{2,1,0:T(8,128)(2,1)S(1)}, u32[]{:S(2)}, u32[]{:S(2)}) %all-to-all-start.1) | async-done | bytes 524320 | tf_op jit(solution)/shard_map/all_to_all | solution.py:489
  46.6 1.2 %fusion = f16[512,512]{0,1:T(8,128)(2,1)} fusion(bf16[512,512]{1,0:T(8,128)(2,1)S(1)} %spread_coupling.1, bf16[512,512]{1,0:T(8,128)(2,1)S(1)} %bitcast.21), kind=kOutput, calls=%fused_computation.1 | convolution fusion | flops 268959744 | bytes 1572864 | tf_op jit(solution)/shard_map/dot_general | solution.py:592
  47.9 4.7 %all-to-all-start.2 = ((f16[16,32,512]{2,1,0:T(8,128)(2,1)}), f16[16,32,512]{2,1,0:T(8,128)(2,1)S(1)}, u32[]{:S(2)}, u32[]{:S(2)}) async-start(f16[16,32,512]{2,1,0:T(8,128)(2,1)} %bitcast.31), calls=%async_computation.2 | async-start | bytes 1048576 | tf_op jit(solution)/shard_map/all_to_all | solution.py:594
  52.5 1.0 %shade.1 = (f32[8,512]{1,0:T(8,128)S(1)}, f32[8,512]{1,0:T(8,128)S(1)}) custom-call(bf16[16,32,512]{2,1,0:T(8,128)(2,1)S(1)} %all-to-all-done.1.x_ref, s32[64]{0:T(128)S(1)} %copy-done.5, f32[8]{0:T(128)S(1)} %copy-done.6), custom_call_target="tpu_custom_call" | custom-call | tf_op jit(solution)/shard_map/shade/pallas_call | solution.py:32
  53.5 1.5 %collective-permute-start.5 = (f32[8,512]{1,0:T(8,128)S(1)}, f32[8,512]{1,0:T(8,128)S(1)}, u32[]{:S(2)}, u32[]{:S(2)}) collective-permute-start(f32[8,512]{1,0:T(8,128)S(1)} %get-tuple-element.53.cum_ref), channel_id=1, source_target_pairs={{0,1},{1,0},{2,3},{3,2},{4,5},{5,4},{6,7},{7,6},{8,9},{9,8},{10,11... | collective-permute-start | bytes 49160 | tf_op jit(solution)/shard_map/ppermute | solution.py:63
  55.0 1.4 %own_ocean.1 = (f32[8,8,64]{2,1,0:T(8,128)}, f32[8,8,64]{2,1,0:T(8,128)S(1)}, f32[8,8,64]{2,1,0:T(8,128)}, f32[8,8,64]{2,1,0:T(8,128)}) custom-call(f32[8,8,64]{2,1,0:T(8,128)S(1)} %bitcast.25, f32[8,8,64]{2,1,0:T(8,128)S(1)} %bitcast.27, f32[2,544,128]{2,1,0:T(8,128)S(1)} %bitcast.22, f32[552,128]{1,0:T(8,128)S(1)} %bitcast.23, ...), custom_call_target="tpu_custom_call" | custom-call | tf_op jit(solution)/shard_map/own_ocean/pallas_call | solution.py:32
  56.4 0.8 %collective-permute-done.5.r_ref = f32[8,512]{1,0:T(8,128)S(1)} collective-permute-done((f32[8,512]{1,0:T(8,128)S(1)}, f32[8,512]{1,0:T(8,128)S(1)}, u32[]{:S(2)}, u32[]{:S(2)}) %collective-permute-start.5) | collective-permute-done | bytes 16416 | tf_op jit(solution)/shard_map/ppermute | solution.py:63
  57.3 1.2 %heat.1 = f32[8,8,64]{2,1,0:T(8,128)} custom-call(f32[8,512]{1,0:T(8,128)S(1)} %get-tuple-element.52.att_ref, f32[8,512]{1,0:T(8,128)S(1)} %get-tuple-element.53.cum_ref, f32[8,512]{1,0:T(8,128)S(1)} %collective-permute-done.5.r_ref, f32[8,8,64]{2,1,0:T(8,128)S(1)} %get-tuple-element.58.w_ref, s32[8,8,64]{2,1,0:T(8,128)S(1)} %bitcast.29), custom_call_target="tpu_custom_call" | custom-call | tf_op jit(solution)/shard_map/heat/pallas_call | solution.py:32
  58.4 8.0 %all-to-all-done.2 = f16[16,32,512]{2,1,0:T(8,128)(2,1)S(1)} async-done(((f16[16,32,512]{2,1,0:T(8,128)(2,1)}), f16[16,32,512]{2,1,0:T(8,128)(2,1)S(1)}, u32[]{:S(2)}, u32[]{:S(2)}) %all-to-all-start.2) | async-done | bytes 524320 | tf_op jit(solution)/shard_map/all_to_all | solution.py:594
  66.5 1.1 %finish_tracers.1 = f32[4,512,128]{2,1,0:T(8,128)} custom-call(f32[16,32,512]{2,1,0:T(8,128)S(1)} %convert_element_type.11.r_ref, f32[4,128,512]{2,1,0:T(8,128)S(1)} %get-tuple-element.62.a_ref), custom_call_target="tpu_custom_call" | custom-call | tf_op jit(solution)/shard_map/finish_tracers/pallas_call | solution.py:32
  (24 shorter events, 1.6 us)
Async XLA Ops:
  2.6 16.2 %all-to-all-start = ((s32[8,64,128]{2,1,0:T(8,128)}), s32[8,64,128]{2,1,0:T(8,128)S(1)}, u32[]{:S(2)}, u32[]{:S(2)}) async-start(s32[8,64,128]{2,1,0:T(8,128)} %get-tuple-element.34), calls=%async_computation | async-start | bytes 524288 | tf_op jit(solution)/shard_map/all_to_all | solution.py:198
  9.8 4.6 %collective-permute-start = (f32[144,128]{1,0:T(8,128)}, f32[144,128]{1,0:T(8,128)S(1)}, u32[]{:S(2)}, u32[]{:S(2)}) collective-permute-start(f32[144,128]{1,0:T(8,128)} %get-tuple-element.35), channel_id=1, source_target_pairs={{0,1},{1,0},{2,3},{3,2},{4,5},{5,4},{6,7},{7,6},{8,9},{9,8},{10,11... | collective-permute-start | bytes 221192 | tf_op jit(solution)/shard_map/ppermute | solution.py:63
  14.4 1.2 %copy-start = (f32[4,64,8,128]{3,2,1,0:T(8,128)S(1)}, f32[4,64,8,128]{3,2,1,0:T(8,128)}, u32[]{:S(2)}) copy-start(f32[4,64,8,128]{3,2,1,0:T(8,128)} %param.14) | copy-start | bytes 3145732
  18.8 1.5 %collective-permute-start.1 = (s32[8,64,128]{2,1,0:T(8,128)S(1)}, s32[8,64,128]{2,1,0:T(8,128)S(1)}, u32[]{:S(2)}, u32[]{:S(2)}) collective-permute-start(s32[8,64,128]{2,1,0:T(8,128)S(1)} %all-to-all-done.a_ref), channel_id=1, source_target_pairs={{0,2},{2,0},{4,6},{6,4},{8,10},{10,8},{12,14},{14,12},{16,18},{18,... | collective-permute-start | bytes 786440 | tf_op jit(solution)/shard_map/ppermute | solution.py:226
  21.3 4.1 %collective-permute-start.2 = (f32[88,128]{1,0:T(8,128)S(1)}, f32[88,128]{1,0:T(8,128)S(1)}, u32[]{:S(2)}, u32[]{:S(2)}) collective-permute-start(f32[88,128]{1,0:T(8,128)S(1)} %get-tuple-element.41.o_ref), channel_id=1, source_target_pairs={{0,1},{1,0},{2,3},{3,2},{4,5},{5,4},{6,7},{7,6},{8,9},{9,8},{10,11... | collective-permute-start | bytes 135176 | tf_op jit(solution)/shard_map/ppermute | solution.py:63
  24.7 9.3 %copy-start.8 = (f32[16,64]{1,0:T(8,128)S(1)}, f32[16,64]{1,0:T(8,128)}, u32[]{:S(2)}) copy-start(f32[16,64]{1,0:T(8,128)} %get-tuple-element.49) | copy-start | bytes 12292
  24.7 9.6 %copy-start.7 = (f32[16,64]{1,0:T(8,128)S(1)}, f32[16,64]{1,0:T(8,128)}, u32[]{:S(2)}) copy-start(f32[16,64]{1,0:T(8,128)} %get-tuple-element.50) | copy-start | bytes 12292
  24.7 13.8 %copy-start.4 = (bf16[64,64]{1,0:T(8,128)(2,1)S(1)}, bf16[64,64]{1,0:T(8,128)(2,1)}, u32[]{:S(2)}) copy-start(bf16[64,64]{1,0:T(8,128)(2,1)} %c_ref.1) | copy-start | bytes 24580
  24.7 27.8 %copy-start.5 = (s32[64]{0:T(128)S(1)}, s32[64]{0:T(128)}, u32[]{:S(2)}) copy-start(s32[64]{0:T(128)} %g_ref.1) | copy-start | bytes 772
  24.7 27.8 %copy-start.6 = (f32[8]{0:T(128)S(1)}, f32[8]{0:T(128)}, u32[]{:S(2)}) copy-start(f32[8]{0:T(128)} %k_ref.1) | copy-start | bytes 100
  25.4 29.6 %copy-start.1 = (f32[64,8,8]{0,2,1:T(8,128)S(1)}, f32[64,8,8]{0,2,1:T(8,128)}, u32[]{:S(2)}) copy-start(f32[64,8,8]{0,2,1:T(8,128)} %param.9) | copy-start | bytes 49156
  25.4 29.6 %copy-start.2 = (f32[64,8,8]{0,2,1:T(8,128)S(1)}, f32[64,8,8]{0,2,1:T(8,128)}, u32[]{:S(2)}) copy-start(f32[64,8,8]{0,2,1:T(8,128)} %param.10) | copy-start | bytes 49156
  25.4 31.8 %copy-start.3 = (s32[64,8,8]{0,2,1:T(8,128)S(1)}, s32[64,8,8]{0,2,1:T(8,128)}, u32[]{:S(2)}) copy-start(s32[64,8,8]{0,2,1:T(8,128)} %param.13) | copy-start | bytes 49156
  28.9 17.7 %all-to-all-start.1 = ((bf16[16,32,512]{2,1,0:T(8,128)(2,1)}), bf16[16,32,512]{2,1,0:T(8,128)(2,1)S(1)}, u32[]{:S(2)}, u32[]{:S(2)}) async-start(bf16[16,32,512]{2,1,0:T(8,128)(2,1)} %get-tuple-element.48), calls=%async_computation.1 | async-start | bytes 1048576 | tf_op jit(solution)/shard_map/all_to_all | solution.py:489
  34.0 10.8 %collective-permute-start.3 = (f32[16,64]{1,0:T(8,128)S(1)}, f32[16,64]{1,0:T(8,128)S(1)}, u32[]{:S(2)}, u32[]{:S(2)}) collective-permute-start(f32[16,64]{1,0:T(8,128)S(1)} %copy-done.8), channel_id=1, source_target_pairs={{0,2},{2,4},{4,6},{6,8},{8,10},{10,12},{12,14},{14,16},{16,18},{18... | collective-permute-start | bytes 12296 | tf_op jit(solution)/shard_map/ppermute | solution.py:493
  34.2 10.6 %collective-permute-start.4 = (f32[16,64]{1,0:T(8,128)S(1)}, f32[16,64]{1,0:T(8,128)S(1)}, u32[]{:S(2)}, u32[]{:S(2)}) collective-permute-start(f32[16,64]{1,0:T(8,128)S(1)} %copy-done.7), channel_id=1, source_target_pairs={{2,0},{4,2},{6,4},{8,6},{10,8},{12,10},{14,12},{16,14},{18,16},{20... | collective-permute-start | bytes 12296 | tf_op jit(solution)/shard_map/ppermute | solution.py:494
  47.9 18.6 %all-to-all-start.2 = ((f16[16,32,512]{2,1,0:T(8,128)(2,1)}), f16[16,32,512]{2,1,0:T(8,128)(2,1)S(1)}, u32[]{:S(2)}, u32[]{:S(2)}) async-start(f16[16,32,512]{2,1,0:T(8,128)(2,1)} %bitcast.31), calls=%async_computation.2 | async-start | bytes 1048576 | tf_op jit(solution)/shard_map/all_to_all | solution.py:594
  53.5 3.8 %collective-permute-start.5 = (f32[8,512]{1,0:T(8,128)S(1)}, f32[8,512]{1,0:T(8,128)S(1)}, u32[]{:S(2)}, u32[]{:S(2)}) collective-permute-start(f32[8,512]{1,0:T(8,128)S(1)} %get-tuple-element.53.cum_ref), channel_id=1, source_target_pairs={{0,1},{1,0},{2,3},{3,2},{4,5},{5,4},{6,7},{7,6},{8,9},{9,8},{10,11... | collective-permute-start | bytes 49160 | tf_op jit(solution)/shard_map/ppermute | solution.py:63
